TPU v7x, 256 devices: a whole 4x4x8 slice. The times are simulated.
256 devices in a mesh: gx: 32 (over y, z), gz: 8 (over x, core).
Axes of the slice: x: 4, y: 4, z: 8, core: 2. Of those that a mesh axis runs over, the one named last changes fastest.
Arguments:
- charge: float32 [64, 1024, 1024], P('gz', 'gx'), may hold values from -24 to 24
- cell_permittivity: float32 [64], replicated, may hold values from 1 to 4
- face_permittivity: float32 [64], replicated, may hold values from 1 to 4
- screening: float32 [64], replicated, may hold values from 0.001 to 0.01
Outputs:
- potential: float32 [64, 1024, 1024], P('gz', 'gx')
All inputs are finite; a program needn't handle non-finite values.
Results may differ from a plain program's by a relative error of at most 0.0003.
Values sent between devices are 32-bit elements; how exact they have to be, the bound alone decides.
No kernel may reach another device: no remote copies, remote signals or barrier semaphores. Data moves between devices by JAX's collectives and lax.ppermute only.
A program may use at most 128 MiB of HBM per device.

v0:
```python
import functools
import math

import jax
import jax.numpy as jnp
import ml_dtypes
import numpy as np
from jax import lax
from jax.experimental import pallas as pl
from jax.experimental.pallas import tpu as pltpu
from jax.sharding import PartitionSpec as P

NX, NY, NZ = 1024, 1024, 64
SLABS, PLANES = 32, 32
HALF = NY // 2
CHIPS = 4
LAYERS = NZ // CHIPS
LANES = 128
highest = lax.Precision.HIGHEST
VMEM_LIMIT = 48 * 1024 * 1024


def split_pair(table):
    high = table.astype(np.float32).astype(ml_dtypes.bfloat16)
    low = (table - high.astype(np.float64)).astype(np.float32).astype(ml_dtypes.bfloat16)
    return high, low


def y_frequencies():
    index = np.arange(HALF)
    even = np.where(index <= HALF // 2, 2 * index, 2 * (index - HALF // 2))
    odd = np.where(index < HALF // 2, 2 * index + 1, 2 * (index - HALF // 2) + 1)
    even_is_cos = index <= HALF // 2
    odd_is_cos = index < HALF // 2
    return np.stack([even, odd]), np.stack([even_is_cos, odd_is_cos])


def y_tables():
    freq, is_cos = y_frequencies()
    point = np.arange(HALF)
    angle = 2.0 * np.pi * (point[None, :, None] * freq[:, None, :] % NY) / NY
    forward = np.where(is_cos[:, None, :], np.cos(angle), np.sin(angle))
    weight = np.where((freq == 0) | (freq == NY // 2), 1.0 / NY, 2.0 / NY)
    backward = np.swapaxes(forward * weight[:, None, :], 1, 2)
    return forward, backward


def y_shifts():
    freq, _ = y_frequencies()
    shift = 4.0 * np.sin(np.pi * freq / NY) ** 2
    return shift.reshape(2, CHIPS, LANES).transpose(1, 0, 2).reshape(2 * CHIPS, LANES)


def slab_basis():
    index = np.arange(PLANES)
    basis = math.sqrt(2.0 / PLANES) * np.sin(np.pi * np.outer(index, index) / PLANES)
    basis[0, :] = 0.0
    basis[:, 0] = 0.0
    basis[0, 0] = 1.0
    return basis


def interface_tables():
    mode = np.arange(SLABS)
    freq = np.where(mode <= SLABS // 2, mode, mode - SLABS // 2)
    is_cos = mode <= SLABS // 2
    weight = np.where((freq == 0) | (freq == SLABS // 2), 1.0, 2.0) / SLABS / SLABS

    def basis(offset):
        angle = 2.0 * np.pi * ((np.arange(SLABS)[:, None] + offset) * freq[None, :] % SLABS) / SLABS
        return np.where(is_cos[None, :], np.cos(angle), np.sin(angle))

    forward = np.zeros((2, 4, SLABS, LANES), np.float32)
    backward = np.zeros((2, 4, SLABS, LANES), np.float32)
    for which in range(2):
        for part in range(4):
            forward[which, part, :, part * SLABS : (part + 1) * SLABS] = basis(which)
            backward[which, part, :, part * SLABS : (part + 1) * SLABS] = basis(which) * weight[None, :]
    alias = freq[None, :] + SLABS * np.arange(SLABS)[:, None]
    alias_shift = 4.0 * np.sin(np.pi * alias / NX) ** 2
    return forward, backward, np.tile(alias_shift, (1, 4)).astype(np.float32)


def fold_tables():
    own = np.zeros((NZ, 8, 2 * NZ), np.float32)
    far = np.zeros((NZ, 8, 2 * NZ), np.float32)
    for layer in range(NZ):
        own[layer, :, layer] = 1.0
        far[layer, :, NZ + layer] = np.where(np.arange(8) % 2 == 1, 1.0, -1.0)
    return own.reshape(8 * NZ, 2 * NZ), far.reshape(8 * NZ, 2 * NZ)


def near_weights():
    weight = slab_basis()[1].copy()
    weight[0] = 0.0
    return np.broadcast_to(weight[:, None], (PLANES, LANES)).astype(np.float32)


def split_values(values):
    high = values.astype(jnp.bfloat16)
    low = (values - high.astype(jnp.float32)).astype(jnp.bfloat16)
    return high, low


def dot_split(left, right):
    left_high, left_low = left
    right_high, right_low = right
    dot = functools.partial(jnp.dot, preferred_element_type=jnp.float32)
    return dot(left_high, right_high) + (dot(left_high, right_low) + dot(left_low, right_high))


def dot_full(left, right, contract):
    return lax.dot_general(
        left, right, (contract, ((), ())), precision=highest, preferred_element_type=jnp.float32
    )


def forward_kernel(place, own, other, table_high, table_low, slab_high, slab_low, out0, out1, out2, out3, modes):
    core, chip = place[0], place[1]
    rows = 8 * PLANES
    own_rows = own[...].reshape(rows, HALF)
    other_rows = other[...].reshape(rows, HALF)
    slab = (slab_high[...], slab_low[...])
    table = (table_high[0], table_low[0])
    for half in range(2):
        values = jnp.where(core == half, own_rows, other_rows)
        spectrum = dot_split(split_values(values), table)
        modes[half * rows : (half + 1) * rows, :] = dot_split(slab, split_values(spectrum))
    for step, out in enumerate((out0, out1, out2, out3)):
        block = lax.rem(chip + step, CHIPS)
        start = pl.multiple_of(block * LANES, LANES)
        out[...] = modes[:, pl.ds(start, LANES)].reshape(LAYERS, PLANES, LANES)


def pivot_kernel(shift, cell, face, screening, out):
    shifts = shift[...]
    previous = None
    for layer in range(NZ):
        below = face[layer - 1] if layer > 0 else face[NZ - 1]
        pivot = (below + face[layer] + screening[layer]) + cell[layer] * shifts
        if previous is not None:
            pivot = pivot - (below * below) * previous
        previous = 1.0 / pivot
        out[layer] = previous


def first_solve_kernel(place, in0, in1, in2, in3, inverse, weights, fold_own, fold_far, cell, face, field, ends, part, folded, folded_own):
    chip = place[1]
    for step, source in enumerate((in0, in1, in2, in3)):
        block = lax.rem(chip + CHIPS - step, CHIPS)
        field[pl.ds(block * LAYERS, LAYERS)] = source[...]
    value = None
    for layer in range(NZ):
        inv = inverse[layer]
        scaled = field[layer] * inv
        value = scaled if value is None else scaled + (face[layer - 1] * inv) * value
        part[layer] = value
    weight = weights[...]
    keep = lax.broadcasted_iota(jnp.int32, (8, LANES), 0) == 0
    value = None
    for layer in reversed(range(NZ)):
        value = part[layer] if value is None else part[layer] + (face[layer] * inverse[layer]) * value
        weighted = weight * value
        total = (weighted[0:8] + weighted[8:16]) + (weighted[16:24] + weighted[24:32])
        total = total * cell[layer]
        folded[layer] = total
        folded_own[layer] = total + jnp.where(keep, field[layer, 0:8], 0.0)
    near = folded_own[...].reshape(8 * NZ, LANES)
    far = folded[...].reshape(8 * NZ, LANES)
    ends[...] = dot_full(near, fold_own[...], ((0,), (0,))) + dot_full(far, fold_far[...], ((0,), (0,)))


def interface_kernel(ends, inverse, forward, backward, fold_own, face, out, source, part, folded):
    total = jnp.zeros((NZ, LANES), jnp.float32)
    for slot in range(4):
        block = ends[pl.ds(slot, SLABS, stride=4), :]
        turned = block.T
        total = total + dot_full(turned[:NZ], forward[0, slot], ((1,), (0,)))
        total = total + dot_full(turned[NZ:], forward[1, slot], ((1,), (0,)))
    source[...] = total
    value = None
    for layer in range(NZ):
        inv = inverse[layer]
        row = jnp.broadcast_to(source[layer : layer + 1, :], (SLABS, LANES))
        scaled = row * inv
        value = scaled if value is None else scaled + (face[layer - 1] * inv) * value
        part[layer] = value
    value = None
    for layer in reversed(range(NZ)):
        value = part[layer] if value is None else part[layer] + (face[layer] * inverse[layer]) * value
        folded[layer] = (value[0:8] + value[8:16]) + (value[16:24] + value[24:32])
    solved = dot_full(fold_own[...], folded[...].reshape(8 * NZ, LANES), ((0,), (0,)))
    lower = solved
    upper = jnp.concatenate([solved[NZ:], solved[:NZ]], axis=0)
    for slot in range(4):
        block = dot_full(backward[0, slot], lower, ((1,), (1,))) + dot_full(backward[1, slot], upper, ((1,), (1,)))
        out[pl.ds(slot, SLABS, stride=4), :] = block


def second_solve_kernel(place, field, ends, inverse, weights, cell, face, out0, out1, out2, out3, part, edges):
    chip = place[1]
    edges[...] = ends[...].T
    weight = weights[...]
    sublane = lax.broadcasted_iota(jnp.int32, (8, LANES), 0)
    sign = jnp.where(lax.rem(sublane, 2) == 1, 1.0, -1.0)
    keep = lax.broadcasted_iota(jnp.int32, (PLANES, LANES), 0) == 0
    value = None
    for layer in range(NZ):
        inv = inverse[layer]
        near = edges[layer : layer + 1, :]
        far = edges[NZ + layer : NZ + layer + 1, :]
        edge = (near + sign * far) * cell[layer]
        edge = jnp.concatenate([edge] * 4, axis=0)
        scaled = (field[layer] + weight * edge) * inv
        value = scaled if value is None else scaled + (face[layer - 1] * inv) * value
        part[layer] = value
    value = None
    for layer in reversed(range(NZ)):
        value = part[layer] if value is None else part[layer] + (face[layer] * inverse[layer]) * value
        part[layer] = jnp.where(keep, edges[layer : layer + 1, :], value)
    for step, out in enumerate((out0, out1, out2, out3)):
        block = lax.rem(chip + step, CHIPS)
        out[...] = part[pl.ds(block * LAYERS, LAYERS)]


def backward_kernel(place, in0, in1, in2, in3, table_high, table_low, slab_high, slab_low, out, modes):
    chip = place[1]
    rows = 8 * PLANES
    for step, source in enumerate((in0, in1, in2, in3)):
        block = lax.rem(chip + CHIPS - step, CHIPS)
        start = pl.multiple_of(block * LANES, LANES)
        modes[:, pl.ds(start, LANES)] = source[...].reshape(rows, LANES)
    slab = (slab_high[...], slab_low[...])
    table = (table_high[0], table_low[0])
    planes = dot_split(slab, split_values(modes[...]))
    out[...] = dot_split(split_values(planes), table).reshape(8, PLANES, HALF)


def whole(*shape):
    return pl.BlockSpec(shape, lambda step, place: (0,) * len(shape))


scalars = pl.BlockSpec(memory_space=pltpu.SMEM)


def call(kernel, place, inputs, in_specs, outs, scratch, flops=10_000_000, bytes_accessed=4_000_000):
    grid_spec = pltpu.PrefetchScalarGridSpec(
        num_scalar_prefetch=1,
        grid=(1,),
        in_specs=in_specs,
        out_specs=[whole(*shape) for shape in outs],
        scratch_shapes=[pltpu.VMEM(shape, jnp.float32) for shape in scratch],
    )
    return pl.pallas_call(
        kernel,
        grid_spec=grid_spec,
        out_shape=[jax.ShapeDtypeStruct(shape, jnp.float32) for shape in outs],
        compiler_params=pltpu.CompilerParams(vmem_limit_bytes=VMEM_LIMIT),
        cost_estimate=pl.CostEstimate(flops=flops, bytes_accessed=bytes_accessed, transcendentals=0),
    )(place, *inputs)


def body(charge, cell, face, screening):
    gx, gz = lax.axis_index("gx"), lax.axis_index("gz")
    core, chip = lax.rem(gz, 2), lax.div(gz, 2)
    place = jnp.stack([core, chip, 1 - core]).astype(jnp.int32)
    forward_y, backward_y = y_tables()
    fy_high, fy_low = split_pair(forward_y)
    by_high, by_low = split_pair(backward_y)
    basis = slab_basis()
    slab_high, slab_low = split_pair(np.kron(np.eye(8), basis))
    slab_forward, slab_backward, alias_shift = interface_tables()
    fold_own, fold_far = fold_tables()
    weights = near_weights()
    shift_y = y_shifts().astype(np.float32)
    slab_shift = (4.0 * np.sin(np.pi * np.arange(PLANES) / (2 * PLANES)) ** 2).astype(np.float32)

    mode_row = lax.dynamic_slice_in_dim(jnp.asarray(shift_y), gz, 1, 0)
    mode_shift = mode_row + jnp.asarray(slab_shift)[:, None]
    spread = np.repeat(shift_y.reshape(2 * CHIPS * SLABS, 4), SLABS, axis=1)
    alias_total = jnp.asarray(alias_shift) + lax.dynamic_slice_in_dim(jnp.asarray(spread), gz * SLABS + gx, 1, 0)

    cube = (LAYERS, PLANES, LANES)
    tall = (NZ, PLANES, LANES)
    square = (LANES, LANES)

    def pivots(shift):
        def kernel(place, *refs):
            pivot_kernel(*refs)

        return call(kernel, place, (shift, cell, face, screening), [whole(PLANES, LANES), scalars, scalars, scalars], [tall], [])[0]

    pair = [(s, s ^ 1) for s in range(2 * CHIPS)]

    def chip_shift(step):
        return [(s, (s + 2 * step) % (2 * CHIPS)) for s in range(2 * CHIPS)]

    sign = jnp.where(core == 0, 1.0, -1.0)
    lower, upper = charge[:, :, :HALF], charge[:, :, HALF:]
    kept = lower + sign * upper
    sent = lower - sign * upper
    other = lax.ppermute(sent, "gz", pair)
    table_spec = pl.BlockSpec((1, HALF, HALF), lambda step, place: (place[0], 0, 0))
    slab_spec = whole(8 * PLANES, 8 * PLANES)
    half_block = whole(8, PLANES, HALF)
    blocks = call(
        forward_kernel,
        place,
        (kept, other, fy_high, fy_low, slab_high, slab_low),
        [half_block, half_block, table_spec, table_spec, slab_spec, slab_spec],
        [cube] * 4,
        [(LAYERS * PLANES, HALF)],
    )
    arrived = [blocks[0]] + [lax.ppermute(blocks[step], "gz", chip_shift(step)) for step in (1, 2, 3)]
    inverse = pivots(mode_shift)
    alias_inverse = pivots(alias_total)
    field, ends = call(
        first_solve_kernel,
        place,
        (*arrived, inverse, weights, fold_own, fold_far, cell, face),
        [whole(*cube)] * 4 + [whole(*tall), whole(PLANES, LANES), whole(*fold_own.shape), whole(*fold_own.shape), scalars, scalars],
        [tall, square],
        [tall, (NZ, 8, LANES), (NZ, 8, LANES)],
    )
    ends = lax.all_to_all(ends.reshape(SLABS, 4, LANES), "gx", 0, 0, tiled=True).reshape(square)

    def interface(place, *refs):
        interface_kernel(*refs)

    ends = call(
        interface,
        place,
        (ends, alias_inverse, slab_forward, slab_backward, fold_own, face),
        [whole(*square), whole(*tall), whole(*slab_forward.shape), whole(*slab_forward.shape), whole(*fold_own.shape), scalars],
        [square],
        [(NZ, LANES), tall, (NZ, 8, LANES)],
    )[0]
    ends = lax.all_to_all(ends.reshape(SLABS, 4, LANES), "gx", 0, 0, tiled=True).reshape(square)
    solved = call(
        second_solve_kernel,
        place,
        (field, ends, inverse, weights, cell, face),
        [whole(*tall), whole(*square), whole(*tall), whole(PLANES, LANES), scalars, scalars],
        [cube] * 4,
        [tall, square],
    )
    arrived = [solved[0]] + [lax.ppermute(solved[step], "gz", chip_shift(step)) for step in (1, 2, 3)]

    def back(which):
        part_spec = pl.BlockSpec((8, PLANES, LANES), lambda step, place: (place[which], 0, 0))
        return call(
            backward_kernel,
            place,
            (*arrived, by_high, by_low, slab_high, slab_low),
            [part_spec] * 4 + [table_spec, table_spec, slab_spec, slab_spec],
            [(8, PLANES, HALF)],
            [(8 * PLANES, HALF)],
        )[0]

    sent = back(2)
    other = lax.ppermute(sent, "gz", pair)
    kept = back(0)
    return jnp.concatenate([kept + other, sign * (kept - other)], axis=2)


def solution(mesh):
    in_specs = (P("gz", "gx", None), P(), P(), P())
    out_specs = P("gz", "gx", None)
    return jax.shard_map(body, mesh=mesh, in_specs=in_specs, out_specs=out_specs, check_vma=False)
```

profile of v0, /device:TPU:1, one launch (start us, length us, event | category | flops | bytes accessed | tf_op | source)
XLA Modules:
  0.0 87.7 jit_solution(945494083379364614)
XLA Ops:
  0.0 1.5 %slice_subtract_fusion = (f32[8,32,512]{2,1,0:T(8,128)S(1)}, f32[8,32,512]{2,1,0:T(8,128)S(1)}) fusion(f32[8,32,1024]{2,1,0:T(8,128)} %param.19, f32[]{:T(128)S(6)} %select_n.10), kind=kLoop, calls=%fused_computation.3 | loop fusion | flops 393216 | bytes 2097156 | tf_op jit(solution)/shard_map/sub | solution.py:301
  1.5 3.3 %collective-permute-start = (f32[8,32,512]{2,1,0:T(8,128)S(1)}, f32[8,32,512]{2,1,0:T(8,128)S(1)}, u32[]{:S(2)}, u32[]{:S(2)}) collective-permute-start(f32[8,32,512]{2,1,0:T(8,128)S(1)} %get-tuple-element.27), channel_id=1, source_target_pairs={{0,1},{1,0},{2,3},{3,2},{4,5},{5,4},{6,7},{7,6},{8,9},{9,8},{10,11... | collective-permute-start | bytes 1572872 | tf_op jit(solution)/shard_map/ppermute | solution.py:302
  4.8 0.7 dynamic-slice_bitcast_fusion.1
  5.5 0.1 pad_add_fusion.place
  5.6 0.8 collective-permute-done.other
  6.3 0.0 copy-done.2
  6.3 0.0 copy-done.3
  6.4 1.2 %copy-done.5 = bf16[2,512,512]{2,1,0:T(8,128)(2,1)S(1)} copy-done((bf16[2,512,512]{2,1,0:T(8,128)(2,1)S(1)}, bf16[2,512,512]{2,1,0:T(8,128)(2,1)}, u32[]{:S(2)}) %copy-start.5) | copy-done | bytes 1048600
  7.6 2.5 %shard_map.181 = (f32[16,32,128]{2,1,0:T(8,128)S(1)}, f32[16,32,128]{2,1,0:T(8,128)S(1)}, f32[16,32,128]{2,1,0:T(8,128)S(1)}, f32[16,32,128]{2,1,0:T(8,128)S(1)}) custom-call(s32[3]{0:T(128)S(1)} %pad_add_fusion.place, f32[8,32,512]{2,1,0:T(8,128)S(1)} %get-tuple-element.28.own, f32[8,32,512]{2,1,0:T(8,128)S(1)} %collective-permute-done.other, ...), custom_call_target="tpu_custom_call" | custom-call | flops 10000000 | bytes 4000000 | tf_op jit(solution)/shard_map/pallas_call | solution.py:254
  10.1 0.1 collective-permute-start.1
  10.1 0.0 copy-start.16
  10.2 1.9 %collective-permute-start.2 = (f32[16,32,128]{2,1,0:T(8,128)S(1)}, f32[16,32,128]{2,1,0:T(8,128)S(1)}, u32[]{:S(2)}, u32[]{:S(2)}) collective-permute-start(f32[16,32,128]{2,1,0:T(8,128)S(1)} %get-tuple-element.17), channel_id=1, source_target_pairs={{0,4},{1,5},{2,6},{3,7},{4,0},{5,1},{6,2},{7,3},{8,12},{9,13},{10,... | collective-permute-start | bytes 786440 | tf_op jit(solution)/shard_map/ppermute | solution.py:314
  12.1 1.2 %collective-permute-start.3 = (f32[16,32,128]{2,1,0:T(8,128)S(1)}, f32[16,32,128]{2,1,0:T(8,128)S(1)}, u32[]{:S(2)}, u32[]{:S(2)}) collective-permute-start(f32[16,32,128]{2,1,0:T(8,128)S(1)} %get-tuple-element.18), channel_id=1, source_target_pairs={{0,6},{1,7},{2,0},{3,1},{4,2},{5,3},{6,4},{7,5},{8,14},{9,15},{10,... | collective-permute-start | bytes 786440 | tf_op jit(solution)/shard_map/ppermute | solution.py:314
  13.2 0.1 broadcast_add_fusion.1.refs_0_
  13.3 0.0 copy-done.13
  13.3 0.0 copy-start.6
  13.3 0.0 copy-start.8
  13.3 0.0 copy-start.11
  13.3 1.6 %shard_map.182.inverse = f32[64,32,128]{2,1,0:T(8,128)S(1)} custom-call(s32[3]{0:T(128)S(1)} %pad_add_fusion.place, f32[32,128]{1,0:T(8,128)S(1)} %broadcast_add_fusion.1.refs_0_, f32[64]{0:T(128)S(1)} %copy-done.13, f32[64]{0:T(128)S(1)} %copy-done.12, f32[64]{0:T(128)S(1)} %copy-done.14), custom_call_target="tpu_custom_call" | custom-call | flops 10000000 | bytes 4000000 | tf_op jit(solution)/shard_map/pallas_call | solution.py:254
  14.9 0.7 dynamic-slice_bitcast_fusion
  15.6 3.9 %collective-permute-done.1.in1 = f32[16,32,128]{2,1,0:T(8,128)S(1)} collective-permute-done((f32[16,32,128]{2,1,0:T(8,128)S(1)}, f32[16,32,128]{2,1,0:T(8,128)S(1)}, u32[]{:S(2)}, u32[]{:S(2)}) %collective-permute-start.1) | collective-permute-done | bytes 262176 | tf_op jit(solution)/shard_map/ppermute | solution.py:314
  19.6 4.2 %collective-permute-done.2.in2 = f32[16,32,128]{2,1,0:T(8,128)S(1)} collective-permute-done((f32[16,32,128]{2,1,0:T(8,128)S(1)}, f32[16,32,128]{2,1,0:T(8,128)S(1)}, u32[]{:S(2)}, u32[]{:S(2)}) %collective-permute-start.2) | collective-permute-done | bytes 262176 | tf_op jit(solution)/shard_map/ppermute | solution.py:314
  23.8 1.0 %collective-permute-done.3.in3 = f32[16,32,128]{2,1,0:T(8,128)S(1)} collective-permute-done((f32[16,32,128]{2,1,0:T(8,128)S(1)}, f32[16,32,128]{2,1,0:T(8,128)S(1)}, u32[]{:S(2)}, u32[]{:S(2)}) %collective-permute-start.3) | collective-permute-done | bytes 262176 | tf_op jit(solution)/shard_map/ppermute | solution.py:314
  24.8 0.0 copy-done.6
  24.8 0.0 copy-done.11
  24.8 2.7 %shard_map.183 = (f32[64,32,128]{2,1,0:T(8,128)S(1)}, f32[128,128]{1,0:T(8,128)}) custom-call(s32[3]{0:T(128)S(1)} %pad_add_fusion.place, f32[16,32,128]{2,1,0:T(8,128)S(1)} %get-tuple-element.15.in0, f32[16,32,128]{2,1,0:T(8,128)S(1)} %collective-permute-done.1.in1, f32[16,32,128]{2,1,0:T(8,128)S(1)} %collective-permute-done.2.in2, ...), custom_call_target="tpu_custom_call" | custom-call | flops 10000000 | bytes 4000000 | tf_op jit(solution)/shard_map/pallas_call | solution.py:254
  27.5 10.3 %all-to-all-start = ((f32[32,4,128]{2,1,0:T(4,128)}), f32[32,4,128]{2,1,0:T(4,128)S(1)}, u32[]{:S(2)}, u32[]{:S(2)}) async-start(f32[32,4,128]{2,1,0:T(4,128)} %bitcast.4), calls=%async_computation | async-start | bytes 131072 | tf_op jit(solution)/shard_map/all_to_all | solution.py:325
  37.8 0.0 copy-done.15
  37.8 1.6 %shard_map.184.refs_1_ = f32[64,32,128]{2,1,0:T(8,128)S(1)} custom-call(s32[3]{0:T(128)S(1)} %pad_add_fusion.place, f32[32,128]{1,0:T(8,128)S(1)} %broadcast_add_fusion.refs_0_, f32[64]{0:T(128)S(1)} %copy-done.13, f32[64]{0:T(128)S(1)} %copy-done.12, f32[64]{0:T(128)S(1)} %copy-done.14), custom_call_target="tpu_custom_call" | custom-call | flops 10000000 | bytes 4000000 | tf_op jit(solution)/shard_map/pallas_call | solution.py:254
  39.4 7.3 %all-to-all-done = f32[32,4,128]{2,1,0:T(4,128)S(1)} async-done(((f32[32,4,128]{2,1,0:T(4,128)}), f32[32,4,128]{2,1,0:T(4,128)S(1)}, u32[]{:S(2)}, u32[]{:S(2)}) %all-to-all-start) | async-done | bytes 65568 | tf_op jit(solution)/shard_map/all_to_all | solution.py:325
  46.7 0.9 %copy-done.7 = f32[512,128]{1,0:T(8,128)S(1)} copy-done((f32[512,128]{1,0:T(8,128)S(1)}, f32[512,128]{1,0:T(8,128)}, u32[]{:S(2)}) %copy-start.7) | copy-done | bytes 262168
  47.7 0.9 %copy-done.9 = f32[2,4,32,128]{3,2,1,0:T(8,128)S(1)} copy-done((f32[2,4,32,128]{3,2,1,0:T(8,128)S(1)}, f32[2,4,32,128]{3,2,1,0:T(8,128)}, u32[]{:S(2)}) %copy-start.9) | copy-done | bytes 131096
  48.6 0.9 %copy-done.10 = f32[2,4,32,128]{3,2,1,0:T(8,128)S(1)} copy-done((f32[2,4,32,128]{3,2,1,0:T(8,128)S(1)}, f32[2,4,32,128]{3,2,1,0:T(8,128)}, u32[]{:S(2)}) %copy-start.10) | copy-done | bytes 131096
  49.5 3.4 %shard_map.185 = f32[128,128]{1,0:T(8,128)S(1)} custom-call(s32[3]{0:T(128)S(1)} %pad_add_fusion.place, f32[128,128]{1,0:T(8,128)S(1)} %bitcast.11, f32[64,32,128]{2,1,0:T(8,128)S(1)} %shard_map.184.refs_1_, f32[2,4,32,128]{3,2,1,0:T(8,128)S(1)} %copy-done.9, f32[2,4,32,128]{3,2,1,0:T(8,128)S(1)} %copy-done.10, f32[512,128]{1,0:T(8,128)S(1)} %copy-done.7, ...), custom_call_target="tpu_custom_call" | custom-call | flops 10000000 | bytes 4000000 | tf_op jit(solution)/shard_map/pallas_call | solution.py:254
  52.9 12.0 %all_to_all.10 = f32[32,4,128]{2,1,0:T(4,128)S(1)} all-to-all(f32[32,4,128]{2,1,0:T(4,128)S(1)} %bitcast.13), channel_id=1, replica_groups=mesh['gx'=32,'gz'=8] {'gx'}, dimensions={0} | all-to-all | bytes 131072 | tf_op jit(solution)/shard_map/all_to_all | solution.py:338
  64.9 1.6 %shard_map.186 = (f32[16,32,128]{2,1,0:T(8,128)S(1)}, f32[16,32,128]{2,1,0:T(8,128)S(1)}, f32[16,32,128]{2,1,0:T(8,128)S(1)}, f32[16,32,128]{2,1,0:T(8,128)S(1)}) custom-call(s32[3]{0:T(128)S(1)} %pad_add_fusion.place, f32[64,32,128]{2,1,0:T(8,128)S(1)} %get-tuple-element.19.field, f32[128,128]{1,0:T(8,128)S(1)} %bitcast.12, ...), custom_call_target="tpu_custom_call" | custom-call | flops 10000000 | bytes 4000000 | tf_op jit(solution)/shard_map/pallas_call | solution.py:254
  66.5 1.1 %collective-permute-start.4 = (f32[16,32,128]{2,1,0:T(8,128)S(1)}, f32[16,32,128]{2,1,0:T(8,128)S(1)}, u32[]{:S(2)}, u32[]{:S(2)}) collective-permute-start(f32[16,32,128]{2,1,0:T(8,128)S(1)} %get-tuple-element.22), channel_id=1, source_target_pairs={{0,2},{1,3},{2,4},{3,5},{4,6},{5,7},{6,0},{7,1},{8,10},{9,11},{10,... | collective-permute-start | bytes 786440 | tf_op jit(solution)/shard_map/ppermute | solution.py:347
  67.7 2.8 %collective-permute-start.5 = (f32[16,32,128]{2,1,0:T(8,128)S(1)}, f32[16,32,128]{2,1,0:T(8,128)S(1)}, u32[]{:S(2)}, u32[]{:S(2)}) collective-permute-start(f32[16,32,128]{2,1,0:T(8,128)S(1)} %get-tuple-element.23), channel_id=1, source_target_pairs={{0,4},{1,5},{2,6},{3,7},{4,0},{5,1},{6,2},{7,3},{8,12},{9,13},{10,... | collective-permute-start | bytes 786440 | tf_op jit(solution)/shard_map/ppermute | solution.py:347
  70.5 0.3 collective-permute-start.6
  70.7 2.3 %collective-permute-done.4.in1 = f32[16,32,128]{2,1,0:T(8,128)S(1)} collective-permute-done((f32[16,32,128]{2,1,0:T(8,128)S(1)}, f32[16,32,128]{2,1,0:T(8,128)S(1)}, u32[]{:S(2)}, u32[]{:S(2)}) %collective-permute-start.4) | collective-permute-done | bytes 262176 | tf_op jit(solution)/shard_map/ppermute | solution.py:347
  73.1 6.0 %collective-permute-done.5.in2 = f32[16,32,128]{2,1,0:T(8,128)S(1)} collective-permute-done((f32[16,32,128]{2,1,0:T(8,128)S(1)}, f32[16,32,128]{2,1,0:T(8,128)S(1)}, u32[]{:S(2)}, u32[]{:S(2)}) %collective-permute-start.5) | collective-permute-done | bytes 262176 | tf_op jit(solution)/shard_map/ppermute | solution.py:347
  79.0 0.0 collective-permute-done.6.in3
  79.0 1.5 %shard_map.188 = f32[8,32,512]{2,1,0:T(8,128)S(1)} custom-call(s32[3]{0:T(128)S(1)} %pad_add_fusion.place, f32[16,32,128]{2,1,0:T(8,128)S(1)} %get-tuple-element.21.in0, f32[16,32,128]{2,1,0:T(8,128)S(1)} %collective-permute-done.4.in1, f32[16,32,128]{2,1,0:T(8,128)S(1)} %collective-permute-done.5.in2, f32[16,32,128]{2,1,0:T(8,128)S(1)} %collective-permute-done.6.in3, ...), custom_call_target="tpu_custom_call" | custom-call | flops 10000000 | bytes 4000000 | tf_op jit(solution)/shard_map/pallas_call | solution.py:254
  80.6 4.4 %collective-permute-start.7 = (f32[8,32,512]{2,1,0:T(8,128)S(1)}, f32[8,32,512]{2,1,0:T(8,128)S(1)}, u32[]{:S(2)}, u32[]{:S(2)}) collective-permute-start(f32[8,32,512]{2,1,0:T(8,128)S(1)} %shard_map.188), channel_id=1, source_target_pairs={{0,1},{1,0},{2,3},{3,2},{4,5},{5,4},{6,7},{7,6},{8,9},{9,8},{10,11... | collective-permute-start | bytes 1572872 | tf_op jit(solution)/shard_map/ppermute | solution.py:361
  85.0 1.5 %shard_map.187 = f32[8,32,512]{2,1,0:T(8,128)S(1)} custom-call(s32[3]{0:T(128)S(1)} %pad_add_fusion.place, f32[16,32,128]{2,1,0:T(8,128)S(1)} %get-tuple-element.21.in0, f32[16,32,128]{2,1,0:T(8,128)S(1)} %collective-permute-done.4.in1, f32[16,32,128]{2,1,0:T(8,128)S(1)} %collective-permute-done.5.in2, f32[16,32,128]{2,1,0:T(8,128)S(1)} %collective-permute-done.6.in3, ...), custom_call_target="tpu_custom_call" | custom-call | flops 10000000 | bytes 4000000 | tf_op jit(solution)/shard_map/pallas_call | solution.py:254
  86.5 0.0 collective-permute-done.7
  86.5 0.1 fusion
  86.6 1.1 %pad_maximum_fusion = f32[8,32,1024]{2,1,0:T(8,128)} fusion(f32[8,32,512]{2,1,0:T(8,128)S(1)} %get-tuple-element.26, f32[8,32,512]{2,1,0:T(8,128)S(1)} %get-tuple-element.25), kind=kLoop, calls=%fused_computation | loop fusion | flops 262144 | bytes 2097152 | tf_op jit(solution)/shard_map/concatenate | solution.py:363
  (21 shorter events, 0.0 us)
Async XLA Ops:
  0.0 6.3 %copy-start.2 = (bf16[256,256]{1,0:T(8,128)(2,1)S(1)}, bf16[256,256]{1,0:T(8,128)(2,1)}, u32[]{:S(2)}) copy-start(bf16[256,256]{1,0:T(8,128)(2,1)} %constant.64.clone.slab_high) | copy-start | bytes 393220
  0.0 6.3 %copy-start.3 = (bf16[256,256]{1,0:T(8,128)(2,1)S(1)}, bf16[256,256]{1,0:T(8,128)(2,1)}, u32[]{:S(2)}) copy-start(bf16[256,256]{1,0:T(8,128)(2,1)} %constant.65.clone.slab_low) | copy-start | bytes 393220
  0.0 6.3 %copy-start.4 = (bf16[2,512,512]{2,1,0:T(8,128)(2,1)S(1)}, bf16[2,512,512]{2,1,0:T(8,128)(2,1)}, u32[]{:S(2)}) copy-start(bf16[2,512,512]{2,1,0:T(8,128)(2,1)} %constant.62.clone.table_high) | copy-start | bytes 3145732
  1.5 4.9 %collective-permute-start = (f32[8,32,512]{2,1,0:T(8,128)S(1)}, f32[8,32,512]{2,1,0:T(8,128)S(1)}, u32[]{:S(2)}, u32[]{:S(2)}) collective-permute-start(f32[8,32,512]{2,1,0:T(8,128)S(1)} %get-tuple-element.27), channel_id=1, source_target_pairs={{0,1},{1,0},{2,3},{3,2},{4,5},{5,4},{6,7},{7,6},{8,9},{9,8},{10,11... | collective-permute-start | bytes 1572872 | tf_op jit(solution)/shard_map/ppermute | solution.py:302
  6.4 1.2 %copy-start.5 = (bf16[2,512,512]{2,1,0:T(8,128)(2,1)S(1)}, bf16[2,512,512]{2,1,0:T(8,128)(2,1)}, u32[]{:S(2)}) copy-start(bf16[2,512,512]{2,1,0:T(8,128)(2,1)} %constant.63.clone.table_low) | copy-start | bytes 3145732
  10.1 9.5 %collective-permute-start.1 = (f32[16,32,128]{2,1,0:T(8,128)S(1)}, f32[16,32,128]{2,1,0:T(8,128)S(1)}, u32[]{:S(2)}, u32[]{:S(2)}) collective-permute-start(f32[16,32,128]{2,1,0:T(8,128)S(1)} %get-tuple-element.16), channel_id=1, source_target_pairs={{0,2},{1,3},{2,4},{3,5},{4,6},{5,7},{6,0},{7,1},{8,10},{9,11},{10,... | collective-permute-start | bytes 786440 | tf_op jit(solution)/shard_map/ppermute | solution.py:314
  10.1 3.1 %copy-start.16 = (f32[32]{0:T(128)S(1)}, f32[32]{0:T(128)}, u32[]{:S(2)}) copy-start(f32[32]{0:T(128)} %constant.59.clone) | copy-start | bytes 388
  10.2 13.6 %collective-permute-start.2 = (f32[16,32,128]{2,1,0:T(8,128)S(1)}, f32[16,32,128]{2,1,0:T(8,128)S(1)}, u32[]{:S(2)}, u32[]{:S(2)}) collective-permute-start(f32[16,32,128]{2,1,0:T(8,128)S(1)} %get-tuple-element.17), channel_id=1, source_target_pairs={{0,4},{1,5},{2,6},{3,7},{4,0},{5,1},{6,2},{7,3},{8,12},{9,13},{10,... | collective-permute-start | bytes 786440 | tf_op jit(solution)/shard_map/ppermute | solution.py:314
  12.1 1.2 %copy-start.12 = (f32[64]{0:T(128)S(1)}, f32[64]{0:T(128)}, u32[]{:S(2)}) copy-start(f32[64]{0:T(128)} %face.3) | copy-start | bytes 772
  12.1 1.2 %copy-start.13 = (f32[64]{0:T(128)S(1)}, f32[64]{0:T(128)}, u32[]{:S(2)}) copy-start(f32[64]{0:T(128)} %cell.3) | copy-start | bytes 772
  12.1 1.2 %copy-start.14 = (f32[64]{0:T(128)S(1)}, f32[64]{0:T(128)}, u32[]{:S(2)}) copy-start(f32[64]{0:T(128)} %refs_3_.4) | copy-start | bytes 772
  12.1 12.7 %collective-permute-start.3 = (f32[16,32,128]{2,1,0:T(8,128)S(1)}, f32[16,32,128]{2,1,0:T(8,128)S(1)}, u32[]{:S(2)}, u32[]{:S(2)}) collective-permute-start(f32[16,32,128]{2,1,0:T(8,128)S(1)} %get-tuple-element.18), channel_id=1, source_target_pairs={{0,6},{1,7},{2,0},{3,1},{4,2},{5,3},{6,4},{7,5},{8,14},{9,15},{10,... | collective-permute-start | bytes 786440 | tf_op jit(solution)/shard_map/ppermute | solution.py:314
  13.3 11.5 %copy-start.6 = (f32[512,128]{1,0:T(8,128)S(1)}, f32[512,128]{1,0:T(8,128)}, u32[]{:S(2)}) copy-start(f32[512,128]{1,0:T(8,128)} %constant.67.clone.fold_own.refs_4_) | copy-start | bytes 786436
  13.3 11.5 %copy-start.8 = (f32[512,128]{1,0:T(8,128)S(1)}, f32[512,128]{1,0:T(8,128)}, u32[]{:S(2)}) copy-start(f32[512,128]{1,0:T(8,128)} %constant.68.clone.fold_far) | copy-start | bytes 786436
  13.3 11.4 %copy-start.11 = (f32[32,128]{1,0:T(8,128)S(1)}, f32[32,128]{1,0:T(8,128)}, u32[]{:S(2)}) copy-start(f32[32,128]{1,0:T(8,128)} %constant.66.clone.weights) | copy-start | bytes 49156
  27.5 10.3 %copy-start.15 = (f32[32,128]{1,0:T(8,128)S(1)}, f32[32,128]{1,0:T(8,128)}, u32[]{:S(2)}) copy-start(f32[32,128]{1,0:T(8,128)} %constant.60.clone) | copy-start | bytes 49156
  27.5 19.2 %all-to-all-start = ((f32[32,4,128]{2,1,0:T(4,128)}), f32[32,4,128]{2,1,0:T(4,128)S(1)}, u32[]{:S(2)}, u32[]{:S(2)}) async-start(f32[32,4,128]{2,1,0:T(4,128)} %bitcast.4), calls=%async_computation | async-start | bytes 131072 | tf_op jit(solution)/shard_map/all_to_all | solution.py:325
  46.7 1.0 %copy-start.7 = (f32[512,128]{1,0:T(8,128)S(1)}, f32[512,128]{1,0:T(8,128)}, u32[]{:S(2)}) copy-start(f32[512,128]{1,0:T(8,128)} %constant.67.clone.fold_own.refs_4_) | copy-start | bytes 786436
  47.7 0.9 %copy-start.9 = (f32[2,4,32,128]{3,2,1,0:T(8,128)S(1)}, f32[2,4,32,128]{3,2,1,0:T(8,128)}, u32[]{:S(2)}) copy-start(f32[2,4,32,128]{3,2,1,0:T(8,128)} %constant.69.clone.refs_2_) | copy-start | bytes 393220
  48.6 0.9 %copy-start.10 = (f32[2,4,32,128]{3,2,1,0:T(8,128)S(1)}, f32[2,4,32,128]{3,2,1,0:T(8,128)}, u32[]{:S(2)}) copy-start(f32[2,4,32,128]{3,2,1,0:T(8,128)} %constant.70.clone.refs_3_) | copy-start | bytes 393220
  64.9 14.2 %copy-start = (bf16[2,512,512]{2,1,0:T(8,128)(2,1)S(1)}, bf16[2,512,512]{2,1,0:T(8,128)(2,1)}, u32[]{:S(2)}) copy-start(bf16[2,512,512]{2,1,0:T(8,128)(2,1)} %constant.71.clone.table_high) | copy-start | bytes 3145732
  64.9 14.2 %copy-start.1 = (bf16[2,512,512]{2,1,0:T(8,128)(2,1)S(1)}, bf16[2,512,512]{2,1,0:T(8,128)(2,1)}, u32[]{:S(2)}) copy-start(bf16[2,512,512]{2,1,0:T(8,128)(2,1)} %constant.72.clone.table_low) | copy-start | bytes 3145732
  66.5 6.5 %collective-permute-start.4 = (f32[16,32,128]{2,1,0:T(8,128)S(1)}, f32[16,32,128]{2,1,0:T(8,128)S(1)}, u32[]{:S(2)}, u32[]{:S(2)}) collective-permute-start(f32[16,32,128]{2,1,0:T(8,128)S(1)} %get-tuple-element.22), channel_id=1, source_target_pairs={{0,2},{1,3},{2,4},{3,5},{4,6},{5,7},{6,0},{7,1},{8,10},{9,11},{10,... | collective-permute-start | bytes 786440 | tf_op jit(solution)/shard_map/ppermute | solution.py:347
  67.7 11.4 %collective-permute-start.5 = (f32[16,32,128]{2,1,0:T(8,128)S(1)}, f32[16,32,128]{2,1,0:T(8,128)S(1)}, u32[]{:S(2)}, u32[]{:S(2)}) collective-permute-start(f32[16,32,128]{2,1,0:T(8,128)S(1)} %get-tuple-element.23), channel_id=1, source_target_pairs={{0,4},{1,5},{2,6},{3,7},{4,0},{5,1},{6,2},{7,3},{8,12},{9,13},{10,... | collective-permute-start | bytes 786440 | tf_op jit(solution)/shard_map/ppermute | solution.py:347
  70.5 8.5 %collective-permute-start.6 = (f32[16,32,128]{2,1,0:T(8,128)S(1)}, f32[16,32,128]{2,1,0:T(8,128)S(1)}, u32[]{:S(2)}, u32[]{:S(2)}) collective-permute-start(f32[16,32,128]{2,1,0:T(8,128)S(1)} %get-tuple-element.24), channel_id=1, source_target_pairs={{0,6},{1,7},{2,0},{3,1},{4,2},{5,3},{6,4},{7,5},{8,14},{9,15},{10,... | collective-permute-start | bytes 786440 | tf_op jit(solution)/shard_map/ppermute | solution.py:347
  80.6 6.0 %collective-permute-start.7 = (f32[8,32,512]{2,1,0:T(8,128)S(1)}, f32[8,32,512]{2,1,0:T(8,128)S(1)}, u32[]{:S(2)}, u32[]{:S(2)}) collective-permute-start(f32[8,32,512]{2,1,0:T(8,128)S(1)} %shard_map.188), channel_id=1, source_target_pairs={{0,1},{1,0},{2,3},{3,2},{4,5},{5,4},{6,7},{7,6},{8,9},{9,8},{10,11... | collective-permute-start | bytes 1572872 | tf_op jit(solution)/shard_map/ppermute | solution.py:361
where the time goes:
time: 88.1 us; the launch traced here: 87.7 us
  waiting for transfers between devices  25.5 us (29%)
  starting transfers between devices  25.4 us (29%)
  Pallas kernels  16.5 us (19%)
  blocking collectives  12 us (14%)
  local copies, waits for them, and re-layouts  5.43 us (6%)
  other arithmetic  2.79 us (3%)
    pallas_call x8, Pallas kernels, call(): pl.pallas_call(kernel, grid_spec=grid_spec, out_shape=[jax.ShapeDtypeStru...  16.5 us
    all_to_all x1, blocking collectives, body(): lax.all_to_all(ends.reshape(SLABS, 4, LANES), 'gx', 0, 0, tiled=True)  12 us
    all_to_all x1, starting transfers between devices, body(): lax.all_to_all(ends.reshape(SLABS, 4, LANES), 'gx', 0, 0, tiled=True)  10.3 us
    ppermute x3, waiting for transfers between devices, body(): lax.ppermute(blocks[step], 'gz', chip_shift(step))  9.12 us
    ppermute x3, waiting for transfers between devices, body(): lax.ppermute(solved[step], 'gz', chip_shift(step))  8.29 us
    ppermute x2, starting transfers between devices, body(): other = lax.ppermute(sent, 'gz', pair)  7.74 us
    all_to_all x1, waiting for transfers between devices, body(): lax.all_to_all(ends.reshape(SLABS, 4, LANES), 'gx', 0, 0, tiled=True)  7.3 us
    ppermute x3, starting transfers between devices, body(): lax.ppermute(solved[step], 'gz', chip_shift(step))  4.22 us
  transfers between devices with their start and end apart: 9, of which 7 were waited for; matrix products, arithmetic and copies ran while one was open for 2% of the time, Pallas kernels for 5%

commit v1 on v0

v1 whole, which is shorter than its diff:
```python
import functools
import math

import jax
import jax.numpy as jnp
import ml_dtypes
import numpy as np
from jax import lax
from jax.experimental import pallas as pl
from jax.experimental.pallas import tpu as pltpu
from jax.sharding import PartitionSpec as P

NX, NY, NZ = 1024, 1024, 64
SLABS, PLANES = 32, 32
HALF = NY // 2
CHIPS = 4
LAYERS = NZ // CHIPS
PEERS = SLABS * CHIPS
PARTS = 4
LANES = 128
highest = lax.Precision.HIGHEST
VMEM_LIMIT = 48 * 1024 * 1024


def split_pair(table):
    high = table.astype(np.float32).astype(ml_dtypes.bfloat16)
    low = (table - high.astype(np.float64)).astype(np.float32).astype(ml_dtypes.bfloat16)
    return high, low


def y_frequencies():
    index = np.arange(HALF)
    even = np.where(index <= HALF // 2, 2 * index, 2 * (index - HALF // 2))
    odd = np.where(index < HALF // 2, 2 * index + 1, 2 * (index - HALF // 2) + 1)
    even_is_cos = index <= HALF // 2
    odd_is_cos = index < HALF // 2
    return np.stack([even, odd]), np.stack([even_is_cos, odd_is_cos])


def y_tables():
    freq, is_cos = y_frequencies()
    point = np.arange(HALF)
    angle = 2.0 * np.pi * (point[None, :, None] * freq[:, None, :] % NY) / NY
    forward = np.where(is_cos[:, None, :], np.cos(angle), np.sin(angle))
    weight = np.where((freq == 0) | (freq == NY // 2), 1.0 / NY, 2.0 / NY)
    backward = np.swapaxes(forward * weight[:, None, :], 1, 2)
    return forward, backward


def y_shifts():
    freq, _ = y_frequencies()
    return (4.0 * np.sin(np.pi * freq / NY) ** 2).astype(np.float32)


def slab_basis():
    index = np.arange(PLANES)
    basis = math.sqrt(2.0 / PLANES) * np.sin(np.pi * np.outer(index, index) / PLANES)
    basis[0, :] = 0.0
    basis[:, 0] = 0.0
    basis[0, 0] = 1.0
    return basis


def slab_shifts():
    return (4.0 * np.sin(np.pi * np.arange(PLANES) / (2 * PLANES)) ** 2).astype(np.float32)


def near_weights():
    weight = slab_basis()[1].copy()
    weight[0] = 0.0
    return weight.astype(np.float32)


def far_signs():
    return np.where(np.arange(PLANES) % 2 == 1, 1.0, -1.0).astype(np.float32)


def interface_tables():
    mode = np.arange(SLABS)
    freq = np.where(mode <= SLABS // 2, mode, mode - SLABS // 2)
    is_cos = mode <= SLABS // 2
    weight = np.where((freq == 0) | (freq == SLABS // 2), 1.0, 2.0) / SLABS / SLABS

    def basis(offset):
        angle = 2.0 * np.pi * ((np.arange(SLABS)[:, None] + offset) * freq[None, :] % SLABS) / SLABS
        return np.where(is_cos[None, :], np.cos(angle), np.sin(angle))

    forward = np.concatenate([np.tile(basis(0), (1, 4)), np.tile(basis(1), (1, 4))], axis=1)
    high, low = split_pair(forward)
    backward = np.concatenate([np.tile(basis(0) * weight, (1, 4)), np.tile(basis(1) * weight, (1, 4))], axis=0)
    alias = freq[None, None, :] + SLABS * (np.arange(8)[:, None, None] + 8 * np.arange(4)[None, :, None])
    alias_shift = 4.0 * np.sin(np.pi * alias / NX) ** 2
    return (
        np.concatenate([high, low, high], axis=0),
        backward.astype(np.float32),
        alias_shift.reshape(8, LANES).astype(np.float32),
    )


def fold_table():
    fold = np.zeros((2, LAYERS, LAYERS, 8), np.float32)
    for layer in range(LAYERS):
        fold[0, layer, layer, :] = 1.0
        fold[1, layer, layer, :] = far_signs()[:8]
    return fold.reshape(2 * LAYERS, 8 * LAYERS).astype(ml_dtypes.bfloat16)


def spread_tables():
    spread = np.zeros((CHIPS, LAYERS, CHIPS, 2, PARTS, LAYERS), np.float32)
    for chip in range(CHIPS):
        for layer in range(LAYERS):
            spread[chip, layer, chip, :, :, layer] = 1.0
    mask = np.zeros((PARTS, PLANES, 2, PARTS, LAYERS), np.float32)
    for part in range(PARTS):
        mask[part, :, 0, part, :] = near_weights()[:, None]
        mask[part, :, 1, part, :] = (near_weights() * far_signs())[:, None]
    return spread.reshape(NZ, CHIPS * LANES), mask.reshape(LANES, LANES)


def split_values(values):
    high = values.astype(jnp.bfloat16)
    low = (values - high.astype(jnp.float32)).astype(jnp.bfloat16)
    return high, low


def dot_split(left, right, contract=((1,), (0,))):
    left_high, left_low = left
    right_high, right_low = right

    def dot(one, two):
        return lax.dot_general(one, two, (contract, ((), ())), preferred_element_type=jnp.float32)

    return dot(left_high, right_high) + (dot(left_high, right_low) + dot(left_low, right_high))


def dot_full(left, right, contract):
    return lax.dot_general(
        left, right, (contract, ((), ())), precision=highest, preferred_element_type=jnp.float32
    )


def pivot_kernel(place, shift_row, shift_col, cell, face, screening, out):
    base = place[1] * LAYERS
    shifts = shift_col[...] + shift_row[0]
    previous = None
    for layer in range(1, LAYERS):
        below, above = face[base + layer - 1], face[base + layer]
        pivot = (below + above + screening[base + layer]) + cell[base + layer] * shifts
        if previous is not None:
            pivot = pivot - (below * below) * previous
        previous = 1.0 / pivot
        out[layer] = previous


def stack_parts(values):
    return jnp.concatenate([values[:, part * LANES : (part + 1) * LANES] for part in range(PARTS)], axis=0).T


def unstack_parts(values):
    turned = values.T
    return jnp.concatenate([turned[part * PLANES : (part + 1) * PLANES] for part in range(PARTS)], axis=1)


def forward_kernel(place, own, other, table_high, table_low, slab_high, slab_low, inverse, weights, fold, cell, face, modes, out, part, folded):
    core, base = place[0], place[1] * LAYERS
    rows = 8 * PLANES
    own_rows = own[...].reshape(rows, HALF)
    other_rows = other[...].reshape(rows, HALF)
    slab = (slab_high[...], slab_low[...])
    table = (table_high[0], table_low[0])
    for half in range(2):
        values = jnp.where(core == half, own_rows, other_rows)
        spectrum = dot_split(split_values(values), table)
        modes[half * 8 : (half + 1) * 8] = dot_split(slab, split_values(spectrum)).reshape(8, PLANES, HALF)
    value = None
    for layer in range(1, LAYERS):
        inv = inverse[layer]
        scaled = modes[layer] * inv
        value = scaled if value is None else scaled + (face[base + layer - 1] * inv) * value
        part[layer] = value
    weight = weights[...]
    value = None
    folded[0:8] = jnp.zeros((8, HALF), jnp.float32)
    for layer in reversed(range(1, LAYERS)):
        value = part[layer] if value is None else part[layer] + (face[base + layer] * inverse[layer]) * value
        if layer == LAYERS - 1:
            out[pl.ds(1, PEERS, stride=4), :] = stack_parts(face[base + layer] * value)
        weighted = weight * value
        total = (weighted[0:8] + weighted[8:16]) + (weighted[16:24] + weighted[24:32])
        folded[layer * 8 : (layer + 1) * 8] = total * cell[base + layer]
    out[pl.ds(0, PEERS, stride=4), :] = stack_parts(modes[0] + face[base] * value)
    high, low = split_values(folded[...])
    sums = jnp.dot(fold[...], high, preferred_element_type=jnp.float32) + jnp.dot(fold[...], low, preferred_element_type=jnp.float32)
    planes = jnp.concatenate([modes[layer, 0:1] for layer in range(LAYERS)], axis=0)
    near = sums[:LAYERS] + planes
    far = sums[LAYERS:]
    blocks = [half[:, step * LANES : (step + 1) * LANES] for half in (near, far) for step in range(PARTS)]
    out[pl.ds(2, PEERS, stride=4), :] = jnp.concatenate(blocks, axis=0).T
    out[pl.ds(3, PEERS, stride=4), :] = jnp.zeros((PEERS, LANES), jnp.float32)


def prepare_kernel(place, shift_y, alias_shift, mode_shift, spread, mask, cell, face, screening, alias_inverse, response_high, response_low, corners, inverses, columns, scaled):
    start = place[0] * HALF + place[3]
    values = [shift_y[start + part * PEERS] for part in range(PARTS)]
    alias = jnp.concatenate([alias_shift[...] + value for value in values], axis=0)
    lane = lax.broadcasted_iota(jnp.int32, (8, LANES), 1)
    mode = jnp.broadcast_to(mode_shift[...], (8, LANES))
    for part in range(PARTS):
        mode = mode + jnp.where(lax.div(lane, PLANES) == part, values[part], 0.0)
    shifts = jnp.concatenate([alias, mode], axis=0)
    row = lax.broadcasted_iota(jnp.int32, (8, LANES), 0)
    previous = None
    value = None
    for layer in range(NZ):
        below = face[layer - 1] if layer > 0 else face[NZ - 1]
        pivot = (below + face[layer] + screening[layer]) + cell[layer] * shifts
        if previous is not None:
            pivot = pivot - (below * below) * previous
        previous = 1.0 / pivot
        alias_inverse[layer] = previous[: 8 * PARTS]
        inv = previous[8 * PARTS :]
        inverses[layer] = inv
        fresh = jnp.where(row == layer // LAYERS, inv, 0.0) if layer % LAYERS == 0 else None
        if value is None:
            value = fresh
        else:
            value = (face[layer - 1] * inv) * value
            if fresh is not None:
                value = value + fresh
        columns[layer] = value
    value = None
    for layer in reversed(range(NZ)):
        value = columns[layer] if value is None else columns[layer] + (face[layer] * inverses[layer]) * value
        scaled[layer * 8 : (layer + 1) * 8] = cell[layer] * value
        if layer % LAYERS == 0:
            corners[layer // LAYERS] = value
    weight = jnp.concatenate([mask[...]] * CHIPS, axis=1)
    for chip in range(CHIPS):
        column = scaled[pl.ds(chip, NZ, stride=8), :]
        response = dot_full(column, spread[...], ((0,), (0,))) * weight
        high, low = split_values(response)
        response_high[chip * LANES : (chip + 1) * LANES, :] = high
        response_low[chip * LANES : (chip + 1) * LANES, :] = low


def interface_kernel(place, arrived, response_high, response_low, corners, alias_inverse, forward, backward, face, out, source, part, solved):
    def rows(chip, slot):
        return pl.ds(4 * chip + slot, SLABS, stride=4 * CHIPS)

    sides = []
    for chip in range(CHIPS):
        side = arrived[rows(chip, 0), :]
        sides.append(side + arrived[rows(chip - 1, 1), :] if chip > 0 else side)
    response = (response_high[...], response_low[...])
    sums = dot_split(split_values(jnp.concatenate(sides, axis=1)), response)
    sums = sums + jnp.concatenate([arrived[rows(chip, 2), :] for chip in range(CHIPS)], axis=1)
    high, low = split_values(sums)
    stacked = jnp.concatenate([high, high, low], axis=0)
    turned = lax.dot_general(stacked, forward[...], (((0,), (0,)), ((), ())), preferred_element_type=jnp.float32)
    half = PARTS * LAYERS
    for chip in range(CHIPS):
        at = chip * LANES
        source[chip * half : (chip + 1) * half, :] = turned[at : at + half, :LANES] + turned[at + half : at + LANES, LANES:]
    value = None
    for layer in range(NZ):
        inv = alias_inverse[layer]
        first = (layer // LAYERS) * half + layer % LAYERS
        row = jnp.concatenate(
            [jnp.broadcast_to(source[first + step * LAYERS : first + step * LAYERS + 1, :], (8, LANES)) for step in range(PARTS)], axis=0
        )
        scaled = row * inv
        value = scaled if value is None else scaled + (face[layer - 1] * inv) * value
        part[layer] = value
    value = None
    for layer in reversed(range(NZ)):
        value = part[layer] if value is None else part[layer] + (face[layer] * alias_inverse[layer]) * value
        first = (layer // LAYERS) * half + layer % LAYERS
        solved[pl.ds(first, PARTS, stride=LAYERS), :] = jnp.sum(value.reshape(PARTS, 8, LANES), axis=1)
    planes = dot_full(backward[...], solved[...], ((1,), (1,)))
    own = []
    for chip in range(CHIPS):
        at = chip * half
        own.append(jnp.concatenate([planes[:SLABS, at : at + half], planes[SLABS:, at : at + half]], axis=1))
    change = dot_split(split_values(jnp.concatenate(own, axis=1)), response, ((1,), (1,)))
    ends = []
    for chip in range(CHIPS):
        end = change[:, chip * LANES : (chip + 1) * LANES]
        for other in range(CHIPS):
            end = end + corners[chip, other : other + 1, :] * sides[other]
        ends.append(end)
    nothing = jnp.zeros((SLABS, LANES), jnp.float32)
    ends.append(nothing)
    for chip in range(CHIPS):
        out[rows(chip, 0), :] = ends[chip]
        out[rows(chip, 1), :] = ends[chip + 1]
        out[rows(chip, 2), :] = own[chip]
        out[rows(chip, 3), :] = nothing


def second_solve_kernel(place, modes, arrived, inverse, weights, signs, table_high, table_low, slab_high, slab_low, cell, face, kept, sent, part, near, edge):
    core, base = place[0], place[1] * LAYERS
    below = unstack_parts(arrived[pl.ds(0, PEERS, stride=4), :])
    above = unstack_parts(arrived[pl.ds(1, PEERS, stride=4), :])
    turned = arrived[pl.ds(2, PEERS, stride=4), :].T
    for which, target in enumerate((near, edge)):
        for step in range(PARTS):
            at = (which * PARTS + step) * LAYERS
            target[:, step * LANES : (step + 1) * LANES] = turned[at : at + LAYERS]
    weight = weights[...]
    signed = signs[...]
    keep = lax.broadcasted_iota(jnp.int32, (PLANES, HALF), 0) == 0
    value = None
    for layer in range(1, LAYERS):
        inv = inverse[layer]
        both = (near[layer : layer + 1, :] * weight + edge[layer : layer + 1, :] * signed) * cell[base + layer]
        right = modes[layer] + both
        if layer == 1:
            right = right + face[base] * below
        if layer == LAYERS - 1:
            right = right + face[base + layer] * above
        scaled = right * inv
        value = scaled if value is None else scaled + (face[base + layer - 1] * inv) * value
        part[layer] = value
    value = None
    for layer in reversed(range(1, LAYERS)):
        value = part[layer] if value is None else part[layer] + (face[base + layer] * inverse[layer]) * value
        part[layer] = jnp.where(keep, near[layer : layer + 1, :], value)
    part[0] = jnp.where(keep, near[0:1, :], below)
    rows = 8 * PLANES
    kept[...] = part[pl.ds(core * 8, 8)]
    other = part[pl.ds((1 - core) * 8, 8)].reshape(rows, HALF)
    planes = dot_split((slab_high[...], slab_low[...]), split_values(other))
    sent[...] = dot_split(split_values(planes), (table_high[0], table_low[0])).reshape(8, PLANES, HALF)


def backward_kernel(place, modes, table_high, table_low, slab_high, slab_low, out):
    rows = 8 * PLANES
    planes = dot_split((slab_high[...], slab_low[...]), split_values(modes[...].reshape(rows, HALF)))
    out[...] = dot_split(split_values(planes), (table_high[0], table_low[0])).reshape(8, PLANES, HALF)


def whole(*shape):
    return pl.BlockSpec(shape, lambda step, place: (0,) * len(shape))


scalars = pl.BlockSpec(memory_space=pltpu.SMEM)


def call(kernel, place, inputs, in_specs, outs, scratch, cost=10_000_000):
    outs = [out if isinstance(out, jax.ShapeDtypeStruct) else jax.ShapeDtypeStruct(out, jnp.float32) for out in outs]
    grid_spec = pltpu.PrefetchScalarGridSpec(
        num_scalar_prefetch=1,
        grid=(1,),
        in_specs=in_specs,
        out_specs=[whole(*out.shape) for out in outs],
        scratch_shapes=[pltpu.VMEM(shape, jnp.float32) for shape in scratch],
    )
    return pl.pallas_call(
        kernel,
        grid_spec=grid_spec,
        out_shape=outs,
        compiler_params=pltpu.CompilerParams(vmem_limit_bytes=VMEM_LIMIT),
        cost_estimate=pl.CostEstimate(flops=cost, bytes_accessed=4_000_000, transcendentals=0),
    )(place, *inputs)


def body(charge, cell, face, screening):
    gx, gz = lax.axis_index("gx"), lax.axis_index("gz")
    core, chip = lax.rem(gz, 2), lax.div(gz, 2)
    place = jnp.stack([core, chip, 1 - core, gx * CHIPS + chip]).astype(jnp.int32)
    forward_y, backward_y = y_tables()
    fy_high, fy_low = split_pair(forward_y)
    by_high, by_low = split_pair(backward_y)
    slab_high, slab_low = split_pair(np.kron(np.eye(8), slab_basis()))
    forward_slab, backward_slab, alias_shift = interface_tables()
    spread, mask = spread_tables()
    weights = np.broadcast_to(near_weights()[:, None], (PLANES, HALF)).copy()
    signs = weights * far_signs()[:, None]
    shift_y = y_shifts()
    mode_shift = np.tile(slab_shifts(), PARTS)[None, :]

    cube = (8, PLANES, HALF)
    field = (LAYERS, PLANES, HALF)
    message = (4 * PEERS, LANES)
    square = (CHIPS * LANES, CHIPS * LANES)
    groups = [[x * 2 * CHIPS + 2 * c + r for x in range(SLABS) for c in range(CHIPS)] for r in range(2)]

    def exchange(values):
        blocks = values.reshape(PEERS, 4, LANES)
        return lax.all_to_all(blocks, ("gx", "gz"), 0, 0, axis_index_groups=groups, tiled=True).reshape(message)

    pair = [(s, s ^ 1) for s in range(2 * CHIPS)]
    sign = jnp.where(core == 0, 1.0, -1.0)
    lower, upper = charge[:, :, :HALF], charge[:, :, HALF:]
    own = lower + sign * upper
    other = lax.ppermute(lower - sign * upper, "gz", pair)
    row_spec = pl.BlockSpec((1, 1, HALF), lambda step, place: (place[0], 0, 0))
    table_spec = pl.BlockSpec((1, HALF, HALF), lambda step, place: (place[0], 0, 0))
    slab_spec = whole(8 * PLANES, 8 * PLANES)
    inverse = call(
        pivot_kernel,
        place,
        (shift_y[:, None, :], np.broadcast_to(slab_shifts()[:, None], (PLANES, HALF)).copy(), cell, face, screening),
        [row_spec, whole(PLANES, HALF), scalars, scalars, scalars],
        [field],
        [],
    )[0]
    modes, ends = call(
        forward_kernel,
        place,
        (own, other, fy_high, fy_low, slab_high, slab_low, inverse, weights, fold_table(), cell, face),
        [whole(*cube)] * 2 + [table_spec] * 2 + [slab_spec] * 2
        + [whole(*field), whole(PLANES, HALF), whole(2 * LAYERS, 8 * LAYERS), scalars, scalars],
        [field, message],
        [field, (8 * LAYERS, HALF)],
    )
    alias_inverse, response_high, response_low, corners = call(
        prepare_kernel,
        place,
        (shift_y.reshape(-1), alias_shift, mode_shift, spread, mask, cell, face, screening),
        [scalars, whole(8, LANES), whole(1, LANES), whole(*spread.shape), whole(*mask.shape), scalars, scalars, scalars],
        [(NZ, 8 * PARTS, LANES), jax.ShapeDtypeStruct(square, jnp.bfloat16), jax.ShapeDtypeStruct(square, jnp.bfloat16), (CHIPS, 8, LANES)],
        [(NZ, 8, LANES), (NZ, 8, LANES), (8 * NZ, LANES)],
    )
    ends = exchange(ends)
    ends = call(
        interface_kernel,
        place,
        (ends, response_high, response_low, corners, alias_inverse, forward_slab, backward_slab, face),
        [whole(*message), whole(*square), whole(*square), whole(CHIPS, 8, LANES), whole(NZ, 8 * PARTS, LANES)]
        + [whole(*forward_slab.shape), whole(*backward_slab.shape), scalars],
        [message],
        [(CHIPS * PARTS * LAYERS, LANES), (NZ, 8 * PARTS, LANES), (CHIPS * PARTS * LAYERS, LANES)],
    )[0]
    ends = exchange(ends)
    kept, sent = call(
        second_solve_kernel,
        place,
        (modes, ends, inverse, weights, signs, by_high, by_low, slab_high, slab_low, cell, face),
        [whole(*field), whole(*message), whole(*field), whole(PLANES, HALF), whole(PLANES, HALF)]
        + [table_spec] * 2 + [slab_spec] * 2 + [scalars] * 2,
        [cube, cube],
        [field, (LAYERS, HALF), (LAYERS, HALF)],
    )
    other = lax.ppermute(sent, "gz", pair)
    kept = call(
        backward_kernel,
        place,
        (kept, by_high, by_low, slab_high, slab_low),
        [whole(*cube)] + [table_spec] * 2 + [slab_spec] * 2,
        [cube],
        [],
    )[0]
    return jnp.concatenate([kept + other, sign * (kept - other)], axis=2)


def solution(mesh):
    in_specs = (P("gz", "gx", None), P(), P(), P())
    out_specs = P("gz", "gx", None)
    return jax.shard_map(body, mesh=mesh, in_specs=in_specs, out_specs=out_specs, check_vma=False)
```

time: 88.1 us -> 73.2 us (0.83)
  waiting for transfers between devices: 25.5 us -> 9.74 us
  blocking collectives: 12 us -> 18.5 us
  starting transfers between devices: 25.4 us -> 20.8 us
  Pallas kernels: 16.5 us -> 14.5 us
    ppermute x6 -> x1, waiting for transfers between devices: 17.4 us -> 0.01 us  [body(): other = lax.ppermute(lower - sign * upper, 'gz', pair)]
    all_to_all x1, blocking collectives: 12 us -> 18.5 us  [exchange(): lax.all_to_all(blocks, ('gx', 'gz'), 0, 0, axis_index_groups=groups, tile...]
    ppermute x6 -> x1, starting transfers between devices: 7.36 us -> 3.24 us  [body(): other = lax.ppermute(lower - sign * upper, 'gz', pair)]
    ppermute x2 -> x1, starting transfers between devices: 7.74 us -> 3.66 us  [body(): other = lax.ppermute(sent, 'gz', pair)]
    all_to_all x1, starting transfers between devices: 10.3 us -> 13.9 us  [exchange(): lax.all_to_all(blocks, ('gx', 'gz'), 0, 0, axis_index_groups=groups, tile...]
    all_to_all x1, waiting for transfers between devices: 7.3 us -> 9.61 us  [exchange(): lax.all_to_all(blocks, ('gx', 'gz'), 0, 0, axis_index_groups=groups, tile...]
    pallas_call x8 -> x6, Pallas kernels: 16.5 us -> 14.5 us  [call(): pl.pallas_call(kernel, grid_spec=grid_spec, out_shape=outs, compiler_para...]
    add x2 -> x0, local copies, waits for them, and re-layouts: 1.39 us -> none  [the longest x1 0.7 us: body(): jnp.asarray(alias_shift)]
  transfers between devices with their start and end apart: 9 -> 3, of which waited for: 7 -> 2; matrix products, arithmetic and copies ran while one was open for 2% -> 0% of each run, Pallas kernels for 5% -> 8%
where the time goes in v1:
time: 73.2 us; the launch traced here: 72.8 us
  starting transfers between devices  20.8 us (28%)
  blocking collectives  18.5 us (25%)
  Pallas kernels  14.5 us (20%)
  waiting for transfers between devices  9.74 us (13%)
  local copies, waits for them, and re-layouts  5.42 us (7%)
  other arithmetic  3.54 us (5%)
    all_to_all x1, blocking collectives, exchange(): lax.all_to_all(blocks, ('gx', 'gz'), 0, 0, axis_index_groups=groups, tile...  18.5 us
    pallas_call x6, Pallas kernels, call(): pl.pallas_call(kernel, grid_spec=grid_spec, out_shape=outs, compiler_para...  14.5 us
    all_to_all x1, starting transfers between devices, exchange(): lax.all_to_all(blocks, ('gx', 'gz'), 0, 0, axis_index_groups=groups, tile...  13.9 us
    all_to_all x1, waiting for transfers between devices, exchange(): lax.all_to_all(blocks, ('gx', 'gz'), 0, 0, axis_index_groups=groups, tile...  9.61 us
    unnamed x52, local copies, waits for them, and re-layouts  5.42 us
    ppermute x1, starting transfers between devices, body(): other = lax.ppermute(sent, 'gz', pair)  3.66 us
    ppermute x1, starting transfers between devices, body(): other = lax.ppermute(lower - sign * upper, 'gz', pair)  3.24 us
    sub x1, other arithmetic, body(): other = lax.ppermute(lower - sign * upper, 'gz', pair)  2.24 us
  transfers between devices with their start and end apart: 3, of which 2 were waited for; matrix products, arithmetic and copies ran while one was open for 0% of the time, Pallas kernels for 8%

profile of v1, /device:TPU:1, one launch (start us, length us, event | category | flops | bytes accessed | tf_op | source)
XLA Modules:
  0.0 72.8 jit_solution(7253833410983982595)
XLA Ops:
  0.0 2.2 %slice_subtract_fusion = (f32[8,32,512]{2,1,0:T(8,128)}, f32[8,32,512]{2,1,0:T(8,128)S(1)}) fusion(f32[8,32,1024]{2,1,0:T(8,128)} %param.22, f32[]{:T(128)S(6)} %select_n.4), kind=kLoop, calls=%fused_computation.3 | loop fusion | flops 393216 | bytes 2097156 | tf_op jit(solution)/shard_map/sub | solution.py:396
  2.2 3.2 %collective-permute-start = (f32[8,32,512]{2,1,0:T(8,128)}, f32[8,32,512]{2,1,0:T(8,128)S(1)}, u32[]{:S(2)}, u32[]{:S(2)}) collective-permute-start(f32[8,32,512]{2,1,0:T(8,128)} %get-tuple-element.23), channel_id=1, source_target_pairs={{0,1},{1,0},{2,3},{3,2},{4,5},{5,4},{6,7},{7,6},{8,9},{9,8},{10,11... | collective-permute-start | bytes 1572872 | tf_op jit(solution)/shard_map/ppermute | solution.py:396
  5.5 0.1 pad_add_fusion.place
  5.6 0.0 copy-done.15
  5.6 0.6 copy-done.21
  6.2 0.0 copy-done.18
  6.2 0.0 copy-done.20
  6.2 0.0 copy-done.24
  6.2 0.0 copy-start.3
  6.2 0.0 copy-start.10
  6.2 0.0 copy-start.19
  6.2 1.3 %shard_map.208.inverse = f32[16,32,512]{2,1,0:T(8,128)S(1)} custom-call(s32[4]{0:T(128)S(1)} %pad_add_fusion.place, f32[2,1,512]{2,1,0:T(1,128)S(1)} %copy-done.21, f32[32,512]{1,0:T(8,128)S(1)} %copy-done.15, f32[64]{0:T(128)S(1)} %copy-done.20, f32[64]{0:T(128)S(1)} %copy-done.18, f32[64]{0:T(128)S(1)} %copy-done.24), custom_call_target="tpu_custom_call" | custom-call | flops 10000000 | bytes 4000000 | tf_op jit(solution)/shard_map/pallas_call | solution.py:358
  7.5 0.0 collective-permute-done.other
  7.5 0.0 copy-done.4
  7.5 0.0 copy-done.2
  7.5 0.0 copy-done.3
  7.5 0.0 copy-done.10
  7.6 0.0 copy-done.19
  7.6 0.0 copy-start.5
  7.6 1.2 %copy-done.5 = bf16[2,512,512]{2,1,0:T(8,128)(2,1)S(1)} copy-done((bf16[2,512,512]{2,1,0:T(8,128)(2,1)S(1)}, bf16[2,512,512]{2,1,0:T(8,128)(2,1)}, u32[]{:S(2)}) %copy-start.5) | copy-done | bytes 1048600
  8.8 3.3 %shard_map.209 = (f32[16,32,512]{2,1,0:T(8,128)S(1)}, f32[512,128]{1,0:T(8,128)S(1)}) custom-call(s32[4]{0:T(128)S(1)} %pad_add_fusion.place, f32[8,32,512]{2,1,0:T(8,128)S(1)} %get-tuple-element.24.own, f32[8,32,512]{2,1,0:T(8,128)S(1)} %collective-permute-done.other, bf16[2,512,512]{2,1,0:T(8,128)(2,1)S(1)} %copy-done.5, ...), custom_call_target="tpu_custom_call" | custom-call | flops 10000000 | bytes 4000000 | tf_op jit(solution)/shard_map/pallas_call | solution.py:358
  12.1 0.0 copy-start.6
  12.1 1.0 %copy-done.6 = f32[16,32,512]{2,1,0:T(8,128)} copy-done((f32[16,32,512]{2,1,0:T(8,128)}, f32[16,32,512]{2,1,0:T(8,128)S(1)}, u32[]{:S(2)}) %copy-start.6) | copy-done | bytes 1048600
  13.1 0.7 copy-done.11
  13.8 0.0 copy-start.25
  13.8 13.9 %all-to-all-start = ((f32[128,4,128]{2,1,0:T(4,128)}), f32[128,4,128]{2,1,0:T(4,128)S(1)}, u32[]{:S(2)}, u32[]{:S(2)}) async-start(f32[128,4,128]{2,1,0:T(4,128)} %bitcast.11), calls=%async_computation | async-start | bytes 524288 | tf_op jit(solution)/shard_map/all_to_all | solution.py:390
  27.7 0.0 copy-done.12
  27.7 0.0 copy-done.14
  27.7 0.0 copy-done.22
  27.7 0.0 copy-done.23
  27.8 0.0 copy-done.25
  27.8 0.0 copy-start.16
  27.8 0.0 copy-start.17
  27.8 2.9 %shard_map.210 = (f32[64,32,128]{2,1,0:T(8,128)S(1)}, bf16[512,512]{1,0:T(8,128)(2,1)S(1)}, bf16[512,512]{1,0:T(8,128)(2,1)S(1)}, f32[4,8,128]{2,1,0:T(8,128)S(1)}) custom-call(s32[4]{0:T(128)S(1)} %pad_add_fusion.place, f32[1024]{0:T(1024)S(1)} %copy-done.23, f32[8,128]{1,0:T(8,128)S(1)} %copy-done.22, f32[1,128]{1,0:T(1,128)S(1)} %copy-done.25, ...), custom_call_target="tpu_custom_call" | custom-call | flops 10000000 | bytes 4000000 | tf_op jit(solution)/shard_map/pallas_call | solution.py:358
  30.7 0.8 %copy-done.8 = bf16[512,512]{1,0:T(8,128)(2,1)} copy-done((bf16[512,512]{1,0:T(8,128)(2,1)}, bf16[512,512]{1,0:T(8,128)(2,1)S(1)}, u32[]{:S(2)}) %copy-start.8) | copy-done | bytes 524312
  31.5 9.6 %all-to-all-done = f32[128,4,128]{2,1,0:T(4,128)S(1)} async-done(((f32[128,4,128]{2,1,0:T(4,128)}), f32[128,4,128]{2,1,0:T(4,128)S(1)}, u32[]{:S(2)}, u32[]{:S(2)}) %all-to-all-start) | async-done | bytes 262176 | tf_op jit(solution)/shard_map/all_to_all | solution.py:390
  41.1 1.0 %copy-done.9 = bf16[512,512]{1,0:T(8,128)(2,1)S(1)} copy-done((bf16[512,512]{1,0:T(8,128)(2,1)S(1)}, bf16[512,512]{1,0:T(8,128)(2,1)}, u32[]{:S(2)}) %copy-start.9) | copy-done | bytes 524312
  42.1 3.1 %shard_map.211 = f32[512,128]{1,0:T(8,128)S(1)} custom-call(s32[4]{0:T(128)S(1)} %pad_add_fusion.place, f32[512,128]{1,0:T(8,128)S(1)} %bitcast.8, bf16[512,512]{1,0:T(8,128)(2,1)S(1)} %get-tuple-element.15.response_high, bf16[512,512]{1,0:T(8,128)(2,1)S(1)} %copy-done.9, f32[4,8,128]{2,1,0:T(8,128)S(1)} %get-tuple-element.17.corners, ...), custom_call_target="tpu_custom_call" | custom-call | flops 10000000 | bytes 4000000 | tf_op jit(solution)/shard_map/pallas_call | solution.py:358
  45.3 0.0 copy-start.13
  45.3 18.5 %all_to_all.10 = f32[128,4,128]{2,1,0:T(4,128)S(1)} all-to-all(f32[128,4,128]{2,1,0:T(4,128)S(1)} %bitcast.10), channel_id=1, replica_groups={{0,2,4,6,8,10,12,14,16,18,20,22,24,26,28,30,32,34,36,38,40,42,44,46,48,..., dimensions={0} | all-to-all | bytes 524288 | tf_op jit(solution)/shard_map/all_to_all | solution.py:390
  63.8 0.0 copy-done
  63.8 0.0 copy-done.7
  63.8 2.6 %shard_map.212 = (f32[8,32,512]{2,1,0:T(8,128)S(1)}, f32[8,32,512]{2,1,0:T(8,128)S(1)}) custom-call(s32[4]{0:T(128)S(1)} %pad_add_fusion.place, f32[16,32,512]{2,1,0:T(8,128)S(1)} %copy-done.7, f32[512,128]{1,0:T(8,128)S(1)} %bitcast.9, f32[16,32,512]{2,1,0:T(8,128)S(1)} %shard_map.208.inverse, f32[32,512]{1,0:T(8,128)S(1)} %copy-done.10, ...), custom_call_target="tpu_custom_call" | custom-call | flops 10000000 | bytes 4000000 | tf_op jit(solution)/shard_map/pallas_call | solution.py:358
  66.4 3.7 %collective-permute-start.1 = (f32[8,32,512]{2,1,0:T(8,128)S(1)}, f32[8,32,512]{2,1,0:T(8,128)S(1)}, u32[]{:S(2)}, u32[]{:S(2)}) collective-permute-start(f32[8,32,512]{2,1,0:T(8,128)S(1)} %get-tuple-element.20), channel_id=1, source_target_pairs={{0,1},{1,0},{2,3},{3,2},{4,5},{5,4},{6,7},{7,6},{8,9},{9,8},{10,11... | collective-permute-start | bytes 1572872 | tf_op jit(solution)/shard_map/ppermute | solution.py:445
  70.1 1.4 %shard_map.213 = f32[8,32,512]{2,1,0:T(8,128)S(1)} custom-call(s32[4]{0:T(128)S(1)} %pad_add_fusion.place, f32[8,32,512]{2,1,0:T(8,128)S(1)} %get-tuple-element.19.modes, bf16[2,512,512]{2,1,0:T(8,128)(2,1)S(1)} %copy-done.1, bf16[2,512,512]{2,1,0:T(8,128)(2,1)S(1)} %copy-done, bf16[256,256]{1,0:T(8,128)(2,1)S(1)} %copy-done.3, bf16[256,256]{1,0:T(8,128)(2,1)S(1)} %copy-done.2), custom_call_target="tpu_custom_call" | custom-call | flops 10000000 | bytes 4000000 | tf_op jit(solution)/shard_map/pallas_call | solution.py:358
  71.5 0.1 collective-permute-done.1
  71.6 0.2 fusion
  71.8 1.1 %pad_maximum_fusion = f32[8,32,1024]{2,1,0:T(8,128)} fusion(f32[8,32,512]{2,1,0:T(8,128)S(1)} %get-tuple-element.22, f32[8,32,512]{2,1,0:T(8,128)S(1)} %get-tuple-element.21), kind=kLoop, calls=%fused_computation | loop fusion | flops 262144 | bytes 2097152 | tf_op jit(solution)/shard_map/concatenate | solution.py:454
  (21 shorter events, 0.0 us)
Async XLA Ops:
  0.0 5.6 %copy-start.15 = (f32[32,512]{1,0:T(8,128)S(1)}, f32[32,512]{1,0:T(8,128)}, u32[]{:S(2)}) copy-start(f32[32,512]{1,0:T(8,128)} %constant.61.clone.shift_col) | copy-start | bytes 196612
  0.0 7.5 %copy-start.4 = (bf16[2,512,512]{2,1,0:T(8,128)(2,1)S(1)}, bf16[2,512,512]{2,1,0:T(8,128)(2,1)}, u32[]{:S(2)}) copy-start(bf16[2,512,512]{2,1,0:T(8,128)(2,1)} %constant.63.clone.table_low) | copy-start | bytes 3145732
  2.2 5.3 %collective-permute-start = (f32[8,32,512]{2,1,0:T(8,128)}, f32[8,32,512]{2,1,0:T(8,128)S(1)}, u32[]{:S(2)}, u32[]{:S(2)}) collective-permute-start(f32[8,32,512]{2,1,0:T(8,128)} %get-tuple-element.23), channel_id=1, source_target_pairs={{0,1},{1,0},{2,3},{3,2},{4,5},{5,4},{6,7},{7,6},{8,9},{9,8},{10,11... | collective-permute-start | bytes 1572872 | tf_op jit(solution)/shard_map/ppermute | solution.py:396
  5.5 0.7 copy-start.21
  5.5 0.7 copy-start.18
  5.5 0.7 copy-start.20
  5.5 0.7 copy-start.24
  6.2 1.3 %copy-start.2 = (bf16[256,256]{1,0:T(8,128)(2,1)S(1)}, bf16[256,256]{1,0:T(8,128)(2,1)}, u32[]{:S(2)}) copy-start(bf16[256,256]{1,0:T(8,128)(2,1)} %constant.65.clone.slab_low) | copy-start | bytes 393220
  6.2 1.3 %copy-start.3 = (bf16[256,256]{1,0:T(8,128)(2,1)S(1)}, bf16[256,256]{1,0:T(8,128)(2,1)}, u32[]{:S(2)}) copy-start(bf16[256,256]{1,0:T(8,128)(2,1)} %constant.64.clone.slab_high) | copy-start | bytes 393220
  6.2 1.3 %copy-start.10 = (f32[32,512]{1,0:T(8,128)S(1)}, f32[32,512]{1,0:T(8,128)}, u32[]{:S(2)}) copy-start(f32[32,512]{1,0:T(8,128)} %constant.66.clone.weights) | copy-start | bytes 196612
  6.2 1.3 %copy-start.19 = (bf16[32,128]{1,0:T(8,128)(2,1)S(1)}, bf16[32,128]{1,0:T(8,128)(2,1)}, u32[]{:S(2)}) copy-start(bf16[32,128]{1,0:T(8,128)(2,1)} %constant.67.clone.fold) | copy-start | bytes 24580
  7.6 1.2 %copy-start.5 = (bf16[2,512,512]{2,1,0:T(8,128)(2,1)S(1)}, bf16[2,512,512]{2,1,0:T(8,128)(2,1)}, u32[]{:S(2)}) copy-start(bf16[2,512,512]{2,1,0:T(8,128)(2,1)} %constant.62.clone.table_high) | copy-start | bytes 3145732
  12.1 1.0 %copy-start.6 = (f32[16,32,512]{2,1,0:T(8,128)}, f32[16,32,512]{2,1,0:T(8,128)S(1)}, u32[]{:S(2)}) copy-start(f32[16,32,512]{2,1,0:T(8,128)S(1)} %get-tuple-element.13.modes) | copy-start | bytes 3145732
  13.1 0.7 copy-start.11
  13.8 14.0 %copy-start.12 = (f32[64,512]{1,0:T(8,128)S(1)}, f32[64,512]{1,0:T(8,128)}, u32[]{:S(2)}) copy-start(f32[64,512]{1,0:T(8,128)} %constant.71.clone.spread) | copy-start | bytes 393220
  13.8 14.0 %copy-start.14 = (f32[128,128]{1,0:T(8,128)S(1)}, f32[128,128]{1,0:T(8,128)}, u32[]{:S(2)}) copy-start(f32[128,128]{1,0:T(8,128)} %constant.72.clone.mask) | copy-start | bytes 196612
  13.8 14.0 %copy-start.22 = (f32[8,128]{1,0:T(8,128)S(1)}, f32[8,128]{1,0:T(8,128)}, u32[]{:S(2)}) copy-start(f32[8,128]{1,0:T(8,128)} %constant.69.clone.alias_shift) | copy-start | bytes 12292
  13.8 14.0 %copy-start.23 = (f32[1024]{0:T(1024)S(1)}, f32[1024]{0:T(1024)}, u32[]{:S(2)}) copy-start(f32[1024]{0:T(1024)} %constant.68.clone.shift_y) | copy-start | bytes 12292
  13.8 14.0 %copy-start.25 = (f32[1,128]{1,0:T(1,128)S(1)}, f32[1,128]{1,0:T(1,128)}, u32[]{:S(2)}) copy-start(f32[1,128]{1,0:T(1,128)} %constant.70.clone.mode_shift) | copy-start | bytes 1540
  13.8 27.3 %all-to-all-start = ((f32[128,4,128]{2,1,0:T(4,128)}), f32[128,4,128]{2,1,0:T(4,128)S(1)}, u32[]{:S(2)}, u32[]{:S(2)}) async-start(f32[128,4,128]{2,1,0:T(4,128)} %bitcast.11), calls=%async_computation | async-start | bytes 524288 | tf_op jit(solution)/shard_map/all_to_all | solution.py:390
  27.8 13.3 %copy-start.16 = (bf16[96,256]{1,0:T(8,128)(2,1)S(1)}, bf16[96,256]{1,0:T(8,128)(2,1)}, u32[]{:S(2)}) copy-start(bf16[96,256]{1,0:T(8,128)(2,1)} %constant.73.clone.forward) | copy-start | bytes 147460
  27.8 13.3 %copy-start.17 = (f32[64,128]{1,0:T(8,128)S(1)}, f32[64,128]{1,0:T(8,128)}, u32[]{:S(2)}) copy-start(f32[64,128]{1,0:T(8,128)} %constant.74.clone.backward) | copy-start | bytes 98308
  30.7 0.8 %copy-start.8 = (bf16[512,512]{1,0:T(8,128)(2,1)}, bf16[512,512]{1,0:T(8,128)(2,1)S(1)}, u32[]{:S(2)}) copy-start(bf16[512,512]{1,0:T(8,128)(2,1)S(1)} %get-tuple-element.16.response_low) | copy-start | bytes 1572868
  41.1 1.0 %copy-start.9 = (bf16[512,512]{1,0:T(8,128)(2,1)S(1)}, bf16[512,512]{1,0:T(8,128)(2,1)}, u32[]{:S(2)}) copy-start(bf16[512,512]{1,0:T(8,128)(2,1)} %copy-done.8) | copy-start | bytes 1572868
  42.1 21.7 %copy-start = (bf16[2,512,512]{2,1,0:T(8,128)(2,1)S(1)}, bf16[2,512,512]{2,1,0:T(8,128)(2,1)}, u32[]{:S(2)}) copy-start(bf16[2,512,512]{2,1,0:T(8,128)(2,1)} %constant.77.clone.table_low) | copy-start | bytes 3145732
  42.1 21.7 %copy-start.1 = (bf16[2,512,512]{2,1,0:T(8,128)(2,1)S(1)}, bf16[2,512,512]{2,1,0:T(8,128)(2,1)}, u32[]{:S(2)}) copy-start(bf16[2,512,512]{2,1,0:T(8,128)(2,1)} %constant.76.clone.table_high) | copy-start | bytes 3145732
  42.1 21.7 %copy-start.7 = (f32[16,32,512]{2,1,0:T(8,128)S(1)}, f32[16,32,512]{2,1,0:T(8,128)}, u32[]{:S(2)}) copy-start(f32[16,32,512]{2,1,0:T(8,128)} %copy-done.6) | copy-start | bytes 3145732
  45.3 18.6 %copy-start.13 = (f32[32,512]{1,0:T(8,128)S(1)}, f32[32,512]{1,0:T(8,128)}, u32[]{:S(2)}) copy-start(f32[32,512]{1,0:T(8,128)} %constant.75.clone.signs) | copy-start | bytes 196612
  66.4 5.2 %collective-permute-start.1 = (f32[8,32,512]{2,1,0:T(8,128)S(1)}, f32[8,32,512]{2,1,0:T(8,128)S(1)}, u32[]{:S(2)}, u32[]{:S(2)}) collective-permute-start(f32[8,32,512]{2,1,0:T(8,128)S(1)} %get-tuple-element.20), channel_id=1, source_target_pairs={{0,1},{1,0},{2,3},{3,2},{4,5},{5,4},{6,7},{7,6},{8,9},{9,8},{10,11... | collective-permute-start | bytes 1572872 | tf_op jit(solution)/shard_map/ppermute | solution.py:445

commit v2 on v1

--- a/solution.py
+++ b/solution.py
@@ -17,6 +17,7 @@
 LAYERS = NZ // CHIPS
 PEERS = SLABS * CHIPS
 PARTS = 4
+ROWS = 4
 LANES = 128
 highest = lax.Precision.HIGHEST
 VMEM_LIMIT = 48 * 1024 * 1024
@@ -89,11 +90,12 @@
     high, low = split_pair(forward)
     backward = np.concatenate([np.tile(basis(0) * weight, (1, 4)), np.tile(basis(1) * weight, (1, 4))], axis=0)
     alias = freq[None, None, :] + SLABS * (np.arange(8)[:, None, None] + 8 * np.arange(4)[None, :, None])
+    alias = np.repeat(alias, PARTS, axis=0)
     alias_shift = 4.0 * np.sin(np.pi * alias / NX) ** 2
     return (
         np.concatenate([high, low, high], axis=0),
         backward.astype(np.float32),
-        alias_shift.reshape(8, LANES).astype(np.float32),
+        alias_shift.reshape(8 * PARTS, LANES).astype(np.float32),
     )
 
 
@@ -139,9 +141,27 @@
     )
 
 
-def pivot_kernel(place, shift_row, shift_col, cell, face, screening, out):
-    base = place[1] * LAYERS
-    shifts = shift_col[...] + shift_row[0]
+def split_kernel(place, charge, own, sent, held_charge, sems):
+    copies = [pltpu.make_async_copy(charge.at[step], held_charge.at[step], sems.at[step]) for step in range(8)]
+    for copy in copies:
+        copy.start()
+    sign = jnp.where(place[0] == 0, 1.0, -1.0)
+    for step, copy in enumerate(copies):
+        copy.wait()
+        lower, upper = held_charge[step, :, :HALF], sign * held_charge[step, :, HALF:]
+        own[step] = lower + upper
+        sent[step] = lower - upper
+
+
+def early_kernel(place, own, tables_high, tables_low, slab_high, slab_low, shift_y, shift_col, cell, face, screening, inverse, table_high, table_low, modes, sems):
+    core, base = place[0], place[1] * LAYERS
+    copies = [
+        pltpu.make_async_copy(tables_high.at[core], table_high, sems.at[0]),
+        pltpu.make_async_copy(tables_low.at[core], table_low, sems.at[1]),
+    ]
+    for copy in copies:
+        copy.start()
+    shifts = shift_col[...] + shift_y[core]
     previous = None
     for layer in range(1, LAYERS):
         below, above = face[base + layer - 1], face[base + layer]
@@ -149,7 +169,21 @@
         if previous is not None:
             pivot = pivot - (below * below) * previous
         previous = 1.0 / pivot
-        out[layer] = previous
+        inverse[layer] = previous
+    for copy in copies:
+        copy.wait()
+    modes[...] = to_modes(own, table_high, table_low, slab_high, slab_low)
+
+
+def to_modes(planes, table_high, table_low, slab_high, slab_low):
+    values = planes[...].reshape(8 * PLANES, HALF)
+    spectrum = dot_split(split_values(values), (table_high[...], table_low[...]))
+    return dot_split((slab_high[...], slab_low[...]), split_values(spectrum)).reshape(8, PLANES, HALF)
+
+
+def to_planes(modes, table_high, table_low, slab_high, slab_low):
+    values = dot_split((slab_high[...], slab_low[...]), split_values(modes.reshape(8 * PLANES, HALF)))
+    return dot_split(split_values(values), (table_high[...], table_low[...])).reshape(8, PLANES, HALF)
 
 
 def stack_parts(values):
@@ -161,17 +195,14 @@
     return jnp.concatenate([turned[part * PLANES : (part + 1) * PLANES] for part in range(PARTS)], axis=1)
 
 
-def forward_kernel(place, own, other, table_high, table_low, slab_high, slab_low, inverse, weights, fold, cell, face, modes, out, part, folded):
+def forward_kernel(place, own_modes, other, table_high, table_low, slab_high, slab_low, inverse, weights, fold, cell, face, kept, kept_inverse, out, modes, part, folded, sems):
     core, base = place[0], place[1] * LAYERS
-    rows = 8 * PLANES
-    own_rows = own[...].reshape(rows, HALF)
-    other_rows = other[...].reshape(rows, HALF)
-    slab = (slab_high[...], slab_low[...])
-    table = (table_high[0], table_low[0])
-    for half in range(2):
-        values = jnp.where(core == half, own_rows, other_rows)
-        spectrum = dot_split(split_values(values), table)
-        modes[half * 8 : (half + 1) * 8] = dot_split(slab, split_values(spectrum)).reshape(8, PLANES, HALF)
+    copies = [pltpu.make_async_copy(inverse, kept_inverse, sems.at[0])]
+    copies[0].start()
+    modes[pl.ds(core * 8, 8)] = own_modes[...]
+    modes[pl.ds((1 - core) * 8, 8)] = to_modes(other, table_high, table_low, slab_high, slab_low)
+    copies.append(pltpu.make_async_copy(modes, kept, sems.at[1]))
+    copies[1].start()
     value = None
     for layer in range(1, LAYERS):
         inv = inverse[layer]
@@ -184,25 +215,30 @@
     for layer in reversed(range(1, LAYERS)):
         value = part[layer] if value is None else part[layer] + (face[base + layer] * inverse[layer]) * value
         if layer == LAYERS - 1:
-            out[pl.ds(1, PEERS, stride=4), :] = stack_parts(face[base + layer] * value)
+            out[pl.ds(1, PEERS, stride=ROWS), :] = stack_parts(face[base + layer] * value)
         weighted = weight * value
         total = (weighted[0:8] + weighted[8:16]) + (weighted[16:24] + weighted[24:32])
         folded[layer * 8 : (layer + 1) * 8] = total * cell[base + layer]
-    out[pl.ds(0, PEERS, stride=4), :] = stack_parts(modes[0] + face[base] * value)
+    out[pl.ds(0, PEERS, stride=ROWS), :] = stack_parts(modes[0] + face[base] * value)
     high, low = split_values(folded[...])
     sums = jnp.dot(fold[...], high, preferred_element_type=jnp.float32) + jnp.dot(fold[...], low, preferred_element_type=jnp.float32)
     planes = jnp.concatenate([modes[layer, 0:1] for layer in range(LAYERS)], axis=0)
     near = sums[:LAYERS] + planes
     far = sums[LAYERS:]
     blocks = [half[:, step * LANES : (step + 1) * LANES] for half in (near, far) for step in range(PARTS)]
-    out[pl.ds(2, PEERS, stride=4), :] = jnp.concatenate(blocks, axis=0).T
-    out[pl.ds(3, PEERS, stride=4), :] = jnp.zeros((PEERS, LANES), jnp.float32)
+    out[pl.ds(2, PEERS, stride=ROWS), :] = jnp.concatenate(blocks, axis=0).T
+    out[pl.ds(3, PEERS, stride=ROWS), :] = jnp.zeros((PEERS, LANES), jnp.float32)
+    for copy in copies:
+        copy.wait()
 
 
 def prepare_kernel(place, shift_y, alias_shift, mode_shift, spread, mask, cell, face, screening, alias_inverse, response_high, response_low, corners, inverses, columns, scaled):
     start = place[0] * HALF + place[3]
     values = [shift_y[start + part * PEERS] for part in range(PARTS)]
-    alias = jnp.concatenate([alias_shift[...] + value for value in values], axis=0)
+    sublane = lax.rem(lax.broadcasted_iota(jnp.int32, (8 * PARTS, LANES), 0), PARTS)
+    alias = alias_shift[...]
+    for part in range(PARTS):
+        alias = alias + jnp.where(sublane == part, values[part], 0.0)
     lane = lax.broadcasted_iota(jnp.int32, (8, LANES), 1)
     mode = jnp.broadcast_to(mode_shift[...], (8, LANES))
     for part in range(PARTS):
@@ -245,7 +281,7 @@
 
 def interface_kernel(place, arrived, response_high, response_low, corners, alias_inverse, forward, backward, face, out, source, part, solved):
     def rows(chip, slot):
-        return pl.ds(4 * chip + slot, SLABS, stride=4 * CHIPS)
+        return pl.ds(ROWS * chip + slot, SLABS, stride=ROWS * CHIPS)
 
     sides = []
     for chip in range(CHIPS):
@@ -265,9 +301,8 @@
     for layer in range(NZ):
         inv = alias_inverse[layer]
         first = (layer // LAYERS) * half + layer % LAYERS
-        row = jnp.concatenate(
-            [jnp.broadcast_to(source[first + step * LAYERS : first + step * LAYERS + 1, :], (8, LANES)) for step in range(PARTS)], axis=0
-        )
+        row = source[pl.ds(first, PARTS, stride=LAYERS), :]
+        row = jnp.concatenate([row] * 8, axis=0)
         scaled = row * inv
         value = scaled if value is None else scaled + (face[layer - 1] * inv) * value
         part[layer] = value
@@ -275,7 +310,8 @@
     for layer in reversed(range(NZ)):
         value = part[layer] if value is None else part[layer] + (face[layer] * alias_inverse[layer]) * value
         first = (layer // LAYERS) * half + layer % LAYERS
-        solved[pl.ds(first, PARTS, stride=LAYERS), :] = jnp.sum(value.reshape(PARTS, 8, LANES), axis=1)
+        total = (value[0:8] + value[8:16]) + (value[16:24] + value[24:32])
+        solved[pl.ds(first, PARTS, stride=LAYERS), :] = total[:PARTS] + total[PARTS:]
     planes = dot_full(backward[...], solved[...], ((1,), (1,)))
     own = []
     for chip in range(CHIPS):
@@ -297,11 +333,17 @@
         out[rows(chip, 3), :] = nothing
 
 
-def second_solve_kernel(place, modes, arrived, inverse, weights, signs, table_high, table_low, slab_high, slab_low, cell, face, kept, sent, part, near, edge):
+def second_solve_kernel(place, modes, arrived, inverse, weights, signs, tables_high, tables_low, slab_high, slab_low, cell, face, kept, sent, table_high, table_low, part, near, edge, sems):
     core, base = place[0], place[1] * LAYERS
-    below = unstack_parts(arrived[pl.ds(0, PEERS, stride=4), :])
-    above = unstack_parts(arrived[pl.ds(1, PEERS, stride=4), :])
-    turned = arrived[pl.ds(2, PEERS, stride=4), :].T
+    copies = [
+        pltpu.make_async_copy(tables_high.at[core], table_high, sems.at[0]),
+        pltpu.make_async_copy(tables_low.at[core], table_low, sems.at[1]),
+    ]
+    for copy in copies:
+        copy.start()
+    below = unstack_parts(arrived[pl.ds(0, PEERS, stride=ROWS), :])
+    above = unstack_parts(arrived[pl.ds(1, PEERS, stride=ROWS), :])
+    turned = arrived[pl.ds(2, PEERS, stride=ROWS), :].T
     for which, target in enumerate((near, edge)):
         for step in range(PARTS):
             at = (which * PARTS + step) * LAYERS
@@ -326,39 +368,43 @@
         value = part[layer] if value is None else part[layer] + (face[base + layer] * inverse[layer]) * value
         part[layer] = jnp.where(keep, near[layer : layer + 1, :], value)
     part[0] = jnp.where(keep, near[0:1, :], below)
-    rows = 8 * PLANES
     kept[...] = part[pl.ds(core * 8, 8)]
-    other = part[pl.ds((1 - core) * 8, 8)].reshape(rows, HALF)
-    planes = dot_split((slab_high[...], slab_low[...]), split_values(other))
-    sent[...] = dot_split(split_values(planes), (table_high[0], table_low[0])).reshape(8, PLANES, HALF)
+    for copy in copies:
+        copy.wait()
+    sent[...] = to_planes(part[pl.ds((1 - core) * 8, 8)], table_high, table_low, slab_high, slab_low)
 
 
 def backward_kernel(place, modes, table_high, table_low, slab_high, slab_low, out):
-    rows = 8 * PLANES
-    planes = dot_split((slab_high[...], slab_low[...]), split_values(modes[...].reshape(rows, HALF)))
-    out[...] = dot_split(split_values(planes), (table_high[0], table_low[0])).reshape(8, PLANES, HALF)
-
-
-def whole(*shape):
-    return pl.BlockSpec(shape, lambda step, place: (0,) * len(shape))
-
-
+    out[...] = to_planes(modes[...], table_high, table_low, slab_high, slab_low)
+
+
+def join_kernel(place, kept, other, out, joined, sems):
+    sign = jnp.where(place[0] == 0, 1.0, -1.0)
+    copies = []
+    for step in range(8):
+        one, two = kept[step], other[step]
+        joined[step, :, :HALF] = one + two
+        joined[step, :, HALF:] = sign * (one - two)
+        copies.append(pltpu.make_async_copy(joined.at[step], out.at[step], sems.at[step]))
+        copies[-1].start()
+    for copy in copies:
+        copy.wait()
+
+
+held = pl.BlockSpec(memory_space=pltpu.VMEM)
+far = pl.BlockSpec(memory_space=pl.ANY)
 scalars = pl.BlockSpec(memory_space=pltpu.SMEM)
-
-
-def call(kernel, place, inputs, in_specs, outs, scratch, cost=10_000_000):
-    outs = [out if isinstance(out, jax.ShapeDtypeStruct) else jax.ShapeDtypeStruct(out, jnp.float32) for out in outs]
-    grid_spec = pltpu.PrefetchScalarGridSpec(
-        num_scalar_prefetch=1,
-        grid=(1,),
-        in_specs=in_specs,
-        out_specs=[whole(*out.shape) for out in outs],
-        scratch_shapes=[pltpu.VMEM(shape, jnp.float32) for shape in scratch],
-    )
+in_hbm = functools.partial(pltpu.with_memory_space_constraint, memory_space=pltpu.HBM)
+
+
+def call(kernel, place, inputs, in_specs, outs, out_specs, scratch=(), grid=(), cost=10_000_000):
     return pl.pallas_call(
         kernel,
-        grid_spec=grid_spec,
+        grid=grid,
+        in_specs=[scalars, *in_specs],
+        out_specs=out_specs,
         out_shape=outs,
+        scratch_shapes=scratch,
         compiler_params=pltpu.CompilerParams(vmem_limit_bytes=VMEM_LIMIT),
         cost_estimate=pl.CostEstimate(flops=cost, bytes_accessed=4_000_000, transcendentals=0),
     )(place, *inputs)
@@ -381,77 +427,76 @@
 
     cube = (8, PLANES, HALF)
     field = (LAYERS, PLANES, HALF)
-    message = (4 * PEERS, LANES)
+    message = (ROWS * PEERS, LANES)
     square = (CHIPS * LANES, CHIPS * LANES)
+    table = pltpu.VMEM((HALF, HALF), jnp.bfloat16)
     groups = [[x * 2 * CHIPS + 2 * c + r for x in range(SLABS) for c in range(CHIPS)] for r in range(2)]
 
+    def vmem(*shape):
+        return pltpu.VMEM(shape, jnp.float32)
+
     def exchange(values):
-        blocks = values.reshape(PEERS, 4, LANES)
+        blocks = values.reshape(PEERS, ROWS, LANES)
         return lax.all_to_all(blocks, ("gx", "gz"), 0, 0, axis_index_groups=groups, tiled=True).reshape(message)
 
     pair = [(s, s ^ 1) for s in range(2 * CHIPS)]
-    sign = jnp.where(core == 0, 1.0, -1.0)
-    lower, upper = charge[:, :, :HALF], charge[:, :, HALF:]
-    own = lower + sign * upper
-    other = lax.ppermute(lower - sign * upper, "gz", pair)
-    row_spec = pl.BlockSpec((1, 1, HALF), lambda step, place: (place[0], 0, 0))
-    table_spec = pl.BlockSpec((1, HALF, HALF), lambda step, place: (place[0], 0, 0))
-    slab_spec = whole(8 * PLANES, 8 * PLANES)
-    inverse = call(
-        pivot_kernel,
+    lines = vmem(8, PLANES, NY)
+    own, sent = call(
+        split_kernel, place, (in_hbm(charge),), [far], [vmem(*cube), vmem(*cube)], [held] * 2, [lines, pltpu.SemaphoreType.DMA((8,))]
+    )
+    other = lax.ppermute(sent, "gz", pair)
+    inverse, table_high, table_low, own_modes = call(
+        early_kernel,
         place,
-        (shift_y[:, None, :], np.broadcast_to(slab_shifts()[:, None], (PLANES, HALF)).copy(), cell, face, screening),
-        [row_spec, whole(PLANES, HALF), scalars, scalars, scalars],
-        [field],
-        [],
-    )[0]
-    modes, ends = call(
+        (own, in_hbm(fy_high), in_hbm(fy_low), slab_high, slab_low, shift_y[:, None, :], np.broadcast_to(slab_shifts()[:, None], (PLANES, HALF)).copy(), cell, face, screening),
+        [held, far, far] + [held] * 4 + [scalars] * 3,
+        [vmem(*field), table, table, vmem(*cube)],
+        [held] * 4,
+        [pltpu.SemaphoreType.DMA((2,))],
+    )
+    modes, inverse, ends = call(
         forward_kernel,
         place,
-        (own, other, fy_high, fy_low, slab_high, slab_low, inverse, weights, fold_table(), cell, face),
-        [whole(*cube)] * 2 + [table_spec] * 2 + [slab_spec] * 2
-        + [whole(*field), whole(PLANES, HALF), whole(2 * LAYERS, 8 * LAYERS), scalars, scalars],
-        [field, message],
-        [field, (8 * LAYERS, HALF)],
+        (own_modes, other, table_high, table_low, slab_high, slab_low, inverse, weights, fold_table(), cell, face),
+        [held] * 9 + [scalars] * 2,
+        [pltpu.HBM(field, jnp.float32), pltpu.HBM(field, jnp.float32), pltpu.HBM(message, jnp.float32)],
+        [far, far, held],
+        [vmem(*field), vmem(*field), vmem(8 * LAYERS, HALF), pltpu.SemaphoreType.DMA((2,))],
     )
     alias_inverse, response_high, response_low, corners = call(
         prepare_kernel,
         place,
         (shift_y.reshape(-1), alias_shift, mode_shift, spread, mask, cell, face, screening),
-        [scalars, whole(8, LANES), whole(1, LANES), whole(*spread.shape), whole(*mask.shape), scalars, scalars, scalars],
-        [(NZ, 8 * PARTS, LANES), jax.ShapeDtypeStruct(square, jnp.bfloat16), jax.ShapeDtypeStruct(square, jnp.bfloat16), (CHIPS, 8, LANES)],
-        [(NZ, 8, LANES), (NZ, 8, LANES), (8 * NZ, LANES)],
+        [scalars] + [held] * 4 + [scalars] * 3,
+        [vmem(NZ, 8 * PARTS, LANES), pltpu.VMEM(square, jnp.bfloat16), pltpu.VMEM(square, jnp.bfloat16), vmem(CHIPS, 8, LANES)],
+        [held] * 4,
+        [vmem(NZ, 8, LANES), vmem(NZ, 8, LANES), vmem(8 * NZ, LANES)],
     )
     ends = exchange(ends)
     ends = call(
         interface_kernel,
         place,
         (ends, response_high, response_low, corners, alias_inverse, forward_slab, backward_slab, face),
-        [whole(*message), whole(*square), whole(*square), whole(CHIPS, 8, LANES), whole(NZ, 8 * PARTS, LANES)]
-        + [whole(*forward_slab.shape), whole(*backward_slab.shape), scalars],
-        [message],
-        [(CHIPS * PARTS * LAYERS, LANES), (NZ, 8 * PARTS, LANES), (CHIPS * PARTS * LAYERS, LANES)],
-    )[0]
+        [held] * 7 + [scalars],
+        vmem(*message),
+        held,
+        [vmem(CHIPS * PARTS * LAYERS, LANES), vmem(NZ, 8 * PARTS, LANES), vmem(CHIPS * PARTS * LAYERS, LANES)],
+    )
     ends = exchange(ends)
-    kept, sent = call(
+    kept, sent, table_high, table_low = call(
         second_solve_kernel,
         place,
-        (modes, ends, inverse, weights, signs, by_high, by_low, slab_high, slab_low, cell, face),
-        [whole(*field), whole(*message), whole(*field), whole(PLANES, HALF), whole(PLANES, HALF)]
-        + [table_spec] * 2 + [slab_spec] * 2 + [scalars] * 2,
-        [cube, cube],
-        [field, (LAYERS, HALF), (LAYERS, HALF)],
+        (modes, ends, inverse, weights, signs, in_hbm(by_high), in_hbm(by_low), slab_high, slab_low, cell, face),
+        [held] * 5 + [far] * 2 + [held] * 2 + [scalars] * 2,
+        [vmem(*cube), vmem(*cube), table, table],
+        [held] * 4,
+        [vmem(*field), vmem(LAYERS, HALF), vmem(LAYERS, HALF), pltpu.SemaphoreType.DMA((2,))],
     )
     other = lax.ppermute(sent, "gz", pair)
-    kept = call(
-        backward_kernel,
-        place,
-        (kept, by_high, by_low, slab_high, slab_low),
-        [whole(*cube)] + [table_spec] * 2 + [slab_spec] * 2,
-        [cube],
-        [],
-    )[0]
-    return jnp.concatenate([kept + other, sign * (kept - other)], axis=2)
+    kept = call(backward_kernel, place, (kept, table_high, table_low, slab_high, slab_low), [held] * 5, vmem(*cube), held)
+    return call(
+        join_kernel, place, (kept, other), [held] * 2, pltpu.HBM((8, PLANES, NY), jnp.float32), far, [lines, pltpu.SemaphoreType.DMA((8,))]
+    )
 
 
 def solution(mesh):

time: 73.2 us -> 70.7 us (0.966)
  local copies, waits for them, and re-layouts: 5.42 us -> 0.11 us
  Pallas kernels: 14.5 us -> 19.5 us
  other arithmetic: 3.54 us -> 0.08 us
  waiting for transfers between devices: 9.74 us -> 10.7 us
    unnamed x52 -> x38, local copies, waits for them, and re-layouts: 5.42 us -> 0.11 us
    pallas_call x6 -> x8, Pallas kernels: 14.5 us -> 19.5 us  [call(): pl.pallas_call(kernel, grid=grid, in_specs=[scalars, *in_specs], out_spec...]
    ppermute x1 -> x2, starting transfers between devices: 3.66 us -> 7.1 us  [body(): other = lax.ppermute(sent, 'gz', pair)]
    ppermute x1 -> x0, starting transfers between devices: 3.24 us -> none  [body(): other = lax.ppermute(lower - sign * upper, 'gz', pair)]
    sub x1 -> x0, other arithmetic: 2.24 us -> none  [body(): other = lax.ppermute(lower - sign * upper, 'gz', pair)]
    concatenate x1 -> x0, other arithmetic: 1.07 us -> none  [body(): return jnp.concatenate([kept + other, sign * (kept - other)], axis=2)]
    all_to_all x1, waiting for transfers between devices: 9.61 us -> 10.5 us  [exchange(): lax.all_to_all(blocks, ('gx', 'gz'), 0, 0, axis_index_groups=groups, tile...]
  transfers between devices with their start and end apart: 3 -> 3, of which waited for: 2 -> 2; matrix products, arithmetic and copies ran while one was open for 0% -> 0% of each run, Pallas kernels for 8% -> 9%
where the time goes in v2:
time: 70.7 us; the launch traced here: 70.4 us
  starting transfers between devices  21 us (30%)
  Pallas kernels  19.5 us (28%)
  blocking collectives  18.7 us (26%)
  waiting for transfers between devices  10.7 us (15%)
    pallas_call x8, Pallas kernels, call(): pl.pallas_call(kernel, grid=grid, in_specs=[scalars, *in_specs], out_spec...  19.5 us
    all_to_all x1, blocking collectives, exchange(): lax.all_to_all(blocks, ('gx', 'gz'), 0, 0, axis_index_groups=groups, tile...  18.7 us
    all_to_all x1, starting transfers between devices, exchange(): lax.all_to_all(blocks, ('gx', 'gz'), 0, 0, axis_index_groups=groups, tile...  13.9 us
    all_to_all x1, waiting for transfers between devices, exchange(): lax.all_to_all(blocks, ('gx', 'gz'), 0, 0, axis_index_groups=groups, tile...  10.5 us
    ppermute x2, starting transfers between devices, body(): other = lax.ppermute(sent, 'gz', pair)  7.1 us
  transfers between devices with their start and end apart: 3, of which 2 were waited for; matrix products, arithmetic and copies ran while one was open for 0% of the time, Pallas kernels for 9%

profile of v2, /device:TPU:1, one launch (start us, length us, event | category | flops | bytes accessed | tf_op | source)
XLA Modules:
  0.0 70.4 jit_solution(2745410454334413143)
XLA Ops:
  0.0 0.1 pad_add_fusion.place
  0.1 1.9 %shard_map.208 = (f32[8,32,512]{2,1,0:T(8,128)S(1)}, f32[8,32,512]{2,1,0:T(8,128)S(1)}) custom-call(s32[4]{0:T(128)S(1)} %pad_add_fusion.place, f32[8,32,1024]{2,1,0:T(8,128)} %charge.1), custom_call_target="tpu_custom_call" | custom-call | flops 10000000 | bytes 4000000 | tf_op jit(solution)/shard_map/pallas_call | solution.py:401
  2.0 0.0 copy-start.12
  2.0 0.0 copy-start.14
  2.0 0.0 copy-start.17
  2.0 3.3 %collective-permute-start = (f32[8,32,512]{2,1,0:T(8,128)S(1)}, f32[8,32,512]{2,1,0:T(8,128)S(1)}, u32[]{:S(2)}, u32[]{:S(2)}) collective-permute-start(f32[8,32,512]{2,1,0:T(8,128)S(1)} %get-tuple-element.24), channel_id=1, source_target_pairs={{0,1},{1,0},{2,3},{3,2},{4,5},{5,4},{6,7},{7,6},{8,9},{9,8},{10,11... | collective-permute-start | bytes 1572872 | tf_op jit(solution)/shard_map/ppermute | solution.py:447
  5.4 0.0 copy-done
  5.4 0.0 copy-done.1
  5.4 0.0 copy-done.7
  5.4 0.0 copy-done.15
  5.4 0.0 copy-done.12
  5.4 0.0 copy-done.14
  5.4 0.0 copy-done.17
  5.4 0.0 copy-start.4
  5.4 0.0 copy-start.13
  5.4 2.7 %shard_map.209 = (f32[16,32,512]{2,1,0:T(8,128)S(1)}, bf16[512,512]{1,0:T(8,128)(2,1)S(1)}, bf16[512,512]{1,0:T(8,128)(2,1)S(1)}, f32[8,32,512]{2,1,0:T(8,128)S(1)}) custom-call(s32[4]{0:T(128)S(1)} %pad_add_fusion.place, f32[8,32,512]{2,1,0:T(8,128)S(1)} %get-tuple-element.22.own, bf16[2,512,512]{2,1,0:T(8,128)(2,1)} %constant.55.clone.tables_high, ...), custom_call_target="tpu_custom_call" | custom-call | flops 10000000 | bytes 4000000 | tf_op jit(solution)/shard_map/pallas_call | solution.py:401
  8.2 0.0 collective-permute-done.other
  8.2 0.0 copy-done.4
  8.2 0.0 copy-done.13
  8.2 3.9 %shard_map.210 = (f32[16,32,512]{2,1,0:T(8,128)}, f32[16,32,512]{2,1,0:T(8,128)}, f32[512,128]{1,0:T(8,128)}) custom-call(s32[4]{0:T(128)S(1)} %pad_add_fusion.place, f32[8,32,512]{2,1,0:T(8,128)S(1)} %get-tuple-element.23.own_modes, f32[8,32,512]{2,1,0:T(8,128)S(1)} %collective-permute-done.other, bf16[512,512]{1,0:T(8,128)(2,1)S(1)} %get-tuple-element.25.table_high, ...), custom_call_target="tpu_custom_call" | custom-call | flops 10000000 | bytes 4000000 | tf_op jit(solution)/shard_map/pallas_call | solution.py:401
  12.1 0.0 copy-start.5
  12.2 0.0 copy-start.8
  12.2 0.0 copy-start.11
  12.2 0.0 copy-start.16
  12.2 0.0 copy-start.18
  12.2 13.9 %all-to-all-start = ((f32[128,4,128]{2,1,0:T(4,128)}), f32[128,4,128]{2,1,0:T(4,128)S(1)}, u32[]{:S(2)}, u32[]{:S(2)}) async-start(f32[128,4,128]{2,1,0:T(4,128)} %bitcast.11), calls=%async_computation | async-start | bytes 524288 | tf_op jit(solution)/shard_map/all_to_all | solution.py:440
  26.1 0.0 copy-done.5
  26.1 0.0 copy-done.8
  26.2 0.0 copy-done.11
  26.2 0.0 copy-done.16
  26.2 0.0 copy-done.18
  26.2 0.0 copy-start.9
  26.2 0.0 copy-start.10
  26.2 2.4 %shard_map.211 = (f32[64,32,128]{2,1,0:T(8,128)S(1)}, bf16[512,512]{1,0:T(8,128)(2,1)S(1)}, bf16[512,512]{1,0:T(8,128)(2,1)S(1)}, f32[4,8,128]{2,1,0:T(8,128)S(1)}) custom-call(s32[4]{0:T(128)S(1)} %pad_add_fusion.place, f32[1024]{0:T(1024)S(1)} %copy-done.16, f32[32,128]{1,0:T(8,128)S(1)} %copy-done.11, f32[1,128]{1,0:T(1,128)S(1)} %copy-done.18, ...), custom_call_target="tpu_custom_call" | custom-call | flops 10000000 | bytes 4000000 | tf_op jit(solution)/shard_map/pallas_call | solution.py:401
  28.6 10.5 %all-to-all-done = f32[128,4,128]{2,1,0:T(4,128)S(1)} async-done(((f32[128,4,128]{2,1,0:T(4,128)}), f32[128,4,128]{2,1,0:T(4,128)S(1)}, u32[]{:S(2)}, u32[]{:S(2)}) %all-to-all-start) | async-done | bytes 262176 | tf_op jit(solution)/shard_map/all_to_all | solution.py:440
  39.1 0.0 copy-done.9
  39.1 0.0 copy-done.10
  39.1 2.4 %shard_map.212 = f32[512,128]{1,0:T(8,128)S(1)} custom-call(s32[4]{0:T(128)S(1)} %pad_add_fusion.place, f32[512,128]{1,0:T(8,128)S(1)} %bitcast.8, bf16[512,512]{1,0:T(8,128)(2,1)S(1)} %get-tuple-element.30.response_high, bf16[512,512]{1,0:T(8,128)(2,1)S(1)} %get-tuple-element.31.response_low, f32[4,8,128]{2,1,0:T(8,128)S(1)} %get-tuple-element.32.corners, ...), custom_call_target="tpu_custom_call" | custom-call | flops 10000000 | bytes 4000000 | tf_op jit(solution)/shard_map/pallas_call | solution.py:401
  41.5 0.0 copy-start.6
  41.6 18.7 %all_to_all.10 = f32[128,4,128]{2,1,0:T(4,128)S(1)} all-to-all(f32[128,4,128]{2,1,0:T(4,128)S(1)} %bitcast.10), channel_id=1, replica_groups={{0,2,4,6,8,10,12,14,16,18,20,22,24,26,28,30,32,34,36,38,40,42,44,46,48,..., dimensions={0} | all-to-all | bytes 524288 | tf_op jit(solution)/shard_map/all_to_all | solution.py:440
  60.3 0.0 copy-done.2
  60.3 0.0 copy-done.3
  60.3 0.0 copy-done.6
  60.3 3.2 %shard_map.213 = (f32[8,32,512]{2,1,0:T(8,128)S(1)}, f32[8,32,512]{2,1,0:T(8,128)S(1)}, bf16[512,512]{1,0:T(8,128)(2,1)S(1)}, bf16[512,512]{1,0:T(8,128)(2,1)S(1)}) custom-call(s32[4]{0:T(128)S(1)} %pad_add_fusion.place, f32[16,32,512]{2,1,0:T(8,128)S(1)} %copy-done.2, f32[512,128]{1,0:T(8,128)S(1)} %bitcast.9, f32[16,32,512]{2,1,0:T(8,128)S(1)} %copy-done.3, ...), custom_call_target="tpu_custom_call" | custom-call | flops 10000000 | bytes 4000000 | tf_op jit(solution)/shard_map/pallas_call | solution.py:401
  63.5 3.8 %collective-permute-start.1 = (f32[8,32,512]{2,1,0:T(8,128)S(1)}, f32[8,32,512]{2,1,0:T(8,128)S(1)}, u32[]{:S(2)}, u32[]{:S(2)}) collective-permute-start(f32[8,32,512]{2,1,0:T(8,128)S(1)} %get-tuple-element.38), channel_id=1, source_target_pairs={{0,1},{1,0},{2,3},{3,2},{4,5},{5,4},{6,7},{7,6},{8,9},{9,8},{10,11... | collective-permute-start | bytes 1572872 | tf_op jit(solution)/shard_map/ppermute | solution.py:495
  67.3 1.4 %shard_map.214.kept = f32[8,32,512]{2,1,0:T(8,128)S(1)} custom-call(s32[4]{0:T(128)S(1)} %pad_add_fusion.place, f32[8,32,512]{2,1,0:T(8,128)S(1)} %get-tuple-element.35.modes, bf16[512,512]{1,0:T(8,128)(2,1)S(1)} %get-tuple-element.36.table_high, bf16[512,512]{1,0:T(8,128)(2,1)S(1)} %get-tuple-element.37.table_low, bf16[256,256]{1,0:T(8,128)(2,1)S(1)} %copy-done.1, ...), custom_call_target="tpu_custom_call" | custom-call | flops 10000000 | bytes 4000000 | tf_op jit(solution)/shard_map/pallas_call | solution.py:401
  68.7 0.1 collective-permute-done.1.other
  68.8 1.6 %shard_map.215 = f32[8,32,1024]{2,1,0:T(8,128)} custom-call(s32[4]{0:T(128)S(1)} %pad_add_fusion.place, f32[8,32,512]{2,1,0:T(8,128)S(1)} %shard_map.214.kept, f32[8,32,512]{2,1,0:T(8,128)S(1)} %collective-permute-done.1.other), custom_call_target="tpu_custom_call" | custom-call | flops 10000000 | bytes 4000000 | tf_op jit(solution)/shard_map/pallas_call | solution.py:401
  (6 shorter events, 0.0 us)
Async XLA Ops:
  0.1 5.3 %copy-start = (bf16[256,256]{1,0:T(8,128)(2,1)S(1)}, bf16[256,256]{1,0:T(8,128)(2,1)}, u32[]{:S(2)}) copy-start(bf16[256,256]{1,0:T(8,128)(2,1)} %constant.58.clone.slab_low) | copy-start | bytes 393220
  0.1 5.3 %copy-start.1 = (bf16[256,256]{1,0:T(8,128)(2,1)S(1)}, bf16[256,256]{1,0:T(8,128)(2,1)}, u32[]{:S(2)}) copy-start(bf16[256,256]{1,0:T(8,128)(2,1)} %constant.57.clone.slab_high) | copy-start | bytes 393220
  0.1 5.3 %copy-start.7 = (f32[32,512]{1,0:T(8,128)S(1)}, f32[32,512]{1,0:T(8,128)}, u32[]{:S(2)}) copy-start(f32[32,512]{1,0:T(8,128)} %constant.60.clone.shift_col) | copy-start | bytes 196612
  0.1 5.3 %copy-start.15 = (f32[2,1,512]{2,1,0:T(1,128)S(1)}, f32[2,1,512]{2,1,0:T(1,128)}, u32[]{:S(2)}) copy-start(f32[2,1,512]{2,1,0:T(1,128)} %constant.59.clone.shift_y) | copy-start | bytes 12292
  2.0 3.4 %copy-start.12 = (f32[64]{0:T(128)S(1)}, f32[64]{0:T(128)}, u32[]{:S(2)}) copy-start(f32[64]{0:T(128)} %face.9) | copy-start | bytes 772
  2.0 3.4 %copy-start.14 = (f32[64]{0:T(128)S(1)}, f32[64]{0:T(128)}, u32[]{:S(2)}) copy-start(f32[64]{0:T(128)} %cell.7) | copy-start | bytes 772
  2.0 3.4 %copy-start.17 = (f32[64]{0:T(128)S(1)}, f32[64]{0:T(128)}, u32[]{:S(2)}) copy-start(f32[64]{0:T(128)} %screening.3) | copy-start | bytes 772
  2.0 6.1 %collective-permute-start = (f32[8,32,512]{2,1,0:T(8,128)S(1)}, f32[8,32,512]{2,1,0:T(8,128)S(1)}, u32[]{:S(2)}, u32[]{:S(2)}) collective-permute-start(f32[8,32,512]{2,1,0:T(8,128)S(1)} %get-tuple-element.24), channel_id=1, source_target_pairs={{0,1},{1,0},{2,3},{3,2},{4,5},{5,4},{6,7},{7,6},{8,9},{9,8},{10,11... | collective-permute-start | bytes 1572872 | tf_op jit(solution)/shard_map/ppermute | solution.py:447
  5.4 2.8 %copy-start.4 = (f32[32,512]{1,0:T(8,128)S(1)}, f32[32,512]{1,0:T(8,128)}, u32[]{:S(2)}) copy-start(f32[32,512]{1,0:T(8,128)} %constant.61.clone.weights) | copy-start | bytes 196612
  5.4 2.8 %copy-start.13 = (bf16[32,128]{1,0:T(8,128)(2,1)S(1)}, bf16[32,128]{1,0:T(8,128)(2,1)}, u32[]{:S(2)}) copy-start(bf16[32,128]{1,0:T(8,128)(2,1)} %constant.62.clone.fold) | copy-start | bytes 24580
  12.1 14.0 %copy-start.5 = (f32[64,512]{1,0:T(8,128)S(1)}, f32[64,512]{1,0:T(8,128)}, u32[]{:S(2)}) copy-start(f32[64,512]{1,0:T(8,128)} %constant.66.clone.spread) | copy-start | bytes 393220
  12.2 14.0 %copy-start.8 = (f32[128,128]{1,0:T(8,128)S(1)}, f32[128,128]{1,0:T(8,128)}, u32[]{:S(2)}) copy-start(f32[128,128]{1,0:T(8,128)} %constant.67.clone.mask) | copy-start | bytes 196612
  12.2 14.0 %copy-start.11 = (f32[32,128]{1,0:T(8,128)S(1)}, f32[32,128]{1,0:T(8,128)}, u32[]{:S(2)}) copy-start(f32[32,128]{1,0:T(8,128)} %constant.64.clone.alias_shift) | copy-start | bytes 49156
  12.2 14.0 %copy-start.16 = (f32[1024]{0:T(1024)S(1)}, f32[1024]{0:T(1024)}, u32[]{:S(2)}) copy-start(f32[1024]{0:T(1024)} %constant.63.clone.shift_y) | copy-start | bytes 12292
  12.2 14.0 %copy-start.18 = (f32[1,128]{1,0:T(1,128)S(1)}, f32[1,128]{1,0:T(1,128)}, u32[]{:S(2)}) copy-start(f32[1,128]{1,0:T(1,128)} %constant.65.clone.mode_shift) | copy-start | bytes 1540
  12.2 26.9 %all-to-all-start = ((f32[128,4,128]{2,1,0:T(4,128)}), f32[128,4,128]{2,1,0:T(4,128)S(1)}, u32[]{:S(2)}, u32[]{:S(2)}) async-start(f32[128,4,128]{2,1,0:T(4,128)} %bitcast.11), calls=%async_computation | async-start | bytes 524288 | tf_op jit(solution)/shard_map/all_to_all | solution.py:440
  26.2 12.9 %copy-start.9 = (bf16[96,256]{1,0:T(8,128)(2,1)S(1)}, bf16[96,256]{1,0:T(8,128)(2,1)}, u32[]{:S(2)}) copy-start(bf16[96,256]{1,0:T(8,128)(2,1)} %constant.68.clone.forward) | copy-start | bytes 147460
  26.2 12.9 %copy-start.10 = (f32[64,128]{1,0:T(8,128)S(1)}, f32[64,128]{1,0:T(8,128)}, u32[]{:S(2)}) copy-start(f32[64,128]{1,0:T(8,128)} %constant.69.clone.backward) | copy-start | bytes 98308
  39.1 21.2 %copy-start.2 = (f32[16,32,512]{2,1,0:T(8,128)S(1)}, f32[16,32,512]{2,1,0:T(8,128)}, u32[]{:S(2)}) copy-start(f32[16,32,512]{2,1,0:T(8,128)} %get-tuple-element.28.modes) | copy-start | bytes 3145732
  39.1 21.2 %copy-start.3 = (f32[16,32,512]{2,1,0:T(8,128)S(1)}, f32[16,32,512]{2,1,0:T(8,128)}, u32[]{:S(2)}) copy-start(f32[16,32,512]{2,1,0:T(8,128)} %get-tuple-element.34.inverse) | copy-start | bytes 3145732
  41.5 18.7 %copy-start.6 = (f32[32,512]{1,0:T(8,128)S(1)}, f32[32,512]{1,0:T(8,128)}, u32[]{:S(2)}) copy-start(f32[32,512]{1,0:T(8,128)} %constant.72.clone.signs) | copy-start | bytes 196612
  63.5 5.3 %collective-permute-start.1 = (f32[8,32,512]{2,1,0:T(8,128)S(1)}, f32[8,32,512]{2,1,0:T(8,128)S(1)}, u32[]{:S(2)}, u32[]{:S(2)}) collective-permute-start(f32[8,32,512]{2,1,0:T(8,128)S(1)} %get-tuple-element.38), channel_id=1, source_target_pairs={{0,1},{1,0},{2,3},{3,2},{4,5},{5,4},{6,7},{7,6},{8,9},{9,8},{10,11... | collective-permute-start | bytes 1572872 | tf_op jit(solution)/shard_map/ppermute | solution.py:495

commit v3 on v2

--- a/solution.py
+++ b/solution.py
@@ -119,6 +119,18 @@
     return spread.reshape(NZ, CHIPS * LANES), mask.reshape(LANES, LANES)
 
 
+class Column:
+    def __init__(self, ref, which):
+        self.ref, self.start = ref, which * NZ
+
+    def __getitem__(self, layer):
+        return self.ref[self.start + layer]
+
+
+def columns_of(ref):
+    return [Column(ref, which) for which in range(3)]
+
+
 def split_values(values):
     high = values.astype(jnp.bfloat16)
     low = (values - high.astype(jnp.float32)).astype(jnp.bfloat16)
@@ -141,27 +153,26 @@
     )
 
 
-def split_kernel(place, charge, own, sent, held_charge, sems):
+def split_kernel(place, charge, tables_high, tables_low, own, sent, table_high, table_low, held_charge, sems):
     copies = [pltpu.make_async_copy(charge.at[step], held_charge.at[step], sems.at[step]) for step in range(8)]
+    copies.append(pltpu.make_async_copy(tables_high.at[place[0]], table_high, sems.at[8]))
+    copies.append(pltpu.make_async_copy(tables_low.at[place[0]], table_low, sems.at[9]))
     for copy in copies:
         copy.start()
     sign = jnp.where(place[0] == 0, 1.0, -1.0)
-    for step, copy in enumerate(copies):
+    for step, copy in enumerate(copies[:8]):
         copy.wait()
         lower, upper = held_charge[step, :, :HALF], sign * held_charge[step, :, HALF:]
         own[step] = lower + upper
         sent[step] = lower - upper
-
-
-def early_kernel(place, own, tables_high, tables_low, slab_high, slab_low, shift_y, shift_col, cell, face, screening, inverse, table_high, table_low, modes, sems):
-    core, base = place[0], place[1] * LAYERS
-    copies = [
-        pltpu.make_async_copy(tables_high.at[core], table_high, sems.at[0]),
-        pltpu.make_async_copy(tables_low.at[core], table_low, sems.at[1]),
-    ]
-    for copy in copies:
-        copy.start()
-    shifts = shift_col[...] + shift_y[core]
+    for copy in copies[8:]:
+        copy.wait()
+
+
+def chip_pivots(place, shift_y, shift_col, coefficients, inverse):
+    cell, face, screening = columns_of(coefficients)
+    base = place[1] * LAYERS
+    shifts = shift_col[...] + shift_y[place[0]]
     previous = None
     for layer in range(1, LAYERS):
         below, above = face[base + layer - 1], face[base + layer]
@@ -170,8 +181,10 @@
             pivot = pivot - (below * below) * previous
         previous = 1.0 / pivot
         inverse[layer] = previous
-    for copy in copies:
-        copy.wait()
+
+
+def early_kernel(place, own, table_high, table_low, slab_high, slab_low, shift_y, shift_col, coefficients, inverse, modes):
+    chip_pivots(place, shift_y, shift_col, coefficients, inverse)
     modes[...] = to_modes(own, table_high, table_low, slab_high, slab_low)
 
 
@@ -195,14 +208,13 @@
     return jnp.concatenate([turned[part * PLANES : (part + 1) * PLANES] for part in range(PARTS)], axis=1)
 
 
-def forward_kernel(place, own_modes, other, table_high, table_low, slab_high, slab_low, inverse, weights, fold, cell, face, kept, kept_inverse, out, modes, part, folded, sems):
+def forward_kernel(place, own_modes, other, table_high, table_low, slab_high, slab_low, inverse, weights, fold, coefficients, kept, out, modes, part, folded, sem):
     core, base = place[0], place[1] * LAYERS
-    copies = [pltpu.make_async_copy(inverse, kept_inverse, sems.at[0])]
-    copies[0].start()
+    cell, face, _ = columns_of(coefficients)
     modes[pl.ds(core * 8, 8)] = own_modes[...]
     modes[pl.ds((1 - core) * 8, 8)] = to_modes(other, table_high, table_low, slab_high, slab_low)
-    copies.append(pltpu.make_async_copy(modes, kept, sems.at[1]))
-    copies[1].start()
+    copy = pltpu.make_async_copy(modes, kept, sem)
+    copy.start()
     value = None
     for layer in range(1, LAYERS):
         inv = inverse[layer]
@@ -228,11 +240,17 @@
     blocks = [half[:, step * LANES : (step + 1) * LANES] for half in (near, far) for step in range(PARTS)]
     out[pl.ds(2, PEERS, stride=ROWS), :] = jnp.concatenate(blocks, axis=0).T
     out[pl.ds(3, PEERS, stride=ROWS), :] = jnp.zeros((PEERS, LANES), jnp.float32)
+    copy.wait()
+
+
+def prepare_kernel(place, shift_y, alias_shift, mode_shift, spread, mask, tables_high, tables_low, coefficients, alias_inverse, response_high, response_low, corners, table_high, table_low, inverses, columns, scaled, sems):
+    copies = [
+        pltpu.make_async_copy(tables_high.at[place[0]], table_high, sems.at[0]),
+        pltpu.make_async_copy(tables_low.at[place[0]], table_low, sems.at[1]),
+    ]
     for copy in copies:
-        copy.wait()
-
-
-def prepare_kernel(place, shift_y, alias_shift, mode_shift, spread, mask, cell, face, screening, alias_inverse, response_high, response_low, corners, inverses, columns, scaled):
+        copy.start()
+    cell, face, screening = columns_of(coefficients)
     start = place[0] * HALF + place[3]
     values = [shift_y[start + part * PEERS] for part in range(PARTS)]
     sublane = lax.rem(lax.broadcasted_iota(jnp.int32, (8 * PARTS, LANES), 0), PARTS)
@@ -277,9 +295,17 @@
         high, low = split_values(response)
         response_high[chip * LANES : (chip + 1) * LANES, :] = high
         response_low[chip * LANES : (chip + 1) * LANES, :] = low
-
-
-def interface_kernel(place, arrived, response_high, response_low, corners, alias_inverse, forward, backward, face, out, source, part, solved):
+    for copy in copies:
+        copy.wait()
+
+
+def interface_kernel(place, arrived, response_high, response_low, alias_inverse, forward_far, backward_far, corners_far, coefficients, out, source, part, solved, forward, backward, corners, sems):
+    pairs = ((forward_far, forward), (backward_far, backward), (corners_far, corners))
+    copies = [pltpu.make_async_copy(*pair, sems.at[step]) for step, pair in enumerate(pairs)]
+    for copy in copies:
+        copy.start()
+    face = columns_of(coefficients)[1]
+
     def rows(chip, slot):
         return pl.ds(ROWS * chip + slot, SLABS, stride=ROWS * CHIPS)
 
@@ -292,6 +318,8 @@
     sums = sums + jnp.concatenate([arrived[rows(chip, 2), :] for chip in range(CHIPS)], axis=1)
     high, low = split_values(sums)
     stacked = jnp.concatenate([high, high, low], axis=0)
+    for copy in copies:
+        copy.wait()
     turned = lax.dot_general(stacked, forward[...], (((0,), (0,)), ((), ())), preferred_element_type=jnp.float32)
     half = PARTS * LAYERS
     for chip in range(CHIPS):
@@ -333,14 +361,10 @@
         out[rows(chip, 3), :] = nothing
 
 
-def second_solve_kernel(place, modes, arrived, inverse, weights, signs, tables_high, tables_low, slab_high, slab_low, cell, face, kept, sent, table_high, table_low, part, near, edge, sems):
+def second_solve_kernel(place, modes, arrived, shift_y, shift_col, weights, signs, table_high, table_low, slab_high, slab_low, coefficients, kept, sent, part, near, edge, inverse):
     core, base = place[0], place[1] * LAYERS
-    copies = [
-        pltpu.make_async_copy(tables_high.at[core], table_high, sems.at[0]),
-        pltpu.make_async_copy(tables_low.at[core], table_low, sems.at[1]),
-    ]
-    for copy in copies:
-        copy.start()
+    cell, face, _ = columns_of(coefficients)
+    chip_pivots(place, shift_y, shift_col, coefficients, inverse)
     below = unstack_parts(arrived[pl.ds(0, PEERS, stride=ROWS), :])
     above = unstack_parts(arrived[pl.ds(1, PEERS, stride=ROWS), :])
     turned = arrived[pl.ds(2, PEERS, stride=ROWS), :].T
@@ -369,26 +393,11 @@
         part[layer] = jnp.where(keep, near[layer : layer + 1, :], value)
     part[0] = jnp.where(keep, near[0:1, :], below)
     kept[...] = part[pl.ds(core * 8, 8)]
-    for copy in copies:
-        copy.wait()
     sent[...] = to_planes(part[pl.ds((1 - core) * 8, 8)], table_high, table_low, slab_high, slab_low)
 
 
 def backward_kernel(place, modes, table_high, table_low, slab_high, slab_low, out):
     out[...] = to_planes(modes[...], table_high, table_low, slab_high, slab_low)
-
-
-def join_kernel(place, kept, other, out, joined, sems):
-    sign = jnp.where(place[0] == 0, 1.0, -1.0)
-    copies = []
-    for step in range(8):
-        one, two = kept[step], other[step]
-        joined[step, :, :HALF] = one + two
-        joined[step, :, HALF:] = sign * (one - two)
-        copies.append(pltpu.make_async_copy(joined.at[step], out.at[step], sems.at[step]))
-        copies[-1].start()
-    for copy in copies:
-        copy.wait()
 
 
 held = pl.BlockSpec(memory_space=pltpu.VMEM)
@@ -430,6 +439,7 @@
     message = (ROWS * PEERS, LANES)
     square = (CHIPS * LANES, CHIPS * LANES)
     table = pltpu.VMEM((HALF, HALF), jnp.bfloat16)
+    far_table = pltpu.HBM((HALF, HALF), jnp.bfloat16)
     groups = [[x * 2 * CHIPS + 2 * c + r for x in range(SLABS) for c in range(CHIPS)] for r in range(2)]
 
     def vmem(*shape):
@@ -441,62 +451,69 @@
 
     pair = [(s, s ^ 1) for s in range(2 * CHIPS)]
     lines = vmem(8, PLANES, NY)
-    own, sent = call(
-        split_kernel, place, (in_hbm(charge),), [far], [vmem(*cube), vmem(*cube)], [held] * 2, [lines, pltpu.SemaphoreType.DMA((8,))]
+    own, sent, table_high, table_low = call(
+        split_kernel,
+        place,
+        (in_hbm(charge), in_hbm(fy_high), in_hbm(fy_low)),
+        [far] * 3,
+        [vmem(*cube), vmem(*cube), table, table],
+        [held] * 4,
+        [lines, pltpu.SemaphoreType.DMA((10,))],
     )
     other = lax.ppermute(sent, "gz", pair)
-    inverse, table_high, table_low, own_modes = call(
+    shifts = (shift_y[:, None, :], np.broadcast_to(slab_shifts()[:, None], (PLANES, HALF)).copy())
+    coefficients = jnp.concatenate([cell, face, screening])
+    inverse, own_modes = call(
         early_kernel,
         place,
-        (own, in_hbm(fy_high), in_hbm(fy_low), slab_high, slab_low, shift_y[:, None, :], np.broadcast_to(slab_shifts()[:, None], (PLANES, HALF)).copy(), cell, face, screening),
-        [held, far, far] + [held] * 4 + [scalars] * 3,
-        [vmem(*field), table, table, vmem(*cube)],
-        [held] * 4,
-        [pltpu.SemaphoreType.DMA((2,))],
-    )
-    modes, inverse, ends = call(
+        (own, table_high, table_low, slab_high, slab_low, *shifts, coefficients),
+        [held] * 7 + [scalars],
+        [vmem(*field), vmem(*cube)],
+        [held] * 2,
+    )
+    modes, ends = call(
         forward_kernel,
         place,
-        (own_modes, other, table_high, table_low, slab_high, slab_low, inverse, weights, fold_table(), cell, face),
-        [held] * 9 + [scalars] * 2,
-        [pltpu.HBM(field, jnp.float32), pltpu.HBM(field, jnp.float32), pltpu.HBM(message, jnp.float32)],
-        [far, far, held],
-        [vmem(*field), vmem(*field), vmem(8 * LAYERS, HALF), pltpu.SemaphoreType.DMA((2,))],
-    )
-    alias_inverse, response_high, response_low, corners = call(
+        (own_modes, other, table_high, table_low, slab_high, slab_low, inverse, weights, fold_table(), coefficients),
+        [held] * 9 + [scalars],
+        [pltpu.HBM(field, jnp.float32), pltpu.HBM(message, jnp.float32)],
+        [far, held],
+        [vmem(*field), vmem(*field), vmem(8 * LAYERS, HALF), pltpu.SemaphoreType.DMA],
+    )
+    alias_inverse, response_high, response_low, corners, table_high, table_low = call(
         prepare_kernel,
         place,
-        (shift_y.reshape(-1), alias_shift, mode_shift, spread, mask, cell, face, screening),
-        [scalars] + [held] * 4 + [scalars] * 3,
-        [vmem(NZ, 8 * PARTS, LANES), pltpu.VMEM(square, jnp.bfloat16), pltpu.VMEM(square, jnp.bfloat16), vmem(CHIPS, 8, LANES)],
-        [held] * 4,
-        [vmem(NZ, 8, LANES), vmem(NZ, 8, LANES), vmem(8 * NZ, LANES)],
+        (shift_y.reshape(-1), alias_shift, mode_shift, spread, mask, in_hbm(by_high), in_hbm(by_low), coefficients),
+        [scalars] + [held] * 4 + [far] * 2 + [scalars],
+        [vmem(NZ, 8 * PARTS, LANES), pltpu.VMEM(square, jnp.bfloat16), pltpu.VMEM(square, jnp.bfloat16), pltpu.HBM((CHIPS, 8, LANES), jnp.float32), far_table, far_table],
+        [held] * 4 + [far] * 2,
+        [vmem(NZ, 8, LANES), vmem(NZ, 8, LANES), vmem(8 * NZ, LANES), pltpu.SemaphoreType.DMA((2,))],
     )
     ends = exchange(ends)
     ends = call(
         interface_kernel,
         place,
-        (ends, response_high, response_low, corners, alias_inverse, forward_slab, backward_slab, face),
-        [held] * 7 + [scalars],
+        (ends, response_high, response_low, alias_inverse, in_hbm(forward_slab), in_hbm(backward_slab), in_hbm(corners), coefficients),
+        [held] * 4 + [far] * 3 + [scalars],
         vmem(*message),
         held,
-        [vmem(CHIPS * PARTS * LAYERS, LANES), vmem(NZ, 8 * PARTS, LANES), vmem(CHIPS * PARTS * LAYERS, LANES)],
+        [vmem(CHIPS * PARTS * LAYERS, LANES), vmem(NZ, 8 * PARTS, LANES), vmem(CHIPS * PARTS * LAYERS, LANES)]
+        + [pltpu.VMEM(forward_slab.shape, jnp.bfloat16), vmem(*backward_slab.shape), vmem(CHIPS, 8, LANES), pltpu.SemaphoreType.DMA((3,))],
     )
     ends = exchange(ends)
-    kept, sent, table_high, table_low = call(
+    kept, sent = call(
         second_solve_kernel,
         place,
-        (modes, ends, inverse, weights, signs, in_hbm(by_high), in_hbm(by_low), slab_high, slab_low, cell, face),
-        [held] * 5 + [far] * 2 + [held] * 2 + [scalars] * 2,
-        [vmem(*cube), vmem(*cube), table, table],
-        [held] * 4,
-        [vmem(*field), vmem(LAYERS, HALF), vmem(LAYERS, HALF), pltpu.SemaphoreType.DMA((2,))],
+        (modes, ends, *shifts, weights, signs, table_high, table_low, slab_high, slab_low, coefficients),
+        [held] * 10 + [scalars],
+        [vmem(*cube), vmem(*cube)],
+        [held] * 2,
+        [vmem(*field), vmem(LAYERS, HALF), vmem(LAYERS, HALF), vmem(*field)],
     )
     other = lax.ppermute(sent, "gz", pair)
     kept = call(backward_kernel, place, (kept, table_high, table_low, slab_high, slab_low), [held] * 5, vmem(*cube), held)
-    return call(
-        join_kernel, place, (kept, other), [held] * 2, pltpu.HBM((8, PLANES, NY), jnp.float32), far, [lines, pltpu.SemaphoreType.DMA((8,))]
-    )
+    sign = jnp.where(core == 0, 1.0, -1.0)
+    return jnp.concatenate([kept + other, sign * (kept - other)], axis=2)
 
 
 def solution(mesh):

time: 70.7 us -> 96.3 us (1.36)
  Pallas kernels: 19.5 us -> 48.1 us
  waiting for transfers between devices: 10.7 us -> 0.14 us
  blocking collectives: 18.7 us -> 25 us
  other arithmetic: 0.08 us -> 1.36 us
    pallas_call x8 -> x7, Pallas kernels: 19.5 us -> 48.1 us  [call(): pl.pallas_call(kernel, grid=grid, in_specs=[scalars, *in_specs], out_spec...]
    all_to_all x1, waiting for transfers between devices: 10.5 us -> 0.01 us  [exchange(): lax.all_to_all(blocks, ('gx', 'gz'), 0, 0, axis_index_groups=groups, tile...]
    all_to_all x1, blocking collectives: 18.7 us -> 25 us  [exchange(): lax.all_to_all(blocks, ('gx', 'gz'), 0, 0, axis_index_groups=groups, tile...]
    concatenate x0 -> x2, other arithmetic: none -> 1.14 us  [the longest x1 1.06 us: body(): return jnp.concatenate([kept + other, sign * (kept - other)], axis=2)]
  transfers between devices with their start and end apart: 3 -> 3, of which waited for: 2 -> 1; matrix products, arithmetic and copies ran while one was open for 0% -> 0% of each run, Pallas kernels for 9% -> 39%
where the time goes in v3:
time: 96.3 us; the launch traced here: 96 us
  Pallas kernels  48.1 us (50%)
  blocking collectives  25 us (26%)
  starting transfers between devices  21 us (22%)
  other arithmetic  1.36 us (1%)
    pallas_call x7, Pallas kernels, call(): pl.pallas_call(kernel, grid=grid, in_specs=[scalars, *in_specs], out_spec...  48.1 us
    all_to_all x1, blocking collectives, exchange(): lax.all_to_all(blocks, ('gx', 'gz'), 0, 0, axis_index_groups=groups, tile...  25 us
    all_to_all x1, starting transfers between devices, exchange(): lax.all_to_all(blocks, ('gx', 'gz'), 0, 0, axis_index_groups=groups, tile...  13.9 us
    ppermute x2, starting transfers between devices, body(): other = lax.ppermute(sent, 'gz', pair)  7.11 us
  transfers between devices with their start and end apart: 3, of which 1 were waited for; matrix products, arithmetic and copies ran while one was open for 0% of the time, Pallas kernels for 39%

profile of v3, /device:TPU:1, one launch (start us, length us, event | category | flops | bytes accessed | tf_op | source)
XLA Modules:
  0.0 96.0 jit_solution(18378494456619162823)
XLA Ops:
  0.0 0.1 pad_add_fusion.place
  0.1 2.2 %shard_map.208 = (f32[8,32,512]{2,1,0:T(8,128)S(1)}, f32[8,32,512]{2,1,0:T(8,128)S(1)}, bf16[512,512]{1,0:T(8,128)(2,1)S(1)}, bf16[512,512]{1,0:T(8,128)(2,1)S(1)}) custom-call(s32[4]{0:T(128)S(1)} %pad_add_fusion.place, f32[8,32,1024]{2,1,0:T(8,128)} %charge.1, bf16[2,512,512]{2,1,0:T(8,128)(2,1)} %constant.60.clone.tables_high, ...), custom_call_target="tpu_custom_call" | custom-call | flops 10000000 | bytes 4000000 | tf_op jit(solution)/shard_map/pallas_call | solution.py:410
  2.3 0.0 copy-start.15
  2.4 0.0 copy-start.16
  2.4 0.0 copy-start.17
  2.4 0.0 copy-start.11
  2.4 3.3 %collective-permute-start = (f32[8,32,512]{2,1,0:T(8,128)S(1)}, f32[8,32,512]{2,1,0:T(8,128)S(1)}, u32[]{:S(2)}, u32[]{:S(2)}) collective-permute-start(f32[8,32,512]{2,1,0:T(8,128)S(1)} %get-tuple-element.25), channel_id=1, source_target_pairs={{0,1},{1,0},{2,3},{3,2},{4,5},{5,4},{6,7},{7,6},{8,9},{9,8},{10,11... | collective-permute-start | bytes 1572872 | tf_op jit(solution)/shard_map/ppermute | solution.py:463
  5.7 0.0 copy-done.15
  5.7 0.0 copy-done.16
  5.7 0.0 copy-done.17
  5.7 0.1 pad_maximum_fusion.1.coefficients
  5.8 0.0 copy-done.2
  5.8 0.0 copy-done.3
  5.8 0.0 copy-done.5
  5.8 0.0 copy-done.11
  5.8 0.0 copy-start.6
  5.8 0.0 copy-start.12
  5.8 1.6 %shard_map.209 = (f32[16,32,512]{2,1,0:T(8,128)S(1)}, f32[8,32,512]{2,1,0:T(8,128)S(1)}) custom-call(s32[4]{0:T(128)S(1)} %pad_add_fusion.place, f32[8,32,512]{2,1,0:T(8,128)S(1)} %get-tuple-element.21.own, bf16[512,512]{1,0:T(8,128)(2,1)S(1)} %get-tuple-element.22.table_high, bf16[512,512]{1,0:T(8,128)(2,1)S(1)} %get-tuple-element.23.table_low, ...), custom_call_target="tpu_custom_call" | custom-call | flops 10000000 | bytes 4000000 | tf_op jit(solution)/shard_map/pallas_call | solution.py:410
  7.5 0.0 collective-permute-done.other
  7.5 0.0 copy-done.6
  7.5 0.0 copy-done.12
  7.5 3.6 %shard_map.210 = (f32[16,32,512]{2,1,0:T(8,128)}, f32[512,128]{1,0:T(8,128)}) custom-call(s32[4]{0:T(128)S(1)} %pad_add_fusion.place, f32[8,32,512]{2,1,0:T(8,128)S(1)} %get-tuple-element.24.own_modes, f32[8,32,512]{2,1,0:T(8,128)S(1)} %collective-permute-done.other, bf16[512,512]{1,0:T(8,128)(2,1)S(1)} %get-tuple-element.22.table_high, ...), custom_call_target="tpu_custom_call" | custom-call | flops 10000000 | bytes 4000000 | tf_op jit(solution)/shard_map/pallas_call | solution.py:410
  11.1 0.0 copy-start.7
  11.2 0.0 copy-start.9
  11.2 0.0 copy-start.10
  11.2 0.0 copy-start.13
  11.2 0.0 copy-start.14
  11.2 13.9 %all-to-all-start = ((f32[128,4,128]{2,1,0:T(4,128)}), f32[128,4,128]{2,1,0:T(4,128)S(1)}, u32[]{:S(2)}, u32[]{:S(2)}) async-start(f32[128,4,128]{2,1,0:T(4,128)} %bitcast.11), calls=%async_computation | async-start | bytes 524288 | tf_op jit(solution)/shard_map/all_to_all | solution.py:450
  25.1 0.0 copy-done.7
  25.1 0.0 copy-done.9
  25.2 0.0 copy-done.10
  25.2 0.0 copy-done.13
  25.2 0.0 copy-done.14
  25.2 34.1 %shard_map.211 = (f32[64,32,128]{2,1,0:T(8,128)S(1)}, bf16[512,512]{1,0:T(8,128)(2,1)S(1)}, bf16[512,512]{1,0:T(8,128)(2,1)S(1)}, f32[4,8,128]{2,1,0:T(8,128)}, ...) custom-call(s32[4]{0:T(128)S(1)} %pad_add_fusion.place, f32[1024]{0:T(1024)S(1)} %copy-done.13, ...), custom_call_target="tpu_custom_call" | custom-call | flops 10000000 | bytes 4000000 | tf_op jit(solution)/shard_map/pallas_call | solution.py:410
  59.3 0.0 all-to-all-done
  59.3 0.0 copy-start.1
  59.3 0.0 copy-start.4
  59.3 0.0 copy-start.8
  59.3 3.0 %shard_map.212 = f32[512,128]{1,0:T(8,128)S(1)} custom-call(s32[4]{0:T(128)S(1)} %pad_add_fusion.place, f32[512,128]{1,0:T(8,128)S(1)} %bitcast.9, bf16[512,512]{1,0:T(8,128)(2,1)S(1)} %get-tuple-element.29.response_high, bf16[512,512]{1,0:T(8,128)(2,1)S(1)} %get-tuple-element.30.response_low, f32[64,32,128]{2,1,0:T(8,128)S(1)} %get-tuple-element.31.alias_inverse, ...), custom_call_target="tpu_custom_call" | custom-call | flops 10000000 | bytes 4000000 | tf_op jit(solution)/shard_map/pallas_call | solution.py:410
  62.3 0.0 copy-start
  62.4 25.0 %all_to_all.10 = f32[128,4,128]{2,1,0:T(4,128)S(1)} all-to-all(f32[128,4,128]{2,1,0:T(4,128)S(1)} %bitcast.10), channel_id=1, replica_groups={{0,2,4,6,8,10,12,14,16,18,20,22,24,26,28,30,32,34,36,38,40,42,44,46,48,..., dimensions={0} | all-to-all | bytes 524288 | tf_op jit(solution)/shard_map/all_to_all | solution.py:450
  87.3 0.0 copy-done.1
  87.3 2.1 %shard_map.213 = (f32[8,32,512]{2,1,0:T(8,128)S(1)}, f32[8,32,512]{2,1,0:T(8,128)S(1)}) custom-call(s32[4]{0:T(128)S(1)} %pad_add_fusion.place, f32[16,32,512]{2,1,0:T(8,128)S(1)} %copy-done.4, f32[512,128]{1,0:T(8,128)S(1)} %bitcast.8, f32[2,1,512]{2,1,0:T(1,128)S(1)} %copy-done.11, f32[32,512]{1,0:T(8,128)S(1)} %copy-done.5, f32[32,512]{1,0:T(8,128)S(1)} %copy-done.6, ...), custom_call_target="tpu_custom_call" | custom-call | flops 10000000 | bytes 4000000 | tf_op jit(solution)/shard_map/pallas_call | solution.py:410
  89.5 3.8 %collective-permute-start.1 = (f32[8,32,512]{2,1,0:T(8,128)S(1)}, f32[8,32,512]{2,1,0:T(8,128)S(1)}, u32[]{:S(2)}, u32[]{:S(2)}) collective-permute-start(f32[8,32,512]{2,1,0:T(8,128)S(1)} %get-tuple-element.36), channel_id=1, source_target_pairs={{0,1},{1,0},{2,3},{3,2},{4,5},{5,4},{6,7},{7,6},{8,9},{9,8},{10,11... | collective-permute-start | bytes 1572872 | tf_op jit(solution)/shard_map/ppermute | solution.py:513
  93.3 1.4 %shard_map.214 = f32[8,32,512]{2,1,0:T(8,128)S(1)} custom-call(s32[4]{0:T(128)S(1)} %pad_add_fusion.place, f32[8,32,512]{2,1,0:T(8,128)S(1)} %get-tuple-element.35.modes, bf16[512,512]{1,0:T(8,128)(2,1)S(1)} %copy-done, bf16[512,512]{1,0:T(8,128)(2,1)S(1)} %copy-done.1, bf16[256,256]{1,0:T(8,128)(2,1)S(1)} %copy-done.3, bf16[256,256]{1,0:T(8,128)(2,1)S(1)} %copy-done.2), custom_call_target="tpu_custom_call" | custom-call | flops 10000000 | bytes 4000000 | tf_op jit(solution)/shard_map/pallas_call | solution.py:410
  94.7 0.1 collective-permute-done.1
  94.8 0.1 fusion
  95.0 1.1 %pad_maximum_fusion = f32[8,32,1024]{2,1,0:T(8,128)} fusion(f32[8,32,512]{2,1,0:T(8,128)S(1)} %get-tuple-element.38, f32[8,32,512]{2,1,0:T(8,128)S(1)} %get-tuple-element.37), kind=kLoop, calls=%fused_computation | loop fusion | flops 262144 | bytes 2097152 | tf_op jit(solution)/shard_map/concatenate | solution.py:516
  (6 shorter events, 0.0 us)
Async XLA Ops:
  0.1 5.7 %copy-start.2 = (bf16[256,256]{1,0:T(8,128)(2,1)S(1)}, bf16[256,256]{1,0:T(8,128)(2,1)}, u32[]{:S(2)}) copy-start(bf16[256,256]{1,0:T(8,128)(2,1)} %constant.63.clone.slab_low) | copy-start | bytes 393220
  0.1 5.7 %copy-start.3 = (bf16[256,256]{1,0:T(8,128)(2,1)S(1)}, bf16[256,256]{1,0:T(8,128)(2,1)}, u32[]{:S(2)}) copy-start(bf16[256,256]{1,0:T(8,128)(2,1)} %constant.62.clone.slab_high) | copy-start | bytes 393220
  0.1 5.7 %copy-start.5 = (f32[32,512]{1,0:T(8,128)S(1)}, f32[32,512]{1,0:T(8,128)}, u32[]{:S(2)}) copy-start(f32[32,512]{1,0:T(8,128)} %constant.65.clone.shift_col) | copy-start | bytes 196612
  2.3 3.4 %copy-start.15 = (f32[64]{0:T(128)S(1)}, f32[64]{0:T(128)}, u32[]{:S(2)}) copy-start(f32[64]{0:T(128)} %param.25) | copy-start | bytes 772
  2.4 3.4 %copy-start.16 = (f32[64]{0:T(128)S(1)}, f32[64]{0:T(128)}, u32[]{:S(2)}) copy-start(f32[64]{0:T(128)} %param.24) | copy-start | bytes 772
  2.4 3.4 %copy-start.17 = (f32[64]{0:T(128)S(1)}, f32[64]{0:T(128)}, u32[]{:S(2)}) copy-start(f32[64]{0:T(128)} %param.23) | copy-start | bytes 772
  2.4 3.4 %copy-start.11 = (f32[2,1,512]{2,1,0:T(1,128)S(1)}, f32[2,1,512]{2,1,0:T(1,128)}, u32[]{:S(2)}) copy-start(f32[2,1,512]{2,1,0:T(1,128)} %constant.64.clone.shift_y) | copy-start | bytes 12292
  2.4 5.1 %collective-permute-start = (f32[8,32,512]{2,1,0:T(8,128)S(1)}, f32[8,32,512]{2,1,0:T(8,128)S(1)}, u32[]{:S(2)}, u32[]{:S(2)}) collective-permute-start(f32[8,32,512]{2,1,0:T(8,128)S(1)} %get-tuple-element.25), channel_id=1, source_target_pairs={{0,1},{1,0},{2,3},{3,2},{4,5},{5,4},{6,7},{7,6},{8,9},{9,8},{10,11... | collective-permute-start | bytes 1572872 | tf_op jit(solution)/shard_map/ppermute | solution.py:463
  5.8 1.7 %copy-start.6 = (f32[32,512]{1,0:T(8,128)S(1)}, f32[32,512]{1,0:T(8,128)}, u32[]{:S(2)}) copy-start(f32[32,512]{1,0:T(8,128)} %constant.66.clone.weights) | copy-start | bytes 196612
  5.8 1.7 %copy-start.12 = (bf16[32,128]{1,0:T(8,128)(2,1)S(1)}, bf16[32,128]{1,0:T(8,128)(2,1)}, u32[]{:S(2)}) copy-start(bf16[32,128]{1,0:T(8,128)(2,1)} %constant.67.clone.fold) | copy-start | bytes 24580
  11.1 14.0 %copy-start.7 = (f32[64,512]{1,0:T(8,128)S(1)}, f32[64,512]{1,0:T(8,128)}, u32[]{:S(2)}) copy-start(f32[64,512]{1,0:T(8,128)} %constant.73.clone.spread) | copy-start | bytes 393220
  11.2 14.0 %copy-start.9 = (f32[128,128]{1,0:T(8,128)S(1)}, f32[128,128]{1,0:T(8,128)}, u32[]{:S(2)}) copy-start(f32[128,128]{1,0:T(8,128)} %constant.74.clone.mask) | copy-start | bytes 196612
  11.2 14.0 %copy-start.10 = (f32[32,128]{1,0:T(8,128)S(1)}, f32[32,128]{1,0:T(8,128)}, u32[]{:S(2)}) copy-start(f32[32,128]{1,0:T(8,128)} %constant.71.clone.alias_shift) | copy-start | bytes 49156
  11.2 14.0 %copy-start.13 = (f32[1024]{0:T(1024)S(1)}, f32[1024]{0:T(1024)}, u32[]{:S(2)}) copy-start(f32[1024]{0:T(1024)} %constant.70.clone.shift_y) | copy-start | bytes 12292
  11.2 14.0 %copy-start.14 = (f32[1,128]{1,0:T(1,128)S(1)}, f32[1,128]{1,0:T(1,128)}, u32[]{:S(2)}) copy-start(f32[1,128]{1,0:T(1,128)} %constant.72.clone.mode_shift) | copy-start | bytes 1540
  11.2 48.1 %all-to-all-start = ((f32[128,4,128]{2,1,0:T(4,128)}), f32[128,4,128]{2,1,0:T(4,128)S(1)}, u32[]{:S(2)}, u32[]{:S(2)}) async-start(f32[128,4,128]{2,1,0:T(4,128)} %bitcast.11), calls=%async_computation | async-start | bytes 524288 | tf_op jit(solution)/shard_map/all_to_all | solution.py:450
  59.3 28.0 %copy-start.1 = (bf16[512,512]{1,0:T(8,128)(2,1)S(1)}, bf16[512,512]{1,0:T(8,128)(2,1)}, u32[]{:S(2)}) copy-start(bf16[512,512]{1,0:T(8,128)(2,1)} %get-tuple-element.34.table_low) | copy-start | bytes 1572868
  59.3 28.0 %copy-start.4 = (f32[16,32,512]{2,1,0:T(8,128)S(1)}, f32[16,32,512]{2,1,0:T(8,128)}, u32[]{:S(2)}) copy-start(f32[16,32,512]{2,1,0:T(8,128)} %get-tuple-element.27.modes) | copy-start | bytes 3145732
  59.3 28.0 %copy-start.8 = (f32[32,512]{1,0:T(8,128)S(1)}, f32[32,512]{1,0:T(8,128)}, u32[]{:S(2)}) copy-start(f32[32,512]{1,0:T(8,128)} %constant.77.clone.signs) | copy-start | bytes 196612
  62.3 25.0 %copy-start = (bf16[512,512]{1,0:T(8,128)(2,1)S(1)}, bf16[512,512]{1,0:T(8,128)(2,1)}, u32[]{:S(2)}) copy-start(bf16[512,512]{1,0:T(8,128)(2,1)} %get-tuple-element.33.table_high) | copy-start | bytes 1572868
  89.5 5.3 %collective-permute-start.1 = (f32[8,32,512]{2,1,0:T(8,128)S(1)}, f32[8,32,512]{2,1,0:T(8,128)S(1)}, u32[]{:S(2)}, u32[]{:S(2)}) collective-permute-start(f32[8,32,512]{2,1,0:T(8,128)S(1)} %get-tuple-element.36), channel_id=1, source_target_pairs={{0,1},{1,0},{2,3},{3,2},{4,5},{5,4},{6,7},{7,6},{8,9},{9,8},{10,11... | collective-permute-start | bytes 1572872 | tf_op jit(solution)/shard_map/ppermute | solution.py:513

commit v4 on v3

--- a/solution.py
+++ b/solution.py
@@ -169,10 +169,14 @@
         copy.wait()
 
 
+def widen(table):
+    return jnp.concatenate([table[...]] * PARTS, axis=1)
+
+
 def chip_pivots(place, shift_y, shift_col, coefficients, inverse):
     cell, face, screening = columns_of(coefficients)
     base = place[1] * LAYERS
-    shifts = shift_col[...] + shift_y[place[0]]
+    shifts = widen(shift_col) + shift_y[place[0]]
     previous = None
     for layer in range(1, LAYERS):
         below, above = face[base + layer - 1], face[base + layer]
@@ -208,20 +212,23 @@
     return jnp.concatenate([turned[part * PLANES : (part + 1) * PLANES] for part in range(PARTS)], axis=1)
 
 
-def forward_kernel(place, own_modes, other, table_high, table_low, slab_high, slab_low, inverse, weights, fold, coefficients, kept, out, modes, part, folded, sem):
+def forward_kernel(place, own_modes, other, table_high, table_low, slab_high, slab_low, inverse, weights, fold, coefficients, kept, out, modes, part, folded, sems):
     core, base = place[0], place[1] * LAYERS
     cell, face, _ = columns_of(coefficients)
+    copies = [pltpu.make_async_copy(own_modes, kept.at[pl.ds(core * 8, 8)], sems.at[0])]
+    copies[0].start()
     modes[pl.ds(core * 8, 8)] = own_modes[...]
     modes[pl.ds((1 - core) * 8, 8)] = to_modes(other, table_high, table_low, slab_high, slab_low)
-    copy = pltpu.make_async_copy(modes, kept, sem)
-    copy.start()
+    far_half = pl.ds((1 - core) * 8, 8)
+    copies.append(pltpu.make_async_copy(modes.at[far_half], kept.at[far_half], sems.at[1]))
+    copies[1].start()
     value = None
     for layer in range(1, LAYERS):
         inv = inverse[layer]
         scaled = modes[layer] * inv
         value = scaled if value is None else scaled + (face[base + layer - 1] * inv) * value
         part[layer] = value
-    weight = weights[...]
+    weight = widen(weights)
     value = None
     folded[0:8] = jnp.zeros((8, HALF), jnp.float32)
     for layer in reversed(range(1, LAYERS)):
@@ -240,13 +247,14 @@
     blocks = [half[:, step * LANES : (step + 1) * LANES] for half in (near, far) for step in range(PARTS)]
     out[pl.ds(2, PEERS, stride=ROWS), :] = jnp.concatenate(blocks, axis=0).T
     out[pl.ds(3, PEERS, stride=ROWS), :] = jnp.zeros((PEERS, LANES), jnp.float32)
-    copy.wait()
-
-
-def prepare_kernel(place, shift_y, alias_shift, mode_shift, spread, mask, tables_high, tables_low, coefficients, alias_inverse, response_high, response_low, corners, table_high, table_low, inverses, columns, scaled, sems):
+    for copy in copies:
+        copy.wait()
+
+
+def prepare_kernel(place, shift_y, alias_shift, mode_shift, spread, mask, tables_high, tables_low, coefficients, alias_inverse, response_high, response_low, corners, table_high, table_low, inverses, columns, scaled, held_high, held_low, sems):
     copies = [
-        pltpu.make_async_copy(tables_high.at[place[0]], table_high, sems.at[0]),
-        pltpu.make_async_copy(tables_low.at[place[0]], table_low, sems.at[1]),
+        pltpu.make_async_copy(tables_high.at[place[0]], held_high, sems.at[0]),
+        pltpu.make_async_copy(tables_low.at[place[0]], held_low, sems.at[1]),
     ]
     for copy in copies:
         copy.start()
@@ -288,6 +296,11 @@
         scaled[layer * 8 : (layer + 1) * 8] = cell[layer] * value
         if layer % LAYERS == 0:
             corners[layer // LAYERS] = value
+    for copy in copies:
+        copy.wait()
+    copies = [pltpu.make_async_copy(held_high, table_high, sems.at[2]), pltpu.make_async_copy(held_low, table_low, sems.at[3])]
+    for copy in copies:
+        copy.start()
     weight = jnp.concatenate([mask[...]] * CHIPS, axis=1)
     for chip in range(CHIPS):
         column = scaled[pl.ds(chip, NZ, stride=8), :]
@@ -299,11 +312,7 @@
         copy.wait()
 
 
-def interface_kernel(place, arrived, response_high, response_low, alias_inverse, forward_far, backward_far, corners_far, coefficients, out, source, part, solved, forward, backward, corners, sems):
-    pairs = ((forward_far, forward), (backward_far, backward), (corners_far, corners))
-    copies = [pltpu.make_async_copy(*pair, sems.at[step]) for step, pair in enumerate(pairs)]
-    for copy in copies:
-        copy.start()
+def interface_kernel(place, arrived, response_high, response_low, corners, alias_inverse, forward, backward, coefficients, out, source, part, solved):
     face = columns_of(coefficients)[1]
 
     def rows(chip, slot):
@@ -318,8 +327,6 @@
     sums = sums + jnp.concatenate([arrived[rows(chip, 2), :] for chip in range(CHIPS)], axis=1)
     high, low = split_values(sums)
     stacked = jnp.concatenate([high, high, low], axis=0)
-    for copy in copies:
-        copy.wait()
     turned = lax.dot_general(stacked, forward[...], (((0,), (0,)), ((), ())), preferred_element_type=jnp.float32)
     half = PARTS * LAYERS
     for chip in range(CHIPS):
@@ -372,8 +379,8 @@
         for step in range(PARTS):
             at = (which * PARTS + step) * LAYERS
             target[:, step * LANES : (step + 1) * LANES] = turned[at : at + LAYERS]
-    weight = weights[...]
-    signed = signs[...]
+    weight = widen(weights)
+    signed = widen(signs)
     keep = lax.broadcasted_iota(jnp.int32, (PLANES, HALF), 0) == 0
     value = None
     for layer in range(1, LAYERS):
@@ -429,7 +436,7 @@
     slab_high, slab_low = split_pair(np.kron(np.eye(8), slab_basis()))
     forward_slab, backward_slab, alias_shift = interface_tables()
     spread, mask = spread_tables()
-    weights = np.broadcast_to(near_weights()[:, None], (PLANES, HALF)).copy()
+    weights = np.broadcast_to(near_weights()[:, None], (PLANES, LANES)).copy()
     signs = weights * far_signs()[:, None]
     shift_y = y_shifts()
     mode_shift = np.tile(slab_shifts(), PARTS)[None, :]
@@ -461,7 +468,7 @@
         [lines, pltpu.SemaphoreType.DMA((10,))],
     )
     other = lax.ppermute(sent, "gz", pair)
-    shifts = (shift_y[:, None, :], np.broadcast_to(slab_shifts()[:, None], (PLANES, HALF)).copy())
+    shifts = (shift_y[:, None, :], np.broadcast_to(slab_shifts()[:, None], (PLANES, LANES)).copy())
     coefficients = jnp.concatenate([cell, face, screening])
     inverse, own_modes = call(
         early_kernel,
@@ -478,27 +485,26 @@
         [held] * 9 + [scalars],
         [pltpu.HBM(field, jnp.float32), pltpu.HBM(message, jnp.float32)],
         [far, held],
-        [vmem(*field), vmem(*field), vmem(8 * LAYERS, HALF), pltpu.SemaphoreType.DMA],
+        [vmem(*field), vmem(*field), vmem(8 * LAYERS, HALF), pltpu.SemaphoreType.DMA((2,))],
     )
     alias_inverse, response_high, response_low, corners, table_high, table_low = call(
         prepare_kernel,
         place,
         (shift_y.reshape(-1), alias_shift, mode_shift, spread, mask, in_hbm(by_high), in_hbm(by_low), coefficients),
         [scalars] + [held] * 4 + [far] * 2 + [scalars],
-        [vmem(NZ, 8 * PARTS, LANES), pltpu.VMEM(square, jnp.bfloat16), pltpu.VMEM(square, jnp.bfloat16), pltpu.HBM((CHIPS, 8, LANES), jnp.float32), far_table, far_table],
+        [vmem(NZ, 8 * PARTS, LANES), pltpu.VMEM(square, jnp.bfloat16), pltpu.VMEM(square, jnp.bfloat16), vmem(CHIPS, 8, LANES), far_table, far_table],
         [held] * 4 + [far] * 2,
-        [vmem(NZ, 8, LANES), vmem(NZ, 8, LANES), vmem(8 * NZ, LANES), pltpu.SemaphoreType.DMA((2,))],
+        [vmem(NZ, 8, LANES), vmem(NZ, 8, LANES), vmem(8 * NZ, LANES), table, table, pltpu.SemaphoreType.DMA((4,))],
     )
     ends = exchange(ends)
     ends = call(
         interface_kernel,
         place,
-        (ends, response_high, response_low, alias_inverse, in_hbm(forward_slab), in_hbm(backward_slab), in_hbm(corners), coefficients),
-        [held] * 4 + [far] * 3 + [scalars],
+        (ends, response_high, response_low, corners, alias_inverse, forward_slab, backward_slab, coefficients),
+        [held] * 7 + [scalars],
         vmem(*message),
         held,
-        [vmem(CHIPS * PARTS * LAYERS, LANES), vmem(NZ, 8 * PARTS, LANES), vmem(CHIPS * PARTS * LAYERS, LANES)]
-        + [pltpu.VMEM(forward_slab.shape, jnp.bfloat16), vmem(*backward_slab.shape), vmem(CHIPS, 8, LANES), pltpu.SemaphoreType.DMA((3,))],
+        [vmem(CHIPS * PARTS * LAYERS, LANES), vmem(NZ, 8 * PARTS, LANES), vmem(CHIPS * PARTS * LAYERS, LANES)],
     )
     ends = exchange(ends)
     kept, sent = call(

time: 96.3 us -> 68.2 us (0.71)
  Pallas kernels: 48.1 us -> 16.4 us
  waiting for transfers between devices: 0.14 us -> 10.1 us
  blocking collectives: 25 us -> 18.7 us
    pallas_call x7, Pallas kernels: 48.1 us -> 16.4 us  [call(): pl.pallas_call(kernel, grid=grid, in_specs=[scalars, *in_specs], out_spec...]
    all_to_all x1, waiting for transfers between devices: 0.01 us -> 9.92 us  [exchange(): lax.all_to_all(blocks, ('gx', 'gz'), 0, 0, axis_index_groups=groups, tile...]
    all_to_all x1, blocking collectives: 25 us -> 18.7 us  [exchange(): lax.all_to_all(blocks, ('gx', 'gz'), 0, 0, axis_index_groups=groups, tile...]
  transfers between devices with their start and end apart: 3 -> 3, of which waited for: 1 -> 2; matrix products, arithmetic and copies ran while one was open for 0% -> 0% of each run, Pallas kernels for 39% -> 9%
where the time goes in v4:
time: 68.2 us; the launch traced here: 67.9 us
  starting transfers between devices  21 us (31%)
  blocking collectives  18.7 us (27%)
  Pallas kernels  16.4 us (24%)
  waiting for transfers between devices  10.1 us (15%)
  other arithmetic  1.36 us (2%)
    all_to_all x1, blocking collectives, exchange(): lax.all_to_all(blocks, ('gx', 'gz'), 0, 0, axis_index_groups=groups, tile...  18.7 us
    pallas_call x7, Pallas kernels, call(): pl.pallas_call(kernel, grid=grid, in_specs=[scalars, *in_specs], out_spec...  16.4 us
    all_to_all x1, starting transfers between devices, exchange(): lax.all_to_all(blocks, ('gx', 'gz'), 0, 0, axis_index_groups=groups, tile...  13.9 us
    all_to_all x1, waiting for transfers between devices, exchange(): lax.all_to_all(blocks, ('gx', 'gz'), 0, 0, axis_index_groups=groups, tile...  9.92 us
    ppermute x2, starting transfers between devices, body(): other = lax.ppermute(sent, 'gz', pair)  7.11 us
  transfers between devices with their start and end apart: 3, of which 2 were waited for; matrix products, arithmetic and copies ran while one was open for 0% of the time, Pallas kernels for 9%

profile of v4, /device:TPU:1, one launch (start us, length us, event | category | flops | bytes accessed | tf_op | source)
XLA Modules:
  0.0 67.9 jit_solution(15796464292992555635)
XLA Ops:
  0.0 0.1 pad_add_fusion.place
  0.1 2.2 %shard_map.208 = (f32[8,32,512]{2,1,0:T(8,128)S(1)}, f32[8,32,512]{2,1,0:T(8,128)S(1)}, bf16[512,512]{1,0:T(8,128)(2,1)S(1)}, bf16[512,512]{1,0:T(8,128)(2,1)S(1)}) custom-call(s32[4]{0:T(128)S(1)} %pad_add_fusion.place, f32[8,32,1024]{2,1,0:T(8,128)} %charge.1, bf16[2,512,512]{2,1,0:T(8,128)(2,1)} %constant.60.clone.tables_high, ...), custom_call_target="tpu_custom_call" | custom-call | flops 10000000 | bytes 4000000 | tf_op jit(solution)/shard_map/pallas_call | solution.py:417
  2.3 0.0 copy-start.17
  2.4 0.0 copy-start.18
  2.4 0.0 copy-start.19
  2.4 0.0 copy-start.13
  2.4 3.3 %collective-permute-start = (f32[8,32,512]{2,1,0:T(8,128)S(1)}, f32[8,32,512]{2,1,0:T(8,128)S(1)}, u32[]{:S(2)}, u32[]{:S(2)}) collective-permute-start(f32[8,32,512]{2,1,0:T(8,128)S(1)} %get-tuple-element.25), channel_id=1, source_target_pairs={{0,1},{1,0},{2,3},{3,2},{4,5},{5,4},{6,7},{7,6},{8,9},{9,8},{10,11... | collective-permute-start | bytes 1572872 | tf_op jit(solution)/shard_map/ppermute | solution.py:470
  5.7 0.0 copy-done.17
  5.7 0.0 copy-done.18
  5.7 0.0 copy-done.19
  5.7 0.1 pad_maximum_fusion.1.coefficients
  5.8 0.0 copy-done.2
  5.8 0.0 copy-done.3
  5.8 0.0 copy-done.6
  5.8 0.0 copy-done.13
  5.8 0.0 copy-start.7
  5.8 0.0 copy-start.14
  5.8 1.6 %shard_map.209 = (f32[16,32,512]{2,1,0:T(8,128)S(1)}, f32[8,32,512]{2,1,0:T(8,128)S(1)}) custom-call(s32[4]{0:T(128)S(1)} %pad_add_fusion.place, f32[8,32,512]{2,1,0:T(8,128)S(1)} %get-tuple-element.21.own, bf16[512,512]{1,0:T(8,128)(2,1)S(1)} %get-tuple-element.22.table_high, bf16[512,512]{1,0:T(8,128)(2,1)S(1)} %get-tuple-element.23.table_low, ...), custom_call_target="tpu_custom_call" | custom-call | flops 10000000 | bytes 4000000 | tf_op jit(solution)/shard_map/pallas_call | solution.py:417
  7.5 0.0 collective-permute-done.other
  7.5 0.0 copy-done.7
  7.5 0.0 copy-done.14
  7.5 3.6 %shard_map.210 = (f32[16,32,512]{2,1,0:T(8,128)}, f32[512,128]{1,0:T(8,128)}) custom-call(s32[4]{0:T(128)S(1)} %pad_add_fusion.place, f32[8,32,512]{2,1,0:T(8,128)S(1)} %get-tuple-element.24.own_modes, f32[8,32,512]{2,1,0:T(8,128)S(1)} %collective-permute-done.other, bf16[512,512]{1,0:T(8,128)(2,1)S(1)} %get-tuple-element.22.table_high, ...), custom_call_target="tpu_custom_call" | custom-call | flops 10000000 | bytes 4000000 | tf_op jit(solution)/shard_map/pallas_call | solution.py:417
  11.1 0.0 copy-start.5
  11.1 0.0 copy-start.8
  11.1 0.0 copy-start.12
  11.1 0.0 copy-start.15
  11.2 0.0 copy-start.16
  11.2 13.9 %all-to-all-start = ((f32[128,4,128]{2,1,0:T(4,128)}), f32[128,4,128]{2,1,0:T(4,128)S(1)}, u32[]{:S(2)}, u32[]{:S(2)}) async-start(f32[128,4,128]{2,1,0:T(4,128)} %bitcast.11), calls=%async_computation | async-start | bytes 524288 | tf_op jit(solution)/shard_map/all_to_all | solution.py:457
  25.1 0.0 copy-done.5
  25.1 0.0 copy-done.8
  25.1 0.0 copy-done.12
  25.1 0.0 copy-done.15
  25.1 0.0 copy-done.16
  25.2 0.0 copy-start.9
  25.2 0.0 copy-start.10
  25.2 2.9 %shard_map.211 = (f32[64,32,128]{2,1,0:T(8,128)S(1)}, bf16[512,512]{1,0:T(8,128)(2,1)S(1)}, bf16[512,512]{1,0:T(8,128)(2,1)S(1)}, f32[4,8,128]{2,1,0:T(8,128)S(1...) custom-call(s32[4]{0:T(128)S(1)} %pad_add_fusion.place, f32[1024]{0:T(1024)S(1)} %copy-done.15, ...), custom_call_target="tpu_custom_call" | custom-call | flops 10000000 | bytes 4000000 | tf_op jit(solution)/shard_map/pallas_call | solution.py:417
  28.1 9.9 %all-to-all-done = f32[128,4,128]{2,1,0:T(4,128)S(1)} async-done(((f32[128,4,128]{2,1,0:T(4,128)}), f32[128,4,128]{2,1,0:T(4,128)S(1)}, u32[]{:S(2)}, u32[]{:S(2)}) %all-to-all-start) | async-done | bytes 262176 | tf_op jit(solution)/shard_map/all_to_all | solution.py:457
  38.0 0.0 copy-done.10
  38.0 0.0 copy-start.11
  38.1 2.5 %shard_map.212 = f32[512,128]{1,0:T(8,128)S(1)} custom-call(s32[4]{0:T(128)S(1)} %pad_add_fusion.place, f32[512,128]{1,0:T(8,128)S(1)} %bitcast.8, bf16[512,512]{1,0:T(8,128)(2,1)S(1)} %get-tuple-element.29.response_high, bf16[512,512]{1,0:T(8,128)(2,1)S(1)} %get-tuple-element.30.response_low, f32[4,8,128]{2,1,0:T(8,128)S(1)} %get-tuple-element.31.corners, ...), custom_call_target="tpu_custom_call" | custom-call | flops 10000000 | bytes 4000000 | tf_op jit(solution)/shard_map/pallas_call | solution.py:417
  40.5 18.7 %all_to_all.10 = f32[128,4,128]{2,1,0:T(4,128)S(1)} all-to-all(f32[128,4,128]{2,1,0:T(4,128)S(1)} %bitcast.10), channel_id=1, replica_groups={{0,2,4,6,8,10,12,14,16,18,20,22,24,26,28,30,32,34,36,38,40,42,44,46,48,..., dimensions={0} | all-to-all | bytes 524288 | tf_op jit(solution)/shard_map/all_to_all | solution.py:457
  59.3 0.0 copy-done
  59.3 2.1 %shard_map.213 = (f32[8,32,512]{2,1,0:T(8,128)S(1)}, f32[8,32,512]{2,1,0:T(8,128)S(1)}) custom-call(s32[4]{0:T(128)S(1)} %pad_add_fusion.place, f32[16,32,512]{2,1,0:T(8,128)S(1)} %copy-done.4, f32[512,128]{1,0:T(8,128)S(1)} %bitcast.9, f32[2,1,512]{2,1,0:T(1,128)S(1)} %copy-done.13, f32[32,128]{1,0:T(8,128)S(1)} %copy-done.6, f32[32,128]{1,0:T(8,128)S(1)} %copy-done.7, ...), custom_call_target="tpu_custom_call" | custom-call | flops 10000000 | bytes 4000000 | tf_op jit(solution)/shard_map/pallas_call | solution.py:417
  61.4 3.8 %collective-permute-start.1 = (f32[8,32,512]{2,1,0:T(8,128)S(1)}, f32[8,32,512]{2,1,0:T(8,128)S(1)}, u32[]{:S(2)}, u32[]{:S(2)}) collective-permute-start(f32[8,32,512]{2,1,0:T(8,128)S(1)} %get-tuple-element.36), channel_id=1, source_target_pairs={{0,1},{1,0},{2,3},{3,2},{4,5},{5,4},{6,7},{7,6},{8,9},{9,8},{10,11... | collective-permute-start | bytes 1572872 | tf_op jit(solution)/shard_map/ppermute | solution.py:519
  65.2 1.4 %shard_map.214 = f32[8,32,512]{2,1,0:T(8,128)S(1)} custom-call(s32[4]{0:T(128)S(1)} %pad_add_fusion.place, f32[8,32,512]{2,1,0:T(8,128)S(1)} %get-tuple-element.35.modes, bf16[512,512]{1,0:T(8,128)(2,1)S(1)} %copy-done, bf16[512,512]{1,0:T(8,128)(2,1)S(1)} %copy-done.1, bf16[256,256]{1,0:T(8,128)(2,1)S(1)} %copy-done.3, bf16[256,256]{1,0:T(8,128)(2,1)S(1)} %copy-done.2), custom_call_target="tpu_custom_call" | custom-call | flops 10000000 | bytes 4000000 | tf_op jit(solution)/shard_map/pallas_call | solution.py:417
  66.6 0.1 collective-permute-done.1
  66.7 0.1 fusion
  66.9 1.1 %pad_maximum_fusion = f32[8,32,1024]{2,1,0:T(8,128)} fusion(f32[8,32,512]{2,1,0:T(8,128)S(1)} %get-tuple-element.38, f32[8,32,512]{2,1,0:T(8,128)S(1)} %get-tuple-element.37), kind=kLoop, calls=%fused_computation | loop fusion | flops 262144 | bytes 2097152 | tf_op jit(solution)/shard_map/concatenate | solution.py:522
  (10 shorter events, 0.0 us)
Async XLA Ops:
  0.1 5.7 %copy-start.2 = (bf16[256,256]{1,0:T(8,128)(2,1)S(1)}, bf16[256,256]{1,0:T(8,128)(2,1)}, u32[]{:S(2)}) copy-start(bf16[256,256]{1,0:T(8,128)(2,1)} %constant.63.clone.slab_low) | copy-start | bytes 393220
  0.1 5.7 %copy-start.3 = (bf16[256,256]{1,0:T(8,128)(2,1)S(1)}, bf16[256,256]{1,0:T(8,128)(2,1)}, u32[]{:S(2)}) copy-start(bf16[256,256]{1,0:T(8,128)(2,1)} %constant.62.clone.slab_high) | copy-start | bytes 393220
  0.1 5.7 %copy-start.6 = (f32[32,128]{1,0:T(8,128)S(1)}, f32[32,128]{1,0:T(8,128)}, u32[]{:S(2)}) copy-start(f32[32,128]{1,0:T(8,128)} %constant.65.clone.shift_col) | copy-start | bytes 49156
  2.3 3.4 %copy-start.17 = (f32[64]{0:T(128)S(1)}, f32[64]{0:T(128)}, u32[]{:S(2)}) copy-start(f32[64]{0:T(128)} %param.25) | copy-start | bytes 772
  2.4 3.4 %copy-start.18 = (f32[64]{0:T(128)S(1)}, f32[64]{0:T(128)}, u32[]{:S(2)}) copy-start(f32[64]{0:T(128)} %param.24) | copy-start | bytes 772
  2.4 3.4 %copy-start.19 = (f32[64]{0:T(128)S(1)}, f32[64]{0:T(128)}, u32[]{:S(2)}) copy-start(f32[64]{0:T(128)} %param.23) | copy-start | bytes 772
  2.4 3.4 %copy-start.13 = (f32[2,1,512]{2,1,0:T(1,128)S(1)}, f32[2,1,512]{2,1,0:T(1,128)}, u32[]{:S(2)}) copy-start(f32[2,1,512]{2,1,0:T(1,128)} %constant.64.clone.shift_y) | copy-start | bytes 12292
  2.4 5.1 %collective-permute-start = (f32[8,32,512]{2,1,0:T(8,128)S(1)}, f32[8,32,512]{2,1,0:T(8,128)S(1)}, u32[]{:S(2)}, u32[]{:S(2)}) collective-permute-start(f32[8,32,512]{2,1,0:T(8,128)S(1)} %get-tuple-element.25), channel_id=1, source_target_pairs={{0,1},{1,0},{2,3},{3,2},{4,5},{5,4},{6,7},{7,6},{8,9},{9,8},{10,11... | collective-permute-start | bytes 1572872 | tf_op jit(solution)/shard_map/ppermute | solution.py:470
  5.8 1.7 %copy-start.7 = (f32[32,128]{1,0:T(8,128)S(1)}, f32[32,128]{1,0:T(8,128)}, u32[]{:S(2)}) copy-start(f32[32,128]{1,0:T(8,128)} %constant.66.clone.weights) | copy-start | bytes 49156
  5.8 1.7 %copy-start.14 = (bf16[32,128]{1,0:T(8,128)(2,1)S(1)}, bf16[32,128]{1,0:T(8,128)(2,1)}, u32[]{:S(2)}) copy-start(bf16[32,128]{1,0:T(8,128)(2,1)} %constant.67.clone.fold) | copy-start | bytes 24580
  11.1 14.0 %copy-start.5 = (f32[64,512]{1,0:T(8,128)S(1)}, f32[64,512]{1,0:T(8,128)}, u32[]{:S(2)}) copy-start(f32[64,512]{1,0:T(8,128)} %constant.73.clone.spread) | copy-start | bytes 393220
  11.1 14.0 %copy-start.8 = (f32[128,128]{1,0:T(8,128)S(1)}, f32[128,128]{1,0:T(8,128)}, u32[]{:S(2)}) copy-start(f32[128,128]{1,0:T(8,128)} %constant.74.clone.mask) | copy-start | bytes 196612
  11.1 14.0 %copy-start.12 = (f32[32,128]{1,0:T(8,128)S(1)}, f32[32,128]{1,0:T(8,128)}, u32[]{:S(2)}) copy-start(f32[32,128]{1,0:T(8,128)} %constant.71.clone.alias_shift) | copy-start | bytes 49156
  11.1 14.0 %copy-start.15 = (f32[1024]{0:T(1024)S(1)}, f32[1024]{0:T(1024)}, u32[]{:S(2)}) copy-start(f32[1024]{0:T(1024)} %constant.70.clone.shift_y) | copy-start | bytes 12292
  11.2 14.0 %copy-start.16 = (f32[1,128]{1,0:T(1,128)S(1)}, f32[1,128]{1,0:T(1,128)}, u32[]{:S(2)}) copy-start(f32[1,128]{1,0:T(1,128)} %constant.72.clone.mode_shift) | copy-start | bytes 1540
  11.2 26.9 %all-to-all-start = ((f32[128,4,128]{2,1,0:T(4,128)}), f32[128,4,128]{2,1,0:T(4,128)S(1)}, u32[]{:S(2)}, u32[]{:S(2)}) async-start(f32[128,4,128]{2,1,0:T(4,128)} %bitcast.11), calls=%async_computation | async-start | bytes 524288 | tf_op jit(solution)/shard_map/all_to_all | solution.py:457
  25.2 12.9 %copy-start.9 = (bf16[96,256]{1,0:T(8,128)(2,1)S(1)}, bf16[96,256]{1,0:T(8,128)(2,1)}, u32[]{:S(2)}) copy-start(bf16[96,256]{1,0:T(8,128)(2,1)} %constant.75.clone.forward) | copy-start | bytes 147460
  25.2 12.9 %copy-start.10 = (f32[64,128]{1,0:T(8,128)S(1)}, f32[64,128]{1,0:T(8,128)}, u32[]{:S(2)}) copy-start(f32[64,128]{1,0:T(8,128)} %constant.76.clone.backward) | copy-start | bytes 98308
  38.0 21.2 %copy-start.1 = (bf16[512,512]{1,0:T(8,128)(2,1)S(1)}, bf16[512,512]{1,0:T(8,128)(2,1)}, u32[]{:S(2)}) copy-start(bf16[512,512]{1,0:T(8,128)(2,1)} %get-tuple-element.34.table_low) | copy-start | bytes 1572868
  38.0 21.2 %copy-start.4 = (f32[16,32,512]{2,1,0:T(8,128)S(1)}, f32[16,32,512]{2,1,0:T(8,128)}, u32[]{:S(2)}) copy-start(f32[16,32,512]{2,1,0:T(8,128)} %get-tuple-element.27.modes) | copy-start | bytes 3145732
  38.0 21.2 %copy-start.11 = (f32[32,128]{1,0:T(8,128)S(1)}, f32[32,128]{1,0:T(8,128)}, u32[]{:S(2)}) copy-start(f32[32,128]{1,0:T(8,128)} %constant.77.clone.signs) | copy-start | bytes 49156
  40.5 18.7 %copy-start = (bf16[512,512]{1,0:T(8,128)(2,1)S(1)}, bf16[512,512]{1,0:T(8,128)(2,1)}, u32[]{:S(2)}) copy-start(bf16[512,512]{1,0:T(8,128)(2,1)} %get-tuple-element.33.table_high) | copy-start | bytes 1572868
  61.4 5.3 %collective-permute-start.1 = (f32[8,32,512]{2,1,0:T(8,128)S(1)}, f32[8,32,512]{2,1,0:T(8,128)S(1)}, u32[]{:S(2)}, u32[]{:S(2)}) collective-permute-start(f32[8,32,512]{2,1,0:T(8,128)S(1)} %get-tuple-element.36), channel_id=1, source_target_pairs={{0,1},{1,0},{2,3},{3,2},{4,5},{5,4},{6,7},{7,6},{8,9},{9,8},{10,11... | collective-permute-start | bytes 1572872 | tf_op jit(solution)/shard_map/ppermute | solution.py:519

commit v5 on v4

--- a/solution.py
+++ b/solution.py
@@ -119,16 +119,23 @@
     return spread.reshape(NZ, CHIPS * LANES), mask.reshape(LANES, LANES)
 
 
+def position():
+    gz = lax.axis_index("gz")
+    core, chip = lax.rem(gz, 2), lax.div(gz, 2)
+    return core, chip, lax.axis_index("gx") * CHIPS + chip
+
+
 class Column:
-    def __init__(self, ref, which):
-        self.ref, self.start = ref, which * NZ
+    def __init__(self, ref, which, repeat):
+        self.ref, self.start, self.repeat = ref, which * NZ, repeat
 
     def __getitem__(self, layer):
-        return self.ref[self.start + layer]
-
-
-def columns_of(ref):
-    return [Column(ref, which) for which in range(3)]
+        row = self.ref[pl.ds(self.start + layer, 1), :]
+        return jnp.concatenate([row] * self.repeat, axis=1)
+
+
+def columns_of(ref, repeat=1):
+    return [Column(ref, which, repeat) for which in range(3)]
 
 
 def split_values(values):
@@ -153,30 +160,37 @@
     )
 
 
-def split_kernel(place, charge, tables_high, tables_low, own, sent, table_high, table_low, held_charge, sems):
-    copies = [pltpu.make_async_copy(charge.at[step], held_charge.at[step], sems.at[step]) for step in range(8)]
-    copies.append(pltpu.make_async_copy(tables_high.at[place[0]], table_high, sems.at[8]))
-    copies.append(pltpu.make_async_copy(tables_low.at[place[0]], table_low, sems.at[9]))
+def split_kernel(charge, tables_high, tables_low, cell, face, screening, own, sent, table_high, table_low, coefficients, lines, rows, sems):
+    core, _, _ = position()
+    copies = [pltpu.make_async_copy(source, rows.at[step], sems.at[10 + step]) for step, source in enumerate((cell, face, screening))]
+    copies += [pltpu.make_async_copy(charge.at[step], lines.at[step], sems.at[step]) for step in range(8)]
+    copies.append(pltpu.make_async_copy(tables_high.at[core], table_high, sems.at[8]))
+    copies.append(pltpu.make_async_copy(tables_low.at[core], table_low, sems.at[9]))
     for copy in copies:
         copy.start()
-    sign = jnp.where(place[0] == 0, 1.0, -1.0)
-    for step, copy in enumerate(copies[:8]):
+    for step, copy in enumerate(copies[:3]):
         copy.wait()
-        lower, upper = held_charge[step, :, :HALF], sign * held_charge[step, :, HALF:]
+        coefficients[step * NZ : (step + 1) * NZ, :] = jnp.broadcast_to(rows[step], (LANES, NZ)).T
+    sign = jnp.where(core == 0, 1.0, -1.0)
+    for step, copy in enumerate(copies[3:11]):
+        copy.wait()
+        lower, upper = lines[step, :, :HALF], sign * lines[step, :, HALF:]
         own[step] = lower + upper
         sent[step] = lower - upper
-    for copy in copies[8:]:
+    for copy in copies[11:]:
         copy.wait()
 
 
 def widen(table):
-    return jnp.concatenate([table[...]] * PARTS, axis=1)
-
-
-def chip_pivots(place, shift_y, shift_col, coefficients, inverse):
-    cell, face, screening = columns_of(coefficients)
-    base = place[1] * LAYERS
-    shifts = widen(shift_col) + shift_y[place[0]]
+    return jnp.concatenate([table] * PARTS, axis=1)
+
+
+def chip_pivots(shifts, coefficients, inverse):
+    cell, face, screening = columns_of(coefficients, PARTS)
+    core, chip, _ = position()
+    base = chip * LAYERS
+    row = jnp.concatenate([shifts[pl.ds(core * PARTS + part, 1), :] for part in range(PARTS)], axis=1)
+    shifts = widen(shifts[8:]) + row
     previous = None
     for layer in range(1, LAYERS):
         below, above = face[base + layer - 1], face[base + layer]
@@ -187,8 +201,8 @@
         inverse[layer] = previous
 
 
-def early_kernel(place, own, table_high, table_low, slab_high, slab_low, shift_y, shift_col, coefficients, inverse, modes):
-    chip_pivots(place, shift_y, shift_col, coefficients, inverse)
+def early_kernel(own, table_high, table_low, slab_high, slab_low, shifts, coefficients, inverse, modes):
+    chip_pivots(shifts, coefficients, inverse)
     modes[...] = to_modes(own, table_high, table_low, slab_high, slab_low)
 
 
@@ -212,23 +226,19 @@
     return jnp.concatenate([turned[part * PLANES : (part + 1) * PLANES] for part in range(PARTS)], axis=1)
 
 
-def forward_kernel(place, own_modes, other, table_high, table_low, slab_high, slab_low, inverse, weights, fold, coefficients, kept, out, modes, part, folded, sems):
-    core, base = place[0], place[1] * LAYERS
-    cell, face, _ = columns_of(coefficients)
-    copies = [pltpu.make_async_copy(own_modes, kept.at[pl.ds(core * 8, 8)], sems.at[0])]
-    copies[0].start()
+def forward_kernel(own_modes, other, table_high, table_low, slab_high, slab_low, inverse, weights, fold, coefficients, modes, out, part, folded):
+    core, chip, _ = position()
+    base = chip * LAYERS
+    cell, face, _ = columns_of(coefficients, PARTS)
     modes[pl.ds(core * 8, 8)] = own_modes[...]
     modes[pl.ds((1 - core) * 8, 8)] = to_modes(other, table_high, table_low, slab_high, slab_low)
-    far_half = pl.ds((1 - core) * 8, 8)
-    copies.append(pltpu.make_async_copy(modes.at[far_half], kept.at[far_half], sems.at[1]))
-    copies[1].start()
     value = None
     for layer in range(1, LAYERS):
         inv = inverse[layer]
         scaled = modes[layer] * inv
         value = scaled if value is None else scaled + (face[base + layer - 1] * inv) * value
         part[layer] = value
-    weight = widen(weights)
+    weight = widen(weights[:PLANES])
     value = None
     folded[0:8] = jnp.zeros((8, HALF), jnp.float32)
     for layer in reversed(range(1, LAYERS)):
@@ -247,28 +257,30 @@
     blocks = [half[:, step * LANES : (step + 1) * LANES] for half in (near, far) for step in range(PARTS)]
     out[pl.ds(2, PEERS, stride=ROWS), :] = jnp.concatenate(blocks, axis=0).T
     out[pl.ds(3, PEERS, stride=ROWS), :] = jnp.zeros((PEERS, LANES), jnp.float32)
-    for copy in copies:
-        copy.wait()
-
-
-def prepare_kernel(place, shift_y, alias_shift, mode_shift, spread, mask, tables_high, tables_low, coefficients, alias_inverse, response_high, response_low, corners, table_high, table_low, inverses, columns, scaled, held_high, held_low, sems):
+
+
+def keep_kernel(modes, kept, sem):
+    copy = pltpu.make_async_copy(modes, kept, sem)
+    copy.start()
+    copy.wait()
+
+
+def prepare_kernel(modes, shifts, alias_shift, mode_shift, spread, mask, tables_high, tables_low, coefficients, alias_inverse, response_high, response_low, corners, table_high, table_low, inverses, columns, scaled, held_high, held_low, sems):
+    core, _, peer = position()
     copies = [
-        pltpu.make_async_copy(tables_high.at[place[0]], held_high, sems.at[0]),
-        pltpu.make_async_copy(tables_low.at[place[0]], held_low, sems.at[1]),
+        pltpu.make_async_copy(tables_high.at[core], held_high, sems.at[0]),
+        pltpu.make_async_copy(tables_low.at[core], held_low, sems.at[1]),
     ]
     for copy in copies:
         copy.start()
     cell, face, screening = columns_of(coefficients)
-    start = place[0] * HALF + place[3]
-    values = [shift_y[start + part * PEERS] for part in range(PARTS)]
-    sublane = lax.rem(lax.broadcasted_iota(jnp.int32, (8 * PARTS, LANES), 0), PARTS)
-    alias = alias_shift[...]
-    for part in range(PARTS):
-        alias = alias + jnp.where(sublane == part, values[part], 0.0)
+    lane = lax.broadcasted_iota(jnp.int32, (PARTS, LANES), 1)
+    values = jnp.sum(jnp.where(lane == peer, shifts[pl.ds(core * PARTS, PARTS), :], 0.0), axis=1, keepdims=True)
+    alias = alias_shift[...] + jnp.concatenate([values] * 8, axis=0)
     lane = lax.broadcasted_iota(jnp.int32, (8, LANES), 1)
     mode = jnp.broadcast_to(mode_shift[...], (8, LANES))
     for part in range(PARTS):
-        mode = mode + jnp.where(lax.div(lane, PLANES) == part, values[part], 0.0)
+        mode = mode + jnp.where(lax.div(lane, PLANES) == part, values[part : part + 1], 0.0)
     shifts = jnp.concatenate([alias, mode], axis=0)
     row = lax.broadcasted_iota(jnp.int32, (8, LANES), 0)
     previous = None
@@ -312,7 +324,7 @@
         copy.wait()
 
 
-def interface_kernel(place, arrived, response_high, response_low, corners, alias_inverse, forward, backward, coefficients, out, source, part, solved):
+def interface_kernel(arrived, response_high, response_low, corners, alias_inverse, forward, backward, coefficients, out, source, part, solved):
     face = columns_of(coefficients)[1]
 
     def rows(chip, slot):
@@ -368,10 +380,11 @@
         out[rows(chip, 3), :] = nothing
 
 
-def second_solve_kernel(place, modes, arrived, shift_y, shift_col, weights, signs, table_high, table_low, slab_high, slab_low, coefficients, kept, sent, part, near, edge, inverse):
-    core, base = place[0], place[1] * LAYERS
-    cell, face, _ = columns_of(coefficients)
-    chip_pivots(place, shift_y, shift_col, coefficients, inverse)
+def second_solve_kernel(modes, arrived, shifts, weights, table_high, table_low, slab_high, slab_low, coefficients, kept, sent, part, near, edge, inverse):
+    core, chip, _ = position()
+    base = chip * LAYERS
+    cell, face, _ = columns_of(coefficients, PARTS)
+    chip_pivots(shifts, coefficients, inverse)
     below = unstack_parts(arrived[pl.ds(0, PEERS, stride=ROWS), :])
     above = unstack_parts(arrived[pl.ds(1, PEERS, stride=ROWS), :])
     turned = arrived[pl.ds(2, PEERS, stride=ROWS), :].T
@@ -379,8 +392,8 @@
         for step in range(PARTS):
             at = (which * PARTS + step) * LAYERS
             target[:, step * LANES : (step + 1) * LANES] = turned[at : at + LAYERS]
-    weight = widen(weights)
-    signed = widen(signs)
+    weight = widen(weights[:PLANES])
+    signed = widen(weights[PLANES:])
     keep = lax.broadcasted_iota(jnp.int32, (PLANES, HALF), 0) == 0
     value = None
     for layer in range(1, LAYERS):
@@ -403,41 +416,51 @@
     sent[...] = to_planes(part[pl.ds((1 - core) * 8, 8)], table_high, table_low, slab_high, slab_low)
 
 
-def backward_kernel(place, modes, table_high, table_low, slab_high, slab_low, out):
+def backward_kernel(modes, table_high, table_low, slab_high, slab_low, out):
     out[...] = to_planes(modes[...], table_high, table_low, slab_high, slab_low)
+
+
+def join_kernel(kept, other, out, lines, sems):
+    core, _, _ = position()
+    sign = jnp.where(core == 0, 1.0, -1.0)
+    copies = []
+    for step in range(4):
+        at = slice(2 * step, 2 * step + 2)
+        one, two = kept[at], other[at]
+        lines[at, :, :HALF] = one + two
+        lines[at, :, HALF:] = sign * (one - two)
+        copies.append(pltpu.make_async_copy(lines.at[pl.ds(2 * step, 2)], out.at[pl.ds(2 * step, 2)], sems.at[step]))
+        copies[-1].start()
+    for copy in copies:
+        copy.wait()
 
 
 held = pl.BlockSpec(memory_space=pltpu.VMEM)
 far = pl.BlockSpec(memory_space=pl.ANY)
-scalars = pl.BlockSpec(memory_space=pltpu.SMEM)
 in_hbm = functools.partial(pltpu.with_memory_space_constraint, memory_space=pltpu.HBM)
 
 
-def call(kernel, place, inputs, in_specs, outs, out_specs, scratch=(), grid=(), cost=10_000_000):
+def call(kernel, inputs, in_specs, outs, out_specs, scratch=(), cost=10_000_000):
     return pl.pallas_call(
         kernel,
-        grid=grid,
-        in_specs=[scalars, *in_specs],
+        in_specs=in_specs,
         out_specs=out_specs,
         out_shape=outs,
         scratch_shapes=scratch,
         compiler_params=pltpu.CompilerParams(vmem_limit_bytes=VMEM_LIMIT),
         cost_estimate=pl.CostEstimate(flops=cost, bytes_accessed=4_000_000, transcendentals=0),
-    )(place, *inputs)
+    )(*inputs)
 
 
 def body(charge, cell, face, screening):
-    gx, gz = lax.axis_index("gx"), lax.axis_index("gz")
-    core, chip = lax.rem(gz, 2), lax.div(gz, 2)
-    place = jnp.stack([core, chip, 1 - core, gx * CHIPS + chip]).astype(jnp.int32)
     forward_y, backward_y = y_tables()
     fy_high, fy_low = split_pair(forward_y)
     by_high, by_low = split_pair(backward_y)
     slab_high, slab_low = split_pair(np.kron(np.eye(8), slab_basis()))
     forward_slab, backward_slab, alias_shift = interface_tables()
     spread, mask = spread_tables()
-    weights = np.broadcast_to(near_weights()[:, None], (PLANES, LANES)).copy()
-    signs = weights * far_signs()[:, None]
+    weights = np.concatenate([near_weights(), near_weights() * far_signs()])
+    weights = np.broadcast_to(weights[:, None], (2 * PLANES, LANES)).copy()
     shift_y = y_shifts()
     mode_shift = np.tile(slab_shifts(), PARTS)[None, :]
 
@@ -458,50 +481,47 @@
 
     pair = [(s, s ^ 1) for s in range(2 * CHIPS)]
     lines = vmem(8, PLANES, NY)
-    own, sent, table_high, table_low = call(
+    coefficient_rows = [in_hbm(array.reshape(1, NZ)) for array in (cell, face, screening)]
+    own, sent, table_high, table_low, coefficients = call(
         split_kernel,
-        place,
-        (in_hbm(charge), in_hbm(fy_high), in_hbm(fy_low)),
-        [far] * 3,
-        [vmem(*cube), vmem(*cube), table, table],
-        [held] * 4,
-        [lines, pltpu.SemaphoreType.DMA((10,))],
+        (in_hbm(charge), in_hbm(fy_high), in_hbm(fy_low), *coefficient_rows),
+        [far] * 6,
+        [vmem(*cube), vmem(*cube), table, table, vmem(3 * NZ, LANES)],
+        [held] * 5,
+        [lines, vmem(3, 1, NZ), pltpu.SemaphoreType.DMA((13,))],
     )
     other = lax.ppermute(sent, "gz", pair)
-    shifts = (shift_y[:, None, :], np.broadcast_to(slab_shifts()[:, None], (PLANES, LANES)).copy())
-    coefficients = jnp.concatenate([cell, face, screening])
+    shifts = np.concatenate([shift_y.reshape(2 * PARTS, LANES), np.broadcast_to(slab_shifts()[:, None], (PLANES, LANES))])
     inverse, own_modes = call(
         early_kernel,
-        place,
-        (own, table_high, table_low, slab_high, slab_low, *shifts, coefficients),
-        [held] * 7 + [scalars],
+        (own, table_high, table_low, slab_high, slab_low, shifts, coefficients),
+        [held] * 7,
         [vmem(*field), vmem(*cube)],
         [held] * 2,
     )
     modes, ends = call(
         forward_kernel,
-        place,
         (own_modes, other, table_high, table_low, slab_high, slab_low, inverse, weights, fold_table(), coefficients),
-        [held] * 9 + [scalars],
-        [pltpu.HBM(field, jnp.float32), pltpu.HBM(message, jnp.float32)],
-        [far, held],
-        [vmem(*field), vmem(*field), vmem(8 * LAYERS, HALF), pltpu.SemaphoreType.DMA((2,))],
-    )
+        [held] * 10,
+        [vmem(*field), pltpu.HBM(message, jnp.float32)],
+        [held] * 2,
+        [vmem(*field), vmem(8 * LAYERS, HALF)],
+    )
+    modes = call(keep_kernel, (modes,), [held], pltpu.HBM(field, jnp.float32), far, [pltpu.SemaphoreType.DMA])
     alias_inverse, response_high, response_low, corners, table_high, table_low = call(
         prepare_kernel,
-        place,
-        (shift_y.reshape(-1), alias_shift, mode_shift, spread, mask, in_hbm(by_high), in_hbm(by_low), coefficients),
-        [scalars] + [held] * 4 + [far] * 2 + [scalars],
-        [vmem(NZ, 8 * PARTS, LANES), pltpu.VMEM(square, jnp.bfloat16), pltpu.VMEM(square, jnp.bfloat16), vmem(CHIPS, 8, LANES), far_table, far_table],
+        (in_hbm(modes), shifts, alias_shift, mode_shift, spread, mask, in_hbm(by_high), in_hbm(by_low), coefficients),
+        [far] + [held] * 5 + [far] * 2 + [held],
+        [vmem(NZ, 8 * PARTS, LANES), pltpu.VMEM(square, jnp.bfloat16), pltpu.VMEM(square, jnp.bfloat16), vmem(CHIPS, 8, LANES)]
+        + [far_table, far_table],
         [held] * 4 + [far] * 2,
         [vmem(NZ, 8, LANES), vmem(NZ, 8, LANES), vmem(8 * NZ, LANES), table, table, pltpu.SemaphoreType.DMA((4,))],
     )
     ends = exchange(ends)
     ends = call(
         interface_kernel,
-        place,
         (ends, response_high, response_low, corners, alias_inverse, forward_slab, backward_slab, coefficients),
-        [held] * 7 + [scalars],
+        [held] * 8,
         vmem(*message),
         held,
         [vmem(CHIPS * PARTS * LAYERS, LANES), vmem(NZ, 8 * PARTS, LANES), vmem(CHIPS * PARTS * LAYERS, LANES)],
@@ -509,17 +529,17 @@
     ends = exchange(ends)
     kept, sent = call(
         second_solve_kernel,
-        place,
-        (modes, ends, *shifts, weights, signs, table_high, table_low, slab_high, slab_low, coefficients),
-        [held] * 10 + [scalars],
+        (modes, ends, shifts, weights, table_high, table_low, slab_high, slab_low, coefficients),
+        [held] * 9,
         [vmem(*cube), vmem(*cube)],
         [held] * 2,
         [vmem(*field), vmem(LAYERS, HALF), vmem(LAYERS, HALF), vmem(*field)],
     )
     other = lax.ppermute(sent, "gz", pair)
-    kept = call(backward_kernel, place, (kept, table_high, table_low, slab_high, slab_low), [held] * 5, vmem(*cube), held)
-    sign = jnp.where(core == 0, 1.0, -1.0)
-    return jnp.concatenate([kept + other, sign * (kept - other)], axis=2)
+    kept = call(backward_kernel, (kept, table_high, table_low, slab_high, slab_low), [held] * 5, vmem(*cube), held)
+    return call(
+        join_kernel, (kept, other), [held] * 2, pltpu.HBM((8, PLANES, NY), jnp.float32), far, [lines, pltpu.SemaphoreType.DMA((4,))]
+    )
 
 
 def solution(mesh):

time: 68.2 us -> 64.8 us (0.950)
  Pallas kernels: 16.4 us -> 14 us
  other arithmetic: 1.36 us -> 0 us
    pallas_call x7 -> x9, Pallas kernels: 16.4 us -> 14 us  [call(): pl.pallas_call(kernel, in_specs=in_specs, out_specs=out_specs, out_shape=...]
    concatenate x2 -> x0, other arithmetic: 1.14 us -> none  [the longest x1 1.06 us: body(): return jnp.concatenate([kept + other, sign * (kept - other)], axis=2)]
    ppermute x2, waiting for transfers between devices: 0.14 us -> 1.08 us  [body(): other = lax.ppermute(sent, 'gz', pair)]
  transfers between devices with their start and end apart: 3 -> 3, of which waited for: 2 -> 3; matrix products, arithmetic and copies ran while one was open for 0% -> 0% of each run, Pallas kernels for 9% -> 8%
where the time goes in v5:
time: 64.8 us; the launch traced here: 64.6 us
  starting transfers between devices  20.9 us (32%)
  blocking collectives  18.8 us (29%)
  Pallas kernels  14 us (22%)
  waiting for transfers between devices  10.6 us (16%)
    all_to_all x1, blocking collectives, exchange(): lax.all_to_all(blocks, ('gx', 'gz'), 0, 0, axis_index_groups=groups, tile...  18.8 us
    pallas_call x9, Pallas kernels, call(): pl.pallas_call(kernel, in_specs=in_specs, out_specs=out_specs, out_shape=...  14 us
    all_to_all x1, starting transfers between devices, exchange(): lax.all_to_all(blocks, ('gx', 'gz'), 0, 0, axis_index_groups=groups, tile...  13.8 us
    all_to_all x1, waiting for transfers between devices, exchange(): lax.all_to_all(blocks, ('gx', 'gz'), 0, 0, axis_index_groups=groups, tile...  9.53 us
    ppermute x2, starting transfers between devices, body(): other = lax.ppermute(sent, 'gz', pair)  7.07 us
  transfers between devices with their start and end apart: 3, of which 3 were waited for; matrix products, arithmetic and copies ran while one was open for 0% of the time, Pallas kernels for 8%

profile of v5, /device:TPU:1, one launch (start us, length us, event | category | flops | bytes accessed | tf_op | source)
XLA Modules:
  0.0 64.6 jit_solution(11238400843024964968)
XLA Ops:
  0.0 0.0 copy-start.3
  0.0 0.0 copy-start.4
  0.0 0.0 copy-start.5
  0.0 1.8 %shard_map.181 = (f32[8,32,512]{2,1,0:T(8,128)S(1)}, f32[8,32,512]{2,1,0:T(8,128)S(1)}, bf16[512,512]{1,0:T(8,128)(2,1)S(1)}, bf16[512,512]{1,0:T(8,128)(2,1)S(1)}, f32[192,128]{1,0:T(8,128)S(1)}) custom-call(f32[8,32,1024]{2,1,0:T(8,128)} %charge.1, bf16[2,512,512]{2,1,0:T(8,128)(2,1)} %constant.30.clone.tables_high, ...), custom_call_target="tpu_custom_call" | custom-call | flops 10000000 | bytes 4000000 | tf_op jit(solution)/shard_map/pallas_call | solution.py:444
  1.8 3.3 %collective-permute-start = (f32[8,32,512]{2,1,0:T(8,128)S(1)}, f32[8,32,512]{2,1,0:T(8,128)S(1)}, u32[]{:S(2)}, u32[]{:S(2)}) collective-permute-start(f32[8,32,512]{2,1,0:T(8,128)S(1)} %get-tuple-element.27), channel_id=1, source_target_pairs={{0,1},{1,0},{2,3},{3,2},{4,5},{5,4},{6,7},{7,6},{8,9},{9,8},{10,11... | collective-permute-start | bytes 1572872 | tf_op jit(solution)/shard_map/ppermute | solution.py:493
  5.2 0.0 copy-done.3
  5.2 0.0 copy-done.4
  5.2 0.0 copy-done.5
  5.2 0.0 copy-start.6
  5.2 0.0 copy-start.12
  5.2 1.1 %shard_map.182 = (f32[16,32,512]{2,1,0:T(8,128)S(1)}, f32[8,32,512]{2,1,0:T(8,128)S(1)}) custom-call(f32[8,32,512]{2,1,0:T(8,128)S(1)} %get-tuple-element.22.own, bf16[512,512]{1,0:T(8,128)(2,1)S(1)} %get-tuple-element.23.table_high, bf16[512,512]{1,0:T(8,128)(2,1)S(1)} %get-tuple-element.24.table_low, bf16[256,256]{1,0:T(8,128)(2,1)S(1)} %copy-done.4, ...), custom_call_target="tpu_custom_call" | custom-call | flops 10000000 | bytes 4000000 | tf_op jit(solution)/shard_map/pallas_call | solution.py:444
  6.3 0.4 collective-permute-done.other
  6.7 0.0 copy-done.6
  6.7 0.0 copy-done.12
  6.7 2.3 %shard_map.183 = (f32[16,32,512]{2,1,0:T(8,128)S(1)}, f32[512,128]{1,0:T(8,128)}) custom-call(f32[8,32,512]{2,1,0:T(8,128)S(1)} %get-tuple-element.26.own_modes, f32[8,32,512]{2,1,0:T(8,128)S(1)} %collective-permute-done.other, bf16[512,512]{1,0:T(8,128)(2,1)S(1)} %get-tuple-element.23.table_high, bf16[512,512]{1,0:T(8,128)(2,1)S(1)} %get-tuple-element.24.table_low, ...), custom_call_target="tpu_custom_call" | custom-call | flops 10000000 | bytes 4000000 | tf_op jit(solution)/shard_map/pallas_call | solution.py:444
  9.0 13.8 %all-to-all-start = ((f32[128,4,128]{2,1,0:T(4,128)}), f32[128,4,128]{2,1,0:T(4,128)S(1)}, u32[]{:S(2)}, u32[]{:S(2)}) async-start(f32[128,4,128]{2,1,0:T(4,128)} %bitcast.10), calls=%async_computation | async-start | bytes 524288 | tf_op jit(solution)/shard_map/all_to_all | solution.py:480
  22.8 0.0 copy-start.7
  22.8 0.0 copy-start.8
  22.9 0.0 copy-start.11
  22.9 0.0 copy-start.13
  22.9 1.0 %shard_map.184.modes = f32[16,32,512]{2,1,0:T(8,128)} custom-call(f32[16,32,512]{2,1,0:T(8,128)S(1)} %get-tuple-element.29.modes), custom_call_target="tpu_custom_call" | custom-call | flops 10000000 | bytes 4000000 | tf_op jit(solution)/shard_map/pallas_call | solution.py:444
  23.9 0.0 copy-done.7
  23.9 0.0 copy-done.8
  23.9 0.0 copy-done.11
  23.9 0.0 copy-done.13
  23.9 0.0 copy-start.9
  23.9 0.0 copy-start.10
  23.9 2.3 %shard_map.185 = (f32[64,32,128]{2,1,0:T(8,128)S(1)}, bf16[512,512]{1,0:T(8,128)(2,1)S(1)}, bf16[512,512]{1,0:T(8,128)(2,1)S(1)}, f32[4,8,128]{2,1,0:T(8,128)S(1...) custom-call(f32[16,32,512]{2,1,0:T(8,128)} %shard_map.184.modes, f32[40,128]{1,0:T(8,128)S(1)} %copy-done.5, ...), custom_call_target="tpu_custom_call" | custom-call | flops 10000000 | bytes 4000000 | tf_op jit(solution)/shard_map/pallas_call | solution.py:444
  26.2 9.5 %all-to-all-done = f32[128,4,128]{2,1,0:T(4,128)S(1)} async-done(((f32[128,4,128]{2,1,0:T(4,128)}), f32[128,4,128]{2,1,0:T(4,128)S(1)}, u32[]{:S(2)}, u32[]{:S(2)}) %all-to-all-start) | async-done | bytes 262176 | tf_op jit(solution)/shard_map/all_to_all | solution.py:480
  35.8 0.0 copy-done.9
  35.8 0.0 copy-done.10
  35.8 0.0 copy-start
  35.8 0.0 copy-start.2
  35.8 1.9 %shard_map.186 = f32[512,128]{1,0:T(8,128)S(1)} custom-call(f32[512,128]{1,0:T(8,128)S(1)} %bitcast.7, bf16[512,512]{1,0:T(8,128)(2,1)S(1)} %get-tuple-element.31.response_high, bf16[512,512]{1,0:T(8,128)(2,1)S(1)} %get-tuple-element.32.response_low, f32[4,8,128]{2,1,0:T(8,128)S(1)} %get-tuple-element.33.corners, ...), custom_call_target="tpu_custom_call" | custom-call | flops 10000000 | bytes 4000000 | tf_op jit(solution)/shard_map/pallas_call | solution.py:444
  37.7 0.0 copy-start.1
  37.7 18.8 %all_to_all.10 = f32[128,4,128]{2,1,0:T(4,128)S(1)} all-to-all(f32[128,4,128]{2,1,0:T(4,128)S(1)} %bitcast.9), channel_id=1, replica_groups={{0,2,4,6,8,10,12,14,16,18,20,22,24,26,28,30,32,34,36,38,40,42,44,46,48,..., dimensions={0} | all-to-all | bytes 524288 | tf_op jit(solution)/shard_map/all_to_all | solution.py:480
  56.6 0.0 copy-done
  56.6 0.0 copy-done.2
  56.6 0.0 copy-done.1
  56.6 1.7 %shard_map.187 = (f32[8,32,512]{2,1,0:T(8,128)S(1)}, f32[8,32,512]{2,1,0:T(8,128)S(1)}) custom-call(f32[16,32,512]{2,1,0:T(8,128)S(1)} %copy-done, f32[512,128]{1,0:T(8,128)S(1)} %bitcast.8, f32[40,128]{1,0:T(8,128)S(1)} %copy-done.5, f32[64,128]{1,0:T(8,128)S(1)} %copy-done.6, bf16[512,512]{1,0:T(8,128)(2,1)S(1)} %copy-done.1, ...), custom_call_target="tpu_custom_call" | custom-call | flops 10000000 | bytes 4000000 | tf_op jit(solution)/shard_map/pallas_call | solution.py:444
  58.3 3.8 %collective-permute-start.1 = (f32[8,32,512]{2,1,0:T(8,128)S(1)}, f32[8,32,512]{2,1,0:T(8,128)S(1)}, u32[]{:S(2)}, u32[]{:S(2)}) collective-permute-start(f32[8,32,512]{2,1,0:T(8,128)S(1)} %get-tuple-element.38), channel_id=1, source_target_pairs={{0,1},{1,0},{2,3},{3,2},{4,5},{5,4},{6,7},{7,6},{8,9},{9,8},{10,11... | collective-permute-start | bytes 1572872 | tf_op jit(solution)/shard_map/ppermute | solution.py:538
  62.0 0.9 %shard_map.188.kept = f32[8,32,512]{2,1,0:T(8,128)S(1)} custom-call(f32[8,32,512]{2,1,0:T(8,128)S(1)} %get-tuple-element.37.modes, bf16[512,512]{1,0:T(8,128)(2,1)S(1)} %copy-done.1, bf16[512,512]{1,0:T(8,128)(2,1)S(1)} %copy-done.2, bf16[256,256]{1,0:T(8,128)(2,1)S(1)} %copy-done.4, bf16[256,256]{1,0:T(8,128)(2,1)S(1)} %copy-done.3), custom_call_target="tpu_custom_call" | custom-call | flops 10000000 | bytes 4000000 | tf_op jit(solution)/shard_map/pallas_call | solution.py:444
  62.9 0.7 %collective-permute-done.1.other = f32[8,32,512]{2,1,0:T(8,128)S(1)} collective-permute-done((f32[8,32,512]{2,1,0:T(8,128)S(1)}, f32[8,32,512]{2,1,0:T(8,128)S(1)}, u32[]{:S(2)}, u32[]{:S(2)}) %collective-permute-start.1) | collective-permute-done | bytes 524320 | tf_op jit(solution)/shard_map/ppermute | solution.py:538
  63.6 1.0 %shard_map.189 = f32[8,32,1024]{2,1,0:T(8,128)} custom-call(f32[8,32,512]{2,1,0:T(8,128)S(1)} %shard_map.188.kept, f32[8,32,512]{2,1,0:T(8,128)S(1)} %collective-permute-done.1.other), custom_call_target="tpu_custom_call" | custom-call | flops 10000000 | bytes 4000000 | tf_op jit(solution)/shard_map/pallas_call | solution.py:444
Async XLA Ops:
  0.0 5.2 %copy-start.3 = (bf16[256,256]{1,0:T(8,128)(2,1)S(1)}, bf16[256,256]{1,0:T(8,128)(2,1)}, u32[]{:S(2)}) copy-start(bf16[256,256]{1,0:T(8,128)(2,1)} %constant.33.clone.slab_low) | copy-start | bytes 393220
  0.0 5.2 %copy-start.4 = (bf16[256,256]{1,0:T(8,128)(2,1)S(1)}, bf16[256,256]{1,0:T(8,128)(2,1)}, u32[]{:S(2)}) copy-start(bf16[256,256]{1,0:T(8,128)(2,1)} %constant.32.clone.slab_high) | copy-start | bytes 393220
  0.0 5.2 %copy-start.5 = (f32[40,128]{1,0:T(8,128)S(1)}, f32[40,128]{1,0:T(8,128)}, u32[]{:S(2)}) copy-start(f32[40,128]{1,0:T(8,128)} %constant.34.clone.shifts) | copy-start | bytes 61444
  1.8 4.9 %collective-permute-start = (f32[8,32,512]{2,1,0:T(8,128)S(1)}, f32[8,32,512]{2,1,0:T(8,128)S(1)}, u32[]{:S(2)}, u32[]{:S(2)}) collective-permute-start(f32[8,32,512]{2,1,0:T(8,128)S(1)} %get-tuple-element.27), channel_id=1, source_target_pairs={{0,1},{1,0},{2,3},{3,2},{4,5},{5,4},{6,7},{7,6},{8,9},{9,8},{10,11... | collective-permute-start | bytes 1572872 | tf_op jit(solution)/shard_map/ppermute | solution.py:493
  5.2 1.5 %copy-start.6 = (f32[64,128]{1,0:T(8,128)S(1)}, f32[64,128]{1,0:T(8,128)}, u32[]{:S(2)}) copy-start(f32[64,128]{1,0:T(8,128)} %constant.35.clone.weights) | copy-start | bytes 98308
  5.2 1.5 %copy-start.12 = (bf16[32,128]{1,0:T(8,128)(2,1)S(1)}, bf16[32,128]{1,0:T(8,128)(2,1)}, u32[]{:S(2)}) copy-start(bf16[32,128]{1,0:T(8,128)(2,1)} %constant.36.clone.fold) | copy-start | bytes 24580
  9.0 26.7 %all-to-all-start = ((f32[128,4,128]{2,1,0:T(4,128)}), f32[128,4,128]{2,1,0:T(4,128)S(1)}, u32[]{:S(2)}, u32[]{:S(2)}) async-start(f32[128,4,128]{2,1,0:T(4,128)} %bitcast.10), calls=%async_computation | async-start | bytes 524288 | tf_op jit(solution)/shard_map/all_to_all | solution.py:480
  22.8 1.0 %copy-start.7 = (f32[64,512]{1,0:T(8,128)S(1)}, f32[64,512]{1,0:T(8,128)}, u32[]{:S(2)}) copy-start(f32[64,512]{1,0:T(8,128)} %constant.41.clone.spread) | copy-start | bytes 393220
  22.8 1.0 %copy-start.8 = (f32[128,128]{1,0:T(8,128)S(1)}, f32[128,128]{1,0:T(8,128)}, u32[]{:S(2)}) copy-start(f32[128,128]{1,0:T(8,128)} %constant.42.clone.mask) | copy-start | bytes 196612
  22.9 1.0 %copy-start.11 = (f32[32,128]{1,0:T(8,128)S(1)}, f32[32,128]{1,0:T(8,128)}, u32[]{:S(2)}) copy-start(f32[32,128]{1,0:T(8,128)} %constant.39.clone.alias_shift) | copy-start | bytes 49156
  22.9 1.0 %copy-start.13 = (f32[1,128]{1,0:T(1,128)S(1)}, f32[1,128]{1,0:T(1,128)}, u32[]{:S(2)}) copy-start(f32[1,128]{1,0:T(1,128)} %constant.40.clone.mode_shift) | copy-start | bytes 1540
  23.9 11.9 %copy-start.9 = (bf16[96,256]{1,0:T(8,128)(2,1)S(1)}, bf16[96,256]{1,0:T(8,128)(2,1)}, u32[]{:S(2)}) copy-start(bf16[96,256]{1,0:T(8,128)(2,1)} %constant.43.clone.forward) | copy-start | bytes 147460
  23.9 11.9 %copy-start.10 = (f32[64,128]{1,0:T(8,128)S(1)}, f32[64,128]{1,0:T(8,128)}, u32[]{:S(2)}) copy-start(f32[64,128]{1,0:T(8,128)} %constant.44.clone.backward) | copy-start | bytes 98308
  35.8 20.8 %copy-start = (f32[16,32,512]{2,1,0:T(8,128)S(1)}, f32[16,32,512]{2,1,0:T(8,128)}, u32[]{:S(2)}) copy-start(f32[16,32,512]{2,1,0:T(8,128)} %shard_map.184.modes) | copy-start | bytes 3145732
  35.8 20.8 %copy-start.2 = (bf16[512,512]{1,0:T(8,128)(2,1)S(1)}, bf16[512,512]{1,0:T(8,128)(2,1)}, u32[]{:S(2)}) copy-start(bf16[512,512]{1,0:T(8,128)(2,1)} %get-tuple-element.36.table_low) | copy-start | bytes 1572868
  37.7 18.8 %copy-start.1 = (bf16[512,512]{1,0:T(8,128)(2,1)S(1)}, bf16[512,512]{1,0:T(8,128)(2,1)}, u32[]{:S(2)}) copy-start(bf16[512,512]{1,0:T(8,128)(2,1)} %get-tuple-element.35.table_high) | copy-start | bytes 1572868
  58.3 5.3 %collective-permute-start.1 = (f32[8,32,512]{2,1,0:T(8,128)S(1)}, f32[8,32,512]{2,1,0:T(8,128)S(1)}, u32[]{:S(2)}, u32[]{:S(2)}) collective-permute-start(f32[8,32,512]{2,1,0:T(8,128)S(1)} %get-tuple-element.38), channel_id=1, source_target_pairs={{0,1},{1,0},{2,3},{3,2},{4,5},{5,4},{6,7},{7,6},{8,9},{9,8},{10,11... | collective-permute-start | bytes 1572872 | tf_op jit(solution)/shard_map/ppermute | solution.py:538

commit v6 on v5

--- a/solution.py
+++ b/solution.py
@@ -160,12 +160,11 @@
     )
 
 
-def split_kernel(charge, tables_high, tables_low, cell, face, screening, own, sent, table_high, table_low, coefficients, lines, rows, sems):
+def split_kernel(charge, tables_high, cell, face, screening, own, sent, table_high, coefficients, lines, rows, sems):
     core, _, _ = position()
-    copies = [pltpu.make_async_copy(source, rows.at[step], sems.at[10 + step]) for step, source in enumerate((cell, face, screening))]
+    copies = [pltpu.make_async_copy(source, rows.at[step], sems.at[9 + step]) for step, source in enumerate((cell, face, screening))]
     copies += [pltpu.make_async_copy(charge.at[step], lines.at[step], sems.at[step]) for step in range(8)]
     copies.append(pltpu.make_async_copy(tables_high.at[core], table_high, sems.at[8]))
-    copies.append(pltpu.make_async_copy(tables_low.at[core], table_low, sems.at[9]))
     for copy in copies:
         copy.start()
     for step, copy in enumerate(copies[:3]):
@@ -201,9 +200,17 @@
         inverse[layer] = previous
 
 
-def early_kernel(own, table_high, table_low, slab_high, slab_low, shifts, coefficients, inverse, modes):
+def early_kernel(own, table_high, tables_low, slab_high, slab_low, shifts, coefficients, inverse, modes, table_low, sem):
+    core, _, _ = position()
+    copy = pltpu.make_async_copy(tables_low.at[core], table_low, sem)
+    copy.start()
     chip_pivots(shifts, coefficients, inverse)
-    modes[...] = to_modes(own, table_high, table_low, slab_high, slab_low)
+    high, low = split_values(own[...].reshape(8 * PLANES, HALF))
+    dot = functools.partial(jnp.dot, preferred_element_type=jnp.float32)
+    spectrum = dot(high, table_high[...]) + dot(low, table_high[...])
+    copy.wait()
+    spectrum = spectrum + dot(high, table_low[...])
+    modes[...] = dot_split((slab_high[...], slab_low[...]), split_values(spectrum)).reshape(8, PLANES, HALF)
 
 
 def to_modes(planes, table_high, table_low, slab_high, slab_low):
@@ -380,7 +387,7 @@
         out[rows(chip, 3), :] = nothing
 
 
-def second_solve_kernel(modes, arrived, shifts, weights, table_high, table_low, slab_high, slab_low, coefficients, kept, sent, part, near, edge, inverse):
+def second_solve_kernel(modes, arrived, shifts, weights, table_high, table_low, slab_high, slab_low, coefficients, kept, sent_first, sent_last, part, near, edge, inverse):
     core, chip, _ = position()
     base = chip * LAYERS
     cell, face, _ = columns_of(coefficients, PARTS)
@@ -413,40 +420,50 @@
         part[layer] = jnp.where(keep, near[layer : layer + 1, :], value)
     part[0] = jnp.where(keep, near[0:1, :], below)
     kept[...] = part[pl.ds(core * 8, 8)]
-    sent[...] = to_planes(part[pl.ds((1 - core) * 8, 8)], table_high, table_low, slab_high, slab_low)
+    planes = to_planes(part[pl.ds((1 - core) * 8, 8)], table_high, table_low, slab_high, slab_low)
+    sent_first[...] = planes[:4]
+    sent_last[...] = planes[4:]
 
 
 def backward_kernel(modes, table_high, table_low, slab_high, slab_low, out):
     out[...] = to_planes(modes[...], table_high, table_low, slab_high, slab_low)
 
 
-def join_kernel(kept, other, out, lines, sems):
+def join_layers(first, kept, other, out, lines, sems):
     core, _, _ = position()
     sign = jnp.where(core == 0, 1.0, -1.0)
     copies = []
     for step in range(4):
-        at = slice(2 * step, 2 * step + 2)
-        one, two = kept[at], other[at]
-        lines[at, :, :HALF] = one + two
-        lines[at, :, HALF:] = sign * (one - two)
-        copies.append(pltpu.make_async_copy(lines.at[pl.ds(2 * step, 2)], out.at[pl.ds(2 * step, 2)], sems.at[step]))
+        one, two = kept[first + step], other[step]
+        lines[step, :, :HALF] = one + two
+        lines[step, :, HALF:] = sign * (one - two)
+        copies.append(pltpu.make_async_copy(lines.at[step], out.at[first + step], sems.at[step]))
         copies[-1].start()
     for copy in copies:
         copy.wait()
 
 
+def join_first_kernel(kept, other, out, lines, sems):
+    join_layers(0, kept, other, out, lines, sems)
+
+
+def join_last_kernel(kept, other, begun, out, lines, sems):
+    join_layers(4, kept, other, out, lines, sems)
+
+
 held = pl.BlockSpec(memory_space=pltpu.VMEM)
 far = pl.BlockSpec(memory_space=pl.ANY)
 in_hbm = functools.partial(pltpu.with_memory_space_constraint, memory_space=pltpu.HBM)
 
 
-def call(kernel, inputs, in_specs, outs, out_specs, scratch=(), cost=10_000_000):
+def call(kernel, inputs, in_specs, outs, out_specs, scratch=(), cost=10_000_000, aliases={}):
     return pl.pallas_call(
         kernel,
         in_specs=in_specs,
         out_specs=out_specs,
         out_shape=outs,
         scratch_shapes=scratch,
+        input_output_aliases=aliases,
         compiler_params=pltpu.CompilerParams(vmem_limit_bytes=VMEM_LIMIT),
         cost_estimate=pl.CostEstimate(flops=cost, bytes_accessed=4_000_000, transcendentals=0),
     )(*inputs)
@@ -482,22 +499,23 @@
     pair = [(s, s ^ 1) for s in range(2 * CHIPS)]
     lines = vmem(8, PLANES, NY)
     coefficient_rows = [in_hbm(array.reshape(1, NZ)) for array in (cell, face, screening)]
-    own, sent, table_high, table_low, coefficients = call(
+    own, sent, table_high, coefficients = call(
         split_kernel,
-        (in_hbm(charge), in_hbm(fy_high), in_hbm(fy_low), *coefficient_rows),
-        [far] * 6,
-        [vmem(*cube), vmem(*cube), table, table, vmem(3 * NZ, LANES)],
-        [held] * 5,
-        [lines, vmem(3, 1, NZ), pltpu.SemaphoreType.DMA((13,))],
+        (in_hbm(charge), in_hbm(fy_high), *coefficient_rows),
+        [far] * 5,
+        [vmem(*cube), vmem(*cube), table, vmem(3 * NZ, LANES)],
+        [held] * 4,
+        [lines, vmem(3, 1, NZ), pltpu.SemaphoreType.DMA((12,))],
     )
     other = lax.ppermute(sent, "gz", pair)
     shifts = np.concatenate([shift_y.reshape(2 * PARTS, LANES), np.broadcast_to(slab_shifts()[:, None], (PLANES, LANES))])
-    inverse, own_modes = call(
+    inverse, own_modes, table_low = call(
         early_kernel,
-        (own, table_high, table_low, slab_high, slab_low, shifts, coefficients),
-        [held] * 7,
-        [vmem(*field), vmem(*cube)],
-        [held] * 2,
+        (own, table_high, in_hbm(fy_low), slab_high, slab_low, shifts, coefficients),
+        [held] * 2 + [far] + [held] * 4,
+        [vmem(*field), vmem(*cube), table],
+        [held] * 3,
+        [pltpu.SemaphoreType.DMA],
     )
     modes, ends = call(
         forward_kernel,
@@ -527,19 +545,21 @@
         [vmem(CHIPS * PARTS * LAYERS, LANES), vmem(NZ, 8 * PARTS, LANES), vmem(CHIPS * PARTS * LAYERS, LANES)],
     )
     ends = exchange(ends)
-    kept, sent = call(
+    kept, sent_first, sent_last = call(
         second_solve_kernel,
         (modes, ends, shifts, weights, table_high, table_low, slab_high, slab_low, coefficients),
         [held] * 9,
-        [vmem(*cube), vmem(*cube)],
-        [held] * 2,
+        [vmem(*cube), vmem(4, PLANES, HALF), vmem(4, PLANES, HALF)],
+        [held] * 3,
         [vmem(*field), vmem(LAYERS, HALF), vmem(LAYERS, HALF), vmem(*field)],
     )
-    other = lax.ppermute(sent, "gz", pair)
+    other_first = lax.ppermute(sent_first, "gz", pair)
+    other_last = lax.ppermute(sent_last, "gz", pair)
     kept = call(backward_kernel, (kept, table_high, table_low, slab_high, slab_low), [held] * 5, vmem(*cube), held)
-    return call(
-        join_kernel, (kept, other), [held] * 2, pltpu.HBM((8, PLANES, NY), jnp.float32), far, [lines, pltpu.SemaphoreType.DMA((4,))]
-    )
+    scratch = [vmem(4, PLANES, NY), pltpu.SemaphoreType.DMA((4,))]
+    out = pltpu.HBM((8, PLANES, NY), jnp.float32)
+    begun = call(join_first_kernel, (kept, other_first), [held] * 2, out, far, scratch)
+    return call(join_last_kernel, (kept, other_last, in_hbm(begun)), [held] * 2 + [far], out, far, scratch, aliases={2: 0})
 
 
 def solution(mesh):

time: 64.8 us -> 65.4 us (level)
  Pallas kernels: 14 us -> 15.3 us
    ppermute x2 -> x1, starting transfers between devices: 7.07 us -> 3.32 us  [body(): other = lax.ppermute(sent, 'gz', pair)]
    ppermute x0 -> x2, starting transfers between devices: none -> 3.74 us  [the longest x1 3.64 us: body(): other_first = lax.ppermute(sent_first, 'gz', pair)]
    pallas_call x9 -> x10, Pallas kernels: 14 us -> 15.3 us  [call(): pl.pallas_call(kernel, in_specs=in_specs, out_specs=out_specs, out_shape=...]
    ppermute x2 -> x1, waiting for transfers between devices: 1.08 us -> 0.01 us  [body(): other = lax.ppermute(sent, 'gz', pair)]
  transfers between devices with their start and end apart: 3 -> 4, of which waited for: 3 -> 2; matrix products, arithmetic and copies ran while one was open for 0% -> 0% of each run, Pallas kernels for 8% -> 11%
where the time goes in v6:
time: 65.4 us; the launch traced here: 65.1 us
  starting transfers between devices  20.8 us (32%)
  blocking collectives  18.5 us (28%)
  Pallas kernels  15.3 us (23%)
  waiting for transfers between devices  10.2 us (16%)
    all_to_all x1, blocking collectives, exchange(): lax.all_to_all(blocks, ('gx', 'gz'), 0, 0, axis_index_groups=groups, tile...  18.5 us
    pallas_call x10, Pallas kernels, call(): pl.pallas_call(kernel, in_specs=in_specs, out_specs=out_specs, out_shape=...  15.3 us
    all_to_all x1, starting transfers between devices, exchange(): lax.all_to_all(blocks, ('gx', 'gz'), 0, 0, axis_index_groups=groups, tile...  13.8 us
    all_to_all x1, waiting for transfers between devices, exchange(): lax.all_to_all(blocks, ('gx', 'gz'), 0, 0, axis_index_groups=groups, tile...  9.98 us
    ppermute x1, starting transfers between devices, body(): other_first = lax.ppermute(sent_first, 'gz', pair)  3.64 us
    ppermute x1, starting transfers between devices, body(): other = lax.ppermute(sent, 'gz', pair)  3.32 us
  transfers between devices with their start and end apart: 4, of which 2 were waited for; matrix products, arithmetic and copies ran while one was open for 0% of the time, Pallas kernels for 11%

profile of v6, /device:TPU:1, one launch (start us, length us, event | category | flops | bytes accessed | tf_op | source)
XLA Modules:
  0.0 65.1 jit_solution(1907931565286024238)
XLA Ops:
  0.0 0.0 copy-start.1
  0.0 0.0 copy-start.2
  0.0 0.0 copy-start.5
  0.0 1.6 %shard_map.181 = (f32[8,32,512]{2,1,0:T(8,128)S(1)}, f32[8,32,512]{2,1,0:T(8,128)S(1)}, bf16[512,512]{1,0:T(8,128)(2,1)S(1)}, f32[192,128]{1,0:T(8,128)S(1)}) custom-call(f32[8,32,1024]{2,1,0:T(8,128)} %charge.1, bf16[2,512,512]{2,1,0:T(8,128)(2,1)} %constant.30.clone.tables_high, f32[1,64]{1,0:T(1,128)} %bitcast.11, f32[1,64]{1,0:T(1,128)} %bitcast.12, ...), custom_call_target="tpu_custom_call" | custom-call | flops 10000000 | bytes 4000000 | tf_op jit(solution)/shard_map/pallas_call | solution.py:460
  1.7 3.3 %collective-permute-start = (f32[8,32,512]{2,1,0:T(8,128)S(1)}, f32[8,32,512]{2,1,0:T(8,128)S(1)}, u32[]{:S(2)}, u32[]{:S(2)}) collective-permute-start(f32[8,32,512]{2,1,0:T(8,128)S(1)} %get-tuple-element.27), channel_id=1, source_target_pairs={{0,1},{1,0},{2,3},{3,2},{4,5},{5,4},{6,7},{7,6},{8,9},{9,8},{10,11... | collective-permute-start | bytes 1572872 | tf_op jit(solution)/shard_map/ppermute | solution.py:510
  5.0 0.0 copy-done.1
  5.0 0.0 copy-done.2
  5.0 0.0 copy-done.5
  5.0 0.0 copy-start.6
  5.0 0.0 copy-start.12
  5.0 2.0 %shard_map.182 = (f32[16,32,512]{2,1,0:T(8,128)S(1)}, f32[8,32,512]{2,1,0:T(8,128)S(1)}, bf16[512,512]{1,0:T(8,128)(2,1)S(1)}) custom-call(f32[8,32,512]{2,1,0:T(8,128)S(1)} %get-tuple-element.23.own, bf16[512,512]{1,0:T(8,128)(2,1)S(1)} %get-tuple-element.24.table_high, bf16[2,512,512]{2,1,0:T(8,128)(2,1)} %constant.31.clone.tables_low, ...), custom_call_target="tpu_custom_call" | custom-call | flops 10000000 | bytes 4000000 | tf_op jit(solution)/shard_map/pallas_call | solution.py:460
  7.0 0.0 collective-permute-done.other
  7.0 0.0 copy-done.6
  7.0 0.0 copy-done.12
  7.0 2.3 %shard_map.183 = (f32[16,32,512]{2,1,0:T(8,128)S(1)}, f32[512,128]{1,0:T(8,128)}) custom-call(f32[8,32,512]{2,1,0:T(8,128)S(1)} %get-tuple-element.26.own_modes, f32[8,32,512]{2,1,0:T(8,128)S(1)} %collective-permute-done.other, bf16[512,512]{1,0:T(8,128)(2,1)S(1)} %get-tuple-element.24.table_high, bf16[512,512]{1,0:T(8,128)(2,1)S(1)} %get-tuple-element.28.table_low, ...), custom_call_target="tpu_custom_call" | custom-call | flops 10000000 | bytes 4000000 | tf_op jit(solution)/shard_map/pallas_call | solution.py:460
  9.3 13.8 %all-to-all-start = ((f32[128,4,128]{2,1,0:T(4,128)}), f32[128,4,128]{2,1,0:T(4,128)S(1)}, u32[]{:S(2)}, u32[]{:S(2)}) async-start(f32[128,4,128]{2,1,0:T(4,128)} %bitcast.10), calls=%async_computation | async-start | bytes 524288 | tf_op jit(solution)/shard_map/all_to_all | solution.py:497
  23.1 0.0 copy-start.7
  23.1 0.0 copy-start.8
  23.1 0.0 copy-start.11
  23.1 0.0 copy-start.13
  23.1 1.0 %shard_map.184.modes = f32[16,32,512]{2,1,0:T(8,128)} custom-call(f32[16,32,512]{2,1,0:T(8,128)S(1)} %get-tuple-element.30.modes), custom_call_target="tpu_custom_call" | custom-call | flops 10000000 | bytes 4000000 | tf_op jit(solution)/shard_map/pallas_call | solution.py:460
  24.1 0.0 copy-done.7
  24.1 0.0 copy-done.8
  24.2 0.0 copy-done.11
  24.2 0.0 copy-done.13
  24.2 0.0 copy-start.9
  24.2 0.0 copy-start.10
  24.2 2.3 %shard_map.185 = (f32[64,32,128]{2,1,0:T(8,128)S(1)}, bf16[512,512]{1,0:T(8,128)(2,1)S(1)}, bf16[512,512]{1,0:T(8,128)(2,1)S(1)}, f32[4,8,128]{2,1,0:T(8,128)S(1...) custom-call(f32[16,32,512]{2,1,0:T(8,128)} %shard_map.184.modes, f32[40,128]{1,0:T(8,128)S(1)} %copy-done.5, ...), custom_call_target="tpu_custom_call" | custom-call | flops 10000000 | bytes 4000000 | tf_op jit(solution)/shard_map/pallas_call | solution.py:460
  26.5 10.0 %all-to-all-done = f32[128,4,128]{2,1,0:T(4,128)S(1)} async-done(((f32[128,4,128]{2,1,0:T(4,128)}), f32[128,4,128]{2,1,0:T(4,128)S(1)}, u32[]{:S(2)}, u32[]{:S(2)}) %all-to-all-start) | async-done | bytes 262176 | tf_op jit(solution)/shard_map/all_to_all | solution.py:497
  36.5 0.0 copy-done.9
  36.5 0.0 copy-done.10
  36.5 0.0 copy-start
  36.5 0.0 copy-start.4
  36.5 1.9 %shard_map.186 = f32[512,128]{1,0:T(8,128)S(1)} custom-call(f32[512,128]{1,0:T(8,128)S(1)} %bitcast.7, bf16[512,512]{1,0:T(8,128)(2,1)S(1)} %get-tuple-element.32.response_high, bf16[512,512]{1,0:T(8,128)(2,1)S(1)} %get-tuple-element.33.response_low, f32[4,8,128]{2,1,0:T(8,128)S(1)} %get-tuple-element.34.corners, ...), custom_call_target="tpu_custom_call" | custom-call | flops 10000000 | bytes 4000000 | tf_op jit(solution)/shard_map/pallas_call | solution.py:460
  38.4 0.0 copy-start.3
  38.5 18.5 %all_to_all.10 = f32[128,4,128]{2,1,0:T(4,128)S(1)} all-to-all(f32[128,4,128]{2,1,0:T(4,128)S(1)} %bitcast.9), channel_id=1, replica_groups={{0,2,4,6,8,10,12,14,16,18,20,22,24,26,28,30,32,34,36,38,40,42,44,46,48,..., dimensions={0} | all-to-all | bytes 524288 | tf_op jit(solution)/shard_map/all_to_all | solution.py:497
  57.0 0.0 copy-done
  57.0 0.0 copy-done.4
  57.0 0.0 copy-done.3
  57.0 1.6 %shard_map.187 = (f32[8,32,512]{2,1,0:T(8,128)S(1)}, f32[4,32,512]{2,1,0:T(8,128)S(1)}, f32[4,32,512]{2,1,0:T(8,128)S(1)}) custom-call(f32[16,32,512]{2,1,0:T(8,128)S(1)} %copy-done, f32[512,128]{1,0:T(8,128)S(1)} %bitcast.8, f32[40,128]{1,0:T(8,128)S(1)} %copy-done.5, f32[64,128]{1,0:T(8,128)S(1)} %copy-done.6, bf16[512,512]{1,0:T(8,128)(2,1)S(1)} %copy-done.3, ...), custom_call_target="tpu_custom_call" | custom-call | flops 10000000 | bytes 4000000 | tf_op jit(solution)/shard_map/pallas_call | solution.py:460
  58.6 3.6 %collective-permute-start.2 = (f32[4,32,512]{2,1,0:T(8,128)S(1)}, f32[4,32,512]{2,1,0:T(8,128)S(1)}, u32[]{:S(2)}, u32[]{:S(2)}) collective-permute-start(f32[4,32,512]{2,1,0:T(8,128)S(1)} %get-tuple-element.40), channel_id=1, source_target_pairs={{0,1},{1,0},{2,3},{3,2},{4,5},{5,4},{6,7},{7,6},{8,9},{9,8},{10,11... | collective-permute-start | bytes 786440 | tf_op jit(solution)/shard_map/ppermute | solution.py:556
  62.2 0.1 collective-permute-start.1
  62.3 0.9 %shard_map.188.kept = f32[8,32,512]{2,1,0:T(8,128)S(1)} custom-call(f32[8,32,512]{2,1,0:T(8,128)S(1)} %get-tuple-element.38.modes, bf16[512,512]{1,0:T(8,128)(2,1)S(1)} %copy-done.3, bf16[512,512]{1,0:T(8,128)(2,1)S(1)} %copy-done.4, bf16[256,256]{1,0:T(8,128)(2,1)S(1)} %copy-done.2, bf16[256,256]{1,0:T(8,128)(2,1)S(1)} %copy-done.1), custom_call_target="tpu_custom_call" | custom-call | flops 10000000 | bytes 4000000 | tf_op jit(solution)/shard_map/pallas_call | solution.py:460
  63.2 0.2 collective-permute-done.2.other
  63.4 0.8 %shard_map.189.begun = f32[8,32,1024]{2,1,0:T(8,128)} custom-call(f32[8,32,512]{2,1,0:T(8,128)S(1)} %shard_map.188.kept, f32[4,32,512]{2,1,0:T(8,128)S(1)} %collective-permute-done.2.other), custom_call_target="tpu_custom_call" | custom-call | flops 10000000 | bytes 4000000 | tf_op jit(solution)/shard_map/pallas_call | solution.py:460
  64.3 0.0 collective-permute-done.1.other
  64.3 0.8 %shard_map.190 = f32[8,32,1024]{2,1,0:T(8,128)} custom-call(f32[8,32,512]{2,1,0:T(8,128)S(1)} %shard_map.188.kept, f32[4,32,512]{2,1,0:T(8,128)S(1)} %collective-permute-done.1.other, f32[8,32,1024]{2,1,0:T(8,128)} %shard_map.189.begun), custom_call_target="tpu_custom_call", output_to_operand_aliasing={{}: (2, {})} | custom-call | flops 10000000 | bytes 4000000 | tf_op jit(solution)/shard_map/pallas_call | solution.py:460
Async XLA Ops:
  0.0 5.0 %copy-start.1 = (bf16[256,256]{1,0:T(8,128)(2,1)S(1)}, bf16[256,256]{1,0:T(8,128)(2,1)}, u32[]{:S(2)}) copy-start(bf16[256,256]{1,0:T(8,128)(2,1)} %constant.33.clone.slab_low) | copy-start | bytes 393220
  0.0 5.0 %copy-start.2 = (bf16[256,256]{1,0:T(8,128)(2,1)S(1)}, bf16[256,256]{1,0:T(8,128)(2,1)}, u32[]{:S(2)}) copy-start(bf16[256,256]{1,0:T(8,128)(2,1)} %constant.32.clone.slab_high) | copy-start | bytes 393220
  0.0 5.0 %copy-start.5 = (f32[40,128]{1,0:T(8,128)S(1)}, f32[40,128]{1,0:T(8,128)}, u32[]{:S(2)}) copy-start(f32[40,128]{1,0:T(8,128)} %constant.34.clone.shifts) | copy-start | bytes 61444
  1.7 5.3 %collective-permute-start = (f32[8,32,512]{2,1,0:T(8,128)S(1)}, f32[8,32,512]{2,1,0:T(8,128)S(1)}, u32[]{:S(2)}, u32[]{:S(2)}) collective-permute-start(f32[8,32,512]{2,1,0:T(8,128)S(1)} %get-tuple-element.27), channel_id=1, source_target_pairs={{0,1},{1,0},{2,3},{3,2},{4,5},{5,4},{6,7},{7,6},{8,9},{9,8},{10,11... | collective-permute-start | bytes 1572872 | tf_op jit(solution)/shard_map/ppermute | solution.py:510
  5.0 2.0 %copy-start.6 = (f32[64,128]{1,0:T(8,128)S(1)}, f32[64,128]{1,0:T(8,128)}, u32[]{:S(2)}) copy-start(f32[64,128]{1,0:T(8,128)} %constant.35.clone.weights) | copy-start | bytes 98308
  5.0 2.0 %copy-start.12 = (bf16[32,128]{1,0:T(8,128)(2,1)S(1)}, bf16[32,128]{1,0:T(8,128)(2,1)}, u32[]{:S(2)}) copy-start(bf16[32,128]{1,0:T(8,128)(2,1)} %constant.36.clone.fold) | copy-start | bytes 24580
  9.3 27.2 %all-to-all-start = ((f32[128,4,128]{2,1,0:T(4,128)}), f32[128,4,128]{2,1,0:T(4,128)S(1)}, u32[]{:S(2)}, u32[]{:S(2)}) async-start(f32[128,4,128]{2,1,0:T(4,128)} %bitcast.10), calls=%async_computation | async-start | bytes 524288 | tf_op jit(solution)/shard_map/all_to_all | solution.py:497
  23.1 1.0 %copy-start.7 = (f32[64,512]{1,0:T(8,128)S(1)}, f32[64,512]{1,0:T(8,128)}, u32[]{:S(2)}) copy-start(f32[64,512]{1,0:T(8,128)} %constant.41.clone.spread) | copy-start | bytes 393220
  23.1 1.0 %copy-start.8 = (f32[128,128]{1,0:T(8,128)S(1)}, f32[128,128]{1,0:T(8,128)}, u32[]{:S(2)}) copy-start(f32[128,128]{1,0:T(8,128)} %constant.42.clone.mask) | copy-start | bytes 196612
  23.1 1.0 %copy-start.11 = (f32[32,128]{1,0:T(8,128)S(1)}, f32[32,128]{1,0:T(8,128)}, u32[]{:S(2)}) copy-start(f32[32,128]{1,0:T(8,128)} %constant.39.clone.alias_shift) | copy-start | bytes 49156
  23.1 1.0 %copy-start.13 = (f32[1,128]{1,0:T(1,128)S(1)}, f32[1,128]{1,0:T(1,128)}, u32[]{:S(2)}) copy-start(f32[1,128]{1,0:T(1,128)} %constant.40.clone.mode_shift) | copy-start | bytes 1540
  24.2 12.3 %copy-start.9 = (bf16[96,256]{1,0:T(8,128)(2,1)S(1)}, bf16[96,256]{1,0:T(8,128)(2,1)}, u32[]{:S(2)}) copy-start(bf16[96,256]{1,0:T(8,128)(2,1)} %constant.43.clone.forward) | copy-start | bytes 147460
  24.2 12.3 %copy-start.10 = (f32[64,128]{1,0:T(8,128)S(1)}, f32[64,128]{1,0:T(8,128)}, u32[]{:S(2)}) copy-start(f32[64,128]{1,0:T(8,128)} %constant.44.clone.backward) | copy-start | bytes 98308
  36.5 20.5 %copy-start = (f32[16,32,512]{2,1,0:T(8,128)S(1)}, f32[16,32,512]{2,1,0:T(8,128)}, u32[]{:S(2)}) copy-start(f32[16,32,512]{2,1,0:T(8,128)} %shard_map.184.modes) | copy-start | bytes 3145732
  36.5 20.5 %copy-start.4 = (bf16[512,512]{1,0:T(8,128)(2,1)S(1)}, bf16[512,512]{1,0:T(8,128)(2,1)}, u32[]{:S(2)}) copy-start(bf16[512,512]{1,0:T(8,128)(2,1)} %get-tuple-element.37.table_low) | copy-start | bytes 1572868
  38.4 18.5 %copy-start.3 = (bf16[512,512]{1,0:T(8,128)(2,1)S(1)}, bf16[512,512]{1,0:T(8,128)(2,1)}, u32[]{:S(2)}) copy-start(bf16[512,512]{1,0:T(8,128)(2,1)} %get-tuple-element.36.table_high) | copy-start | bytes 1572868
  58.6 4.8 %collective-permute-start.2 = (f32[4,32,512]{2,1,0:T(8,128)S(1)}, f32[4,32,512]{2,1,0:T(8,128)S(1)}, u32[]{:S(2)}, u32[]{:S(2)}) collective-permute-start(f32[4,32,512]{2,1,0:T(8,128)S(1)} %get-tuple-element.40), channel_id=1, source_target_pairs={{0,1},{1,0},{2,3},{3,2},{4,5},{5,4},{6,7},{7,6},{8,9},{9,8},{10,11... | collective-permute-start | bytes 786440 | tf_op jit(solution)/shard_map/ppermute | solution.py:556
  62.2 2.0 %collective-permute-start.1 = (f32[4,32,512]{2,1,0:T(8,128)S(1)}, f32[4,32,512]{2,1,0:T(8,128)S(1)}, u32[]{:S(2)}, u32[]{:S(2)}) collective-permute-start(f32[4,32,512]{2,1,0:T(8,128)S(1)} %get-tuple-element.39), channel_id=1, source_target_pairs={{0,1},{1,0},{2,3},{3,2},{4,5},{5,4},{6,7},{7,6},{8,9},{9,8},{10,11... | collective-permute-start | bytes 786440 | tf_op jit(solution)/shard_map/ppermute | solution.py:557

commit v7 on v6

--- a/solution.py
+++ b/solution.py
@@ -15,6 +15,7 @@
 HALF = NY // 2
 CHIPS = 4
 LAYERS = NZ // CHIPS
+MIDDLE = NZ // 2
 PEERS = SLABS * CHIPS
 PARTS = 4
 ROWS = 4
@@ -152,6 +153,17 @@
         return lax.dot_general(one, two, (contract, ((), ())), preferred_element_type=jnp.float32)
 
     return dot(left_high, right_high) + (dot(left_high, right_low) + dot(left_low, right_high))
+
+
+def dot_stacked(left, right, contract):
+    high, low = split_values(left)
+    rows = left.shape[0]
+
+    def dot(one, two):
+        return lax.dot_general(one, two, (contract, ((), ())), preferred_element_type=jnp.float32)
+
+    both = dot(jnp.concatenate([high, low], axis=0), right[0])
+    return both[:rows] + (both[rows:] + dot(high, right[1]))
 
 
 def dot_full(left, right, contract):
@@ -266,6 +278,33 @@
     out[pl.ds(3, PEERS, stride=ROWS), :] = jnp.zeros((PEERS, LANES), jnp.float32)
 
 
+def solve_layers(right, inverse, face, part, use):
+    upper = lower = None
+    for step in range(MIDDLE):
+        inv = inverse[step]
+        value = right(step) * inv
+        upper = value if upper is None else value + (face[step - 1] * inv) * upper
+        part[step] = upper
+        layer = NZ - 1 - step
+        if layer > MIDDLE:
+            inv = inverse[layer]
+            value = right(layer) * inv
+            lower = value if lower is None else value + (face[layer] * inv) * lower
+            part[layer] = lower
+    inv = inverse[MIDDLE]
+    value = right(MIDDLE) * inv + (face[MIDDLE - 1] * inv) * upper + (face[MIDDLE] * inv) * lower
+    use(MIDDLE, value)
+    upper = lower = value
+    for step in range(1, MIDDLE + 1):
+        layer = MIDDLE - step
+        upper = part[layer] + (face[layer] * inverse[layer]) * upper
+        use(layer, upper)
+        layer = MIDDLE + step
+        if layer < NZ:
+            lower = part[layer] + (face[layer - 1] * inverse[layer]) * lower
+            use(layer, lower)
+
+
 def keep_kernel(modes, kept, sem):
     copy = pltpu.make_async_copy(modes, kept, sem)
     copy.start()
@@ -290,31 +329,41 @@
         mode = mode + jnp.where(lax.div(lane, PLANES) == part, values[part : part + 1], 0.0)
     shifts = jnp.concatenate([alias, mode], axis=0)
     row = lax.broadcasted_iota(jnp.int32, (8, LANES), 0)
-    previous = None
-    value = None
-    for layer in range(NZ):
+
+    def diagonal(layer):
         below = face[layer - 1] if layer > 0 else face[NZ - 1]
-        pivot = (below + face[layer] + screening[layer]) + cell[layer] * shifts
-        if previous is not None:
-            pivot = pivot - (below * below) * previous
-        previous = 1.0 / pivot
-        alias_inverse[layer] = previous[: 8 * PARTS]
-        inv = previous[8 * PARTS :]
-        inverses[layer] = inv
-        fresh = jnp.where(row == layer // LAYERS, inv, 0.0) if layer % LAYERS == 0 else None
-        if value is None:
-            value = fresh
-        else:
-            value = (face[layer - 1] * inv) * value
-            if fresh is not None:
-                value = value + fresh
-        columns[layer] = value
-    value = None
-    for layer in reversed(range(NZ)):
-        value = columns[layer] if value is None else columns[layer] + (face[layer] * inverses[layer]) * value
+        return (below + face[layer] + screening[layer]) + cell[layer] * shifts
+
+    def keep_pivot(layer, inverse):
+        alias_inverse[layer] = inverse[: 8 * PARTS]
+        inverses[layer] = inverse[8 * PARTS :]
+
+    upper = lower = None
+    for step in range(MIDDLE):
+        pivot = diagonal(step)
+        if upper is not None:
+            pivot = pivot - (face[step - 1] * face[step - 1]) * upper
+        upper = 1.0 / pivot
+        keep_pivot(step, upper)
+        layer = NZ - 1 - step
+        if layer > MIDDLE:
+            pivot = diagonal(layer)
+            if lower is not None:
+                pivot = pivot - (face[layer] * face[layer]) * lower
+            lower = 1.0 / pivot
+            keep_pivot(layer, lower)
+    pivot = diagonal(MIDDLE) - (face[MIDDLE - 1] * face[MIDDLE - 1]) * upper
+    keep_pivot(MIDDLE, 1.0 / (pivot - (face[MIDDLE] * face[MIDDLE]) * lower))
+
+    def unit(layer):
+        return jnp.where(row == layer // LAYERS, 1.0, 0.0) if layer % LAYERS == 0 else jnp.zeros((8, LANES), jnp.float32)
+
+    def keep_column(layer, value):
         scaled[layer * 8 : (layer + 1) * 8] = cell[layer] * value
         if layer % LAYERS == 0:
             corners[layer // LAYERS] = value
+
+    solve_layers(unit, inverses, face, columns, keep_column)
     for copy in copies:
         copy.wait()
     copies = [pltpu.make_async_copy(held_high, table_high, sems.at[2]), pltpu.make_async_copy(held_low, table_low, sems.at[3])]
@@ -342,7 +391,7 @@
         side = arrived[rows(chip, 0), :]
         sides.append(side + arrived[rows(chip - 1, 1), :] if chip > 0 else side)
     response = (response_high[...], response_low[...])
-    sums = dot_split(split_values(jnp.concatenate(sides, axis=1)), response)
+    sums = dot_stacked(jnp.concatenate(sides, axis=1), response, ((1,), (0,)))
     sums = sums + jnp.concatenate([arrived[rows(chip, 2), :] for chip in range(CHIPS)], axis=1)
     high, low = split_values(sums)
     stacked = jnp.concatenate([high, high, low], axis=0)
@@ -351,27 +400,25 @@
     for chip in range(CHIPS):
         at = chip * LANES
         source[chip * half : (chip + 1) * half, :] = turned[at : at + half, :LANES] + turned[at + half : at + LANES, LANES:]
-    value = None
-    for layer in range(NZ):
-        inv = alias_inverse[layer]
-        first = (layer // LAYERS) * half + layer % LAYERS
-        row = source[pl.ds(first, PARTS, stride=LAYERS), :]
-        row = jnp.concatenate([row] * 8, axis=0)
-        scaled = row * inv
-        value = scaled if value is None else scaled + (face[layer - 1] * inv) * value
-        part[layer] = value
-    value = None
-    for layer in reversed(range(NZ)):
-        value = part[layer] if value is None else part[layer] + (face[layer] * alias_inverse[layer]) * value
-        first = (layer // LAYERS) * half + layer % LAYERS
+
+    def first_row(layer):
+        return (layer // LAYERS) * half + layer % LAYERS
+
+    def right(layer):
+        row = source[pl.ds(first_row(layer), PARTS, stride=LAYERS), :]
+        return jnp.concatenate([row] * 8, axis=0)
+
+    def keep_sum(layer, value):
         total = (value[0:8] + value[8:16]) + (value[16:24] + value[24:32])
-        solved[pl.ds(first, PARTS, stride=LAYERS), :] = total[:PARTS] + total[PARTS:]
+        solved[pl.ds(first_row(layer), PARTS, stride=LAYERS), :] = total[:PARTS] + total[PARTS:]
+
+    solve_layers(right, alias_inverse, face, part, keep_sum)
     planes = dot_full(backward[...], solved[...], ((1,), (1,)))
     own = []
     for chip in range(CHIPS):
         at = chip * half
         own.append(jnp.concatenate([planes[:SLABS, at : at + half], planes[SLABS:, at : at + half]], axis=1))
-    change = dot_split(split_values(jnp.concatenate(own, axis=1)), response, ((1,), (1,)))
+    change = dot_stacked(jnp.concatenate(own, axis=1), response, ((1,), (1,)))
     ends = []
     for chip in range(CHIPS):
         end = change[:, chip * LANES : (chip + 1) * LANES]
@@ -387,7 +434,7 @@
         out[rows(chip, 3), :] = nothing
 
 
-def second_solve_kernel(modes, arrived, shifts, weights, table_high, table_low, slab_high, slab_low, coefficients, kept, sent_first, sent_last, part, near, edge, inverse):
+def second_solve_kernel(modes, arrived, shifts, weights, table_high, table_low, slab_high, slab_low, coefficients, kept, sent, part, near, edge, inverse):
     core, chip, _ = position()
     base = chip * LAYERS
     cell, face, _ = columns_of(coefficients, PARTS)
@@ -420,50 +467,40 @@
         part[layer] = jnp.where(keep, near[layer : layer + 1, :], value)
     part[0] = jnp.where(keep, near[0:1, :], below)
     kept[...] = part[pl.ds(core * 8, 8)]
-    planes = to_planes(part[pl.ds((1 - core) * 8, 8)], table_high, table_low, slab_high, slab_low)
-    sent_first[...] = planes[:4]
-    sent_last[...] = planes[4:]
+    sent[...] = to_planes(part[pl.ds((1 - core) * 8, 8)], table_high, table_low, slab_high, slab_low)
 
 
 def backward_kernel(modes, table_high, table_low, slab_high, slab_low, out):
     out[...] = to_planes(modes[...], table_high, table_low, slab_high, slab_low)
 
 
-def join_layers(first, kept, other, out, lines, sems):
+def join_kernel(kept, other, out, lines, sems):
     core, _, _ = position()
     sign = jnp.where(core == 0, 1.0, -1.0)
     copies = []
     for step in range(4):
-        one, two = kept[first + step], other[step]
-        lines[step, :, :HALF] = one + two
-        lines[step, :, HALF:] = sign * (one - two)
-        copies.append(pltpu.make_async_copy(lines.at[step], out.at[first + step], sems.at[step]))
+        at = slice(2 * step, 2 * step + 2)
+        one, two = kept[at], other[at]
+        lines[at, :, :HALF] = one + two
+        lines[at, :, HALF:] = sign * (one - two)
+        copies.append(pltpu.make_async_copy(lines.at[pl.ds(2 * step, 2)], out.at[pl.ds(2 * step, 2)], sems.at[step]))
         copies[-1].start()
     for copy in copies:
         copy.wait()
 
 
-def join_first_kernel(kept, other, out, lines, sems):
-    join_layers(0, kept, other, out, lines, sems)
-
-
-def join_last_kernel(kept, other, begun, out, lines, sems):
-    join_layers(4, kept, other, out, lines, sems)
-
-
 held = pl.BlockSpec(memory_space=pltpu.VMEM)
 far = pl.BlockSpec(memory_space=pl.ANY)
 in_hbm = functools.partial(pltpu.with_memory_space_constraint, memory_space=pltpu.HBM)
 
 
-def call(kernel, inputs, in_specs, outs, out_specs, scratch=(), cost=10_000_000, aliases={}):
+def call(kernel, inputs, in_specs, outs, out_specs, scratch=(), cost=10_000_000):
     return pl.pallas_call(
         kernel,
         in_specs=in_specs,
         out_specs=out_specs,
         out_shape=outs,
         scratch_shapes=scratch,
-        input_output_aliases=aliases,
         compiler_params=pltpu.CompilerParams(vmem_limit_bytes=VMEM_LIMIT),
         cost_estimate=pl.CostEstimate(flops=cost, bytes_accessed=4_000_000, transcendentals=0),
     )(*inputs)
@@ -545,21 +582,19 @@
         [vmem(CHIPS * PARTS * LAYERS, LANES), vmem(NZ, 8 * PARTS, LANES), vmem(CHIPS * PARTS * LAYERS, LANES)],
     )
     ends = exchange(ends)
-    kept, sent_first, sent_last = call(
+    kept, sent = call(
         second_solve_kernel,
         (modes, ends, shifts, weights, table_high, table_low, slab_high, slab_low, coefficients),
         [held] * 9,
-        [vmem(*cube), vmem(4, PLANES, HALF), vmem(4, PLANES, HALF)],
-        [held] * 3,
+        [vmem(*cube), vmem(*cube)],
+        [held] * 2,
         [vmem(*field), vmem(LAYERS, HALF), vmem(LAYERS, HALF), vmem(*field)],
     )
-    other_first = lax.ppermute(sent_first, "gz", pair)
-    other_last = lax.ppermute(sent_last, "gz", pair)
+    other = lax.ppermute(sent, "gz", pair)
     kept = call(backward_kernel, (kept, table_high, table_low, slab_high, slab_low), [held] * 5, vmem(*cube), held)
-    scratch = [vmem(4, PLANES, NY), pltpu.SemaphoreType.DMA((4,))]
-    out = pltpu.HBM((8, PLANES, NY), jnp.float32)
-    begun = call(join_first_kernel, (kept, other_first), [held] * 2, out, far, scratch)
-    return call(join_last_kernel, (kept, other_last, in_hbm(begun)), [held] * 2 + [far], out, far, scratch, aliases={2: 0})
+    return call(
+        join_kernel, (kept, other), [held] * 2, pltpu.HBM((8, PLANES, NY), jnp.float32), far, [lines, pltpu.SemaphoreType.DMA((4,))]
+    )
 
 
 def solution(mesh):

time: 65.4 us -> 65 us (level)
  Pallas kernels: 15.3 us -> 14.6 us
    ppermute x2 -> x0, starting transfers between devices: 3.74 us -> none  [the longest x1 3.64 us: body(): other_first = lax.ppermute(sent_first, 'gz', pair)]
    ppermute x1 -> x2, starting transfers between devices: 3.32 us -> 6.97 us  [body(): other = lax.ppermute(sent, 'gz', pair)]
    pallas_call x10 -> x9, Pallas kernels: 15.3 us -> 14.6 us  [call(): pl.pallas_call(kernel, in_specs=in_specs, out_specs=out_specs, out_shape=...]
    ppermute x1 -> x2, waiting for transfers between devices: 0.01 us -> 0.66 us  [body(): other = lax.ppermute(sent, 'gz', pair)]
  transfers between devices with their start and end apart: 4 -> 3, of which waited for: 2 -> 2; matrix products, arithmetic and copies ran while one was open for 0% -> 0% of each run, Pallas kernels for 11% -> 9%
where the time goes in v7:
time: 65 us; the launch traced here: 64.8 us
  starting transfers between devices  20.7 us (32%)
  blocking collectives  18.5 us (28%)
  Pallas kernels  14.6 us (22%)
  waiting for transfers between devices  10.6 us (16%)
    all_to_all x1, blocking collectives, exchange(): lax.all_to_all(blocks, ('gx', 'gz'), 0, 0, axis_index_groups=groups, tile...  18.5 us
    pallas_call x9, Pallas kernels, call(): pl.pallas_call(kernel, in_specs=in_specs, out_specs=out_specs, out_shape=...  14.6 us
    all_to_all x1, starting transfers between devices, exchange(): lax.all_to_all(blocks, ('gx', 'gz'), 0, 0, axis_index_groups=groups, tile...  13.8 us
    all_to_all x1, waiting for transfers between devices, exchange(): lax.all_to_all(blocks, ('gx', 'gz'), 0, 0, axis_index_groups=groups, tile...  9.97 us
    ppermute x2, starting transfers between devices, body(): other = lax.ppermute(sent, 'gz', pair)  6.97 us
  transfers between devices with their start and end apart: 3, of which 2 were waited for; matrix products, arithmetic and copies ran while one was open for 0% of the time, Pallas kernels for 9%

profile of v7, /device:TPU:1, one launch (start us, length us, event | category | flops | bytes accessed | tf_op | source)
XLA Modules:
  0.0 64.8 jit_solution(5469735577943966002)
XLA Ops:
  0.0 0.0 copy-start.1
  0.0 0.0 copy-start.2
  0.0 0.0 copy-start.5
  0.0 1.6 %shard_map.181 = (f32[8,32,512]{2,1,0:T(8,128)S(1)}, f32[8,32,512]{2,1,0:T(8,128)S(1)}, bf16[512,512]{1,0:T(8,128)(2,1)S(1)}, f32[192,128]{1,0:T(8,128)S(1)}) custom-call(f32[8,32,1024]{2,1,0:T(8,128)} %charge.1, bf16[2,512,512]{2,1,0:T(8,128)(2,1)} %constant.30.clone.tables_high, f32[1,64]{1,0:T(1,128)} %bitcast.11, f32[1,64]{1,0:T(1,128)} %bitcast.12, ...), custom_call_target="tpu_custom_call" | custom-call | flops 10000000 | bytes 4000000 | tf_op jit(solution)/shard_map/pallas_call | solution.py:498
  1.7 3.3 %collective-permute-start = (f32[8,32,512]{2,1,0:T(8,128)S(1)}, f32[8,32,512]{2,1,0:T(8,128)S(1)}, u32[]{:S(2)}, u32[]{:S(2)}) collective-permute-start(f32[8,32,512]{2,1,0:T(8,128)S(1)} %get-tuple-element.26), channel_id=1, source_target_pairs={{0,1},{1,0},{2,3},{3,2},{4,5},{5,4},{6,7},{7,6},{8,9},{9,8},{10,11... | collective-permute-start | bytes 1572872 | tf_op jit(solution)/shard_map/ppermute | solution.py:547
  5.0 0.0 copy-done.1
  5.0 0.0 copy-done.2
  5.0 0.0 copy-done.5
  5.0 0.0 copy-start.6
  5.0 0.0 copy-start.12
  5.0 2.0 %shard_map.182 = (f32[16,32,512]{2,1,0:T(8,128)S(1)}, f32[8,32,512]{2,1,0:T(8,128)S(1)}, bf16[512,512]{1,0:T(8,128)(2,1)S(1)}) custom-call(f32[8,32,512]{2,1,0:T(8,128)S(1)} %get-tuple-element.22.own, bf16[512,512]{1,0:T(8,128)(2,1)S(1)} %get-tuple-element.23.table_high, bf16[2,512,512]{2,1,0:T(8,128)(2,1)} %constant.31.clone.tables_low, ...), custom_call_target="tpu_custom_call" | custom-call | flops 10000000 | bytes 4000000 | tf_op jit(solution)/shard_map/pallas_call | solution.py:498
  7.0 0.0 collective-permute-done.other
  7.0 0.0 copy-done.6
  7.0 0.0 copy-done.12
  7.0 2.3 %shard_map.183 = (f32[16,32,512]{2,1,0:T(8,128)S(1)}, f32[512,128]{1,0:T(8,128)}) custom-call(f32[8,32,512]{2,1,0:T(8,128)S(1)} %get-tuple-element.25.own_modes, f32[8,32,512]{2,1,0:T(8,128)S(1)} %collective-permute-done.other, bf16[512,512]{1,0:T(8,128)(2,1)S(1)} %get-tuple-element.23.table_high, bf16[512,512]{1,0:T(8,128)(2,1)S(1)} %get-tuple-element.27.table_low, ...), custom_call_target="tpu_custom_call" | custom-call | flops 10000000 | bytes 4000000 | tf_op jit(solution)/shard_map/pallas_call | solution.py:498
  9.4 13.8 %all-to-all-start = ((f32[128,4,128]{2,1,0:T(4,128)}), f32[128,4,128]{2,1,0:T(4,128)S(1)}, u32[]{:S(2)}, u32[]{:S(2)}) async-start(f32[128,4,128]{2,1,0:T(4,128)} %bitcast.10), calls=%async_computation | async-start | bytes 524288 | tf_op jit(solution)/shard_map/all_to_all | solution.py:534
  23.1 0.0 copy-start.7
  23.1 0.0 copy-start.8
  23.2 0.0 copy-start.11
  23.2 0.0 copy-start.13
  23.2 1.0 %shard_map.184.modes = f32[16,32,512]{2,1,0:T(8,128)} custom-call(f32[16,32,512]{2,1,0:T(8,128)S(1)} %get-tuple-element.29.modes), custom_call_target="tpu_custom_call" | custom-call | flops 10000000 | bytes 4000000 | tf_op jit(solution)/shard_map/pallas_call | solution.py:498
  24.2 0.0 copy-done.7
  24.2 0.0 copy-done.8
  24.2 0.0 copy-done.11
  24.2 0.0 copy-done.13
  24.2 0.0 copy-start.9
  24.2 0.0 copy-start.10
  24.2 2.3 %shard_map.185 = (f32[64,32,128]{2,1,0:T(8,128)S(1)}, bf16[512,512]{1,0:T(8,128)(2,1)S(1)}, bf16[512,512]{1,0:T(8,128)(2,1)S(1)}, f32[4,8,128]{2,1,0:T(8,128)S(1...) custom-call(f32[16,32,512]{2,1,0:T(8,128)} %shard_map.184.modes, f32[40,128]{1,0:T(8,128)S(1)} %copy-done.5, ...), custom_call_target="tpu_custom_call" | custom-call | flops 10000000 | bytes 4000000 | tf_op jit(solution)/shard_map/pallas_call | solution.py:498
  26.5 10.0 %all-to-all-done = f32[128,4,128]{2,1,0:T(4,128)S(1)} async-done(((f32[128,4,128]{2,1,0:T(4,128)}), f32[128,4,128]{2,1,0:T(4,128)S(1)}, u32[]{:S(2)}, u32[]{:S(2)}) %all-to-all-start) | async-done | bytes 262176 | tf_op jit(solution)/shard_map/all_to_all | solution.py:534
  36.5 0.0 copy-done.9
  36.5 0.0 copy-done.10
  36.5 0.0 copy-start
  36.5 0.0 copy-start.4
  36.5 1.8 %shard_map.186 = f32[512,128]{1,0:T(8,128)S(1)} custom-call(f32[512,128]{1,0:T(8,128)S(1)} %bitcast.7, bf16[512,512]{1,0:T(8,128)(2,1)S(1)} %get-tuple-element.31.response_high, bf16[512,512]{1,0:T(8,128)(2,1)S(1)} %get-tuple-element.32.response_low, f32[4,8,128]{2,1,0:T(8,128)S(1)} %get-tuple-element.33.corners, ...), custom_call_target="tpu_custom_call" | custom-call | flops 10000000 | bytes 4000000 | tf_op jit(solution)/shard_map/pallas_call | solution.py:498
  38.3 0.0 copy-start.3
  38.3 18.5 %all_to_all.10 = f32[128,4,128]{2,1,0:T(4,128)S(1)} all-to-all(f32[128,4,128]{2,1,0:T(4,128)S(1)} %bitcast.9), channel_id=1, replica_groups={{0,2,4,6,8,10,12,14,16,18,20,22,24,26,28,30,32,34,36,38,40,42,44,46,48,..., dimensions={0} | all-to-all | bytes 524288 | tf_op jit(solution)/shard_map/all_to_all | solution.py:534
  56.8 0.0 copy-done
  56.8 0.0 copy-done.4
  56.8 0.0 copy-done.3
  56.8 1.7 %shard_map.187 = (f32[8,32,512]{2,1,0:T(8,128)S(1)}, f32[8,32,512]{2,1,0:T(8,128)S(1)}) custom-call(f32[16,32,512]{2,1,0:T(8,128)S(1)} %copy-done, f32[512,128]{1,0:T(8,128)S(1)} %bitcast.8, f32[40,128]{1,0:T(8,128)S(1)} %copy-done.5, f32[64,128]{1,0:T(8,128)S(1)} %copy-done.6, bf16[512,512]{1,0:T(8,128)(2,1)S(1)} %copy-done.3, ...), custom_call_target="tpu_custom_call" | custom-call | flops 10000000 | bytes 4000000 | tf_op jit(solution)/shard_map/pallas_call | solution.py:498
  58.5 3.6 %collective-permute-start.1 = (f32[8,32,512]{2,1,0:T(8,128)S(1)}, f32[8,32,512]{2,1,0:T(8,128)S(1)}, u32[]{:S(2)}, u32[]{:S(2)}) collective-permute-start(f32[8,32,512]{2,1,0:T(8,128)S(1)} %get-tuple-element.38), channel_id=1, source_target_pairs={{0,1},{1,0},{2,3},{3,2},{4,5},{5,4},{6,7},{7,6},{8,9},{9,8},{10,11... | collective-permute-start | bytes 1572872 | tf_op jit(solution)/shard_map/ppermute | solution.py:593
  62.2 0.9 %shard_map.188.kept = f32[8,32,512]{2,1,0:T(8,128)S(1)} custom-call(f32[8,32,512]{2,1,0:T(8,128)S(1)} %get-tuple-element.37.modes, bf16[512,512]{1,0:T(8,128)(2,1)S(1)} %copy-done.3, bf16[512,512]{1,0:T(8,128)(2,1)S(1)} %copy-done.4, bf16[256,256]{1,0:T(8,128)(2,1)S(1)} %copy-done.2, bf16[256,256]{1,0:T(8,128)(2,1)S(1)} %copy-done.1), custom_call_target="tpu_custom_call" | custom-call | flops 10000000 | bytes 4000000 | tf_op jit(solution)/shard_map/pallas_call | solution.py:498
  63.1 0.7 %collective-permute-done.1.other = f32[8,32,512]{2,1,0:T(8,128)S(1)} collective-permute-done((f32[8,32,512]{2,1,0:T(8,128)S(1)}, f32[8,32,512]{2,1,0:T(8,128)S(1)}, u32[]{:S(2)}, u32[]{:S(2)}) %collective-permute-start.1) | collective-permute-done | bytes 524320 | tf_op jit(solution)/shard_map/ppermute | solution.py:593
  63.7 1.0 %shard_map.189 = f32[8,32,1024]{2,1,0:T(8,128)} custom-call(f32[8,32,512]{2,1,0:T(8,128)S(1)} %shard_map.188.kept, f32[8,32,512]{2,1,0:T(8,128)S(1)} %collective-permute-done.1.other), custom_call_target="tpu_custom_call" | custom-call | flops 10000000 | bytes 4000000 | tf_op jit(solution)/shard_map/pallas_call | solution.py:498
Async XLA Ops:
  0.0 5.0 %copy-start.1 = (bf16[256,256]{1,0:T(8,128)(2,1)S(1)}, bf16[256,256]{1,0:T(8,128)(2,1)}, u32[]{:S(2)}) copy-start(bf16[256,256]{1,0:T(8,128)(2,1)} %constant.33.clone.slab_low) | copy-start | bytes 393220
  0.0 5.0 %copy-start.2 = (bf16[256,256]{1,0:T(8,128)(2,1)S(1)}, bf16[256,256]{1,0:T(8,128)(2,1)}, u32[]{:S(2)}) copy-start(bf16[256,256]{1,0:T(8,128)(2,1)} %constant.32.clone.slab_high) | copy-start | bytes 393220
  0.0 5.0 %copy-start.5 = (f32[40,128]{1,0:T(8,128)S(1)}, f32[40,128]{1,0:T(8,128)}, u32[]{:S(2)}) copy-start(f32[40,128]{1,0:T(8,128)} %constant.34.clone.shifts) | copy-start | bytes 61444
  1.7 5.3 %collective-permute-start = (f32[8,32,512]{2,1,0:T(8,128)S(1)}, f32[8,32,512]{2,1,0:T(8,128)S(1)}, u32[]{:S(2)}, u32[]{:S(2)}) collective-permute-start(f32[8,32,512]{2,1,0:T(8,128)S(1)} %get-tuple-element.26), channel_id=1, source_target_pairs={{0,1},{1,0},{2,3},{3,2},{4,5},{5,4},{6,7},{7,6},{8,9},{9,8},{10,11... | collective-permute-start | bytes 1572872 | tf_op jit(solution)/shard_map/ppermute | solution.py:547
  5.0 2.0 %copy-start.6 = (f32[64,128]{1,0:T(8,128)S(1)}, f32[64,128]{1,0:T(8,128)}, u32[]{:S(2)}) copy-start(f32[64,128]{1,0:T(8,128)} %constant.35.clone.weights) | copy-start | bytes 98308
  5.0 2.0 %copy-start.12 = (bf16[32,128]{1,0:T(8,128)(2,1)S(1)}, bf16[32,128]{1,0:T(8,128)(2,1)}, u32[]{:S(2)}) copy-start(bf16[32,128]{1,0:T(8,128)(2,1)} %constant.36.clone.fold) | copy-start | bytes 24580
  9.4 27.2 %all-to-all-start = ((f32[128,4,128]{2,1,0:T(4,128)}), f32[128,4,128]{2,1,0:T(4,128)S(1)}, u32[]{:S(2)}, u32[]{:S(2)}) async-start(f32[128,4,128]{2,1,0:T(4,128)} %bitcast.10), calls=%async_computation | async-start | bytes 524288 | tf_op jit(solution)/shard_map/all_to_all | solution.py:534
  23.1 1.0 %copy-start.7 = (f32[64,512]{1,0:T(8,128)S(1)}, f32[64,512]{1,0:T(8,128)}, u32[]{:S(2)}) copy-start(f32[64,512]{1,0:T(8,128)} %constant.41.clone.spread) | copy-start | bytes 393220
  23.1 1.0 %copy-start.8 = (f32[128,128]{1,0:T(8,128)S(1)}, f32[128,128]{1,0:T(8,128)}, u32[]{:S(2)}) copy-start(f32[128,128]{1,0:T(8,128)} %constant.42.clone.mask) | copy-start | bytes 196612
  23.2 1.0 %copy-start.11 = (f32[32,128]{1,0:T(8,128)S(1)}, f32[32,128]{1,0:T(8,128)}, u32[]{:S(2)}) copy-start(f32[32,128]{1,0:T(8,128)} %constant.39.clone.alias_shift) | copy-start | bytes 49156
  23.2 1.0 %copy-start.13 = (f32[1,128]{1,0:T(1,128)S(1)}, f32[1,128]{1,0:T(1,128)}, u32[]{:S(2)}) copy-start(f32[1,128]{1,0:T(1,128)} %constant.40.clone.mode_shift) | copy-start | bytes 1540
  24.2 12.3 %copy-start.9 = (bf16[96,256]{1,0:T(8,128)(2,1)S(1)}, bf16[96,256]{1,0:T(8,128)(2,1)}, u32[]{:S(2)}) copy-start(bf16[96,256]{1,0:T(8,128)(2,1)} %constant.43.clone.forward) | copy-start | bytes 147460
  24.2 12.3 %copy-start.10 = (f32[64,128]{1,0:T(8,128)S(1)}, f32[64,128]{1,0:T(8,128)}, u32[]{:S(2)}) copy-start(f32[64,128]{1,0:T(8,128)} %constant.44.clone.backward) | copy-start | bytes 98308
  36.5 20.3 %copy-start = (f32[16,32,512]{2,1,0:T(8,128)S(1)}, f32[16,32,512]{2,1,0:T(8,128)}, u32[]{:S(2)}) copy-start(f32[16,32,512]{2,1,0:T(8,128)} %shard_map.184.modes) | copy-start | bytes 3145732
  36.5 20.3 %copy-start.4 = (bf16[512,512]{1,0:T(8,128)(2,1)S(1)}, bf16[512,512]{1,0:T(8,128)(2,1)}, u32[]{:S(2)}) copy-start(bf16[512,512]{1,0:T(8,128)(2,1)} %get-tuple-element.36.table_low) | copy-start | bytes 1572868
  38.3 18.5 %copy-start.3 = (bf16[512,512]{1,0:T(8,128)(2,1)S(1)}, bf16[512,512]{1,0:T(8,128)(2,1)}, u32[]{:S(2)}) copy-start(bf16[512,512]{1,0:T(8,128)(2,1)} %get-tuple-element.35.table_high) | copy-start | bytes 1572868
  58.5 5.2 %collective-permute-start.1 = (f32[8,32,512]{2,1,0:T(8,128)S(1)}, f32[8,32,512]{2,1,0:T(8,128)S(1)}, u32[]{:S(2)}, u32[]{:S(2)}) collective-permute-start(f32[8,32,512]{2,1,0:T(8,128)S(1)} %get-tuple-element.38), channel_id=1, source_target_pairs={{0,1},{1,0},{2,3},{3,2},{4,5},{5,4},{6,7},{7,6},{8,9},{9,8},{10,11... | collective-permute-start | bytes 1572872 | tf_op jit(solution)/shard_map/ppermute | solution.py:593

commit v8 on v7

--- a/solution.py
+++ b/solution.py
@@ -31,12 +31,13 @@
 
 
 def y_frequencies():
+    index = np.arange(HALF // 2)
+    quarter = HALF // 4
+    even = np.concatenate([4 * np.where(index <= quarter, index, index - quarter), 4 * (index % quarter) + 2])
+    even_is_cos = np.concatenate([index <= quarter, index < quarter])
     index = np.arange(HALF)
-    even = np.where(index <= HALF // 2, 2 * index, 2 * (index - HALF // 2))
-    odd = np.where(index < HALF // 2, 2 * index + 1, 2 * (index - HALF // 2) + 1)
-    even_is_cos = index <= HALF // 2
-    odd_is_cos = index < HALF // 2
-    return np.stack([even, odd]), np.stack([even_is_cos, odd_is_cos])
+    odd = 2 * (index % (HALF // 2)) + 1
+    return np.stack([even, odd]), np.stack([even_is_cos, index < HALF // 2])
 
 
 def y_tables():
@@ -225,15 +226,40 @@
     modes[...] = dot_split((slab_high[...], slab_low[...]), split_values(spectrum)).reshape(8, PLANES, HALF)
 
 
-def to_modes(planes, table_high, table_low, slab_high, slab_low):
+def spectrum_into(out, planes, table_high, table_low):
+    core, _, _ = position()
     values = planes[...].reshape(8 * PLANES, HALF)
-    spectrum = dot_split(split_values(values), (table_high[...], table_low[...]))
-    return dot_split((slab_high[...], slab_low[...]), split_values(spectrum)).reshape(8, PLANES, HALF)
-
-
-def to_planes(modes, table_high, table_low, slab_high, slab_low):
+    half = HALF // 2
+
+    @pl.when(core == 0)
+    def _():
+        for at, sign in ((0, 1.0), (half, -1.0)):
+            mixed = values[:, :half] + sign * values[:, half:]
+            table = (table_high[:half, at : at + half], table_low[:half, at : at + half])
+            out[:, :, at : at + half] = dot_split(split_values(mixed), table).reshape(8, PLANES, half)
+
+    @pl.when(core != 0)
+    def _():
+        out[...] = dot_split(split_values(values), (table_high[...], table_low[...])).reshape(8, PLANES, HALF)
+
+
+def planes_into(out, modes, table_high, table_low, slab_high, slab_low):
+    core, _, _ = position()
     values = dot_split((slab_high[...], slab_low[...]), split_values(modes.reshape(8 * PLANES, HALF)))
-    return dot_split(split_values(values), (table_high[...], table_low[...])).reshape(8, PLANES, HALF)
+    half = HALF // 2
+
+    @pl.when(core == 0)
+    def _():
+        one, two = [
+            dot_split(split_values(values[:, at : at + half]), (table_high[at : at + half, :half], table_low[at : at + half, :half]))
+            for at in (0, half)
+        ]
+        out[:, :, :half] = (one + two).reshape(8, PLANES, half)
+        out[:, :, half:] = (one - two).reshape(8, PLANES, half)
+
+    @pl.when(core != 0)
+    def _():
+        out[...] = dot_split(split_values(values), (table_high[...], table_low[...])).reshape(8, PLANES, HALF)
 
 
 def stack_parts(values):
@@ -250,7 +276,9 @@
     base = chip * LAYERS
     cell, face, _ = columns_of(coefficients, PARTS)
     modes[pl.ds(core * 8, 8)] = own_modes[...]
-    modes[pl.ds((1 - core) * 8, 8)] = to_modes(other, table_high, table_low, slab_high, slab_low)
+    spectrum_into(part.at[pl.ds(0, 8)], other, table_high, table_low)
+    spectrum = split_values(part[0:8].reshape(8 * PLANES, HALF))
+    modes[pl.ds((1 - core) * 8, 8)] = dot_split((slab_high[...], slab_low[...]), spectrum).reshape(8, PLANES, HALF)
     value = None
     for layer in range(1, LAYERS):
         inv = inverse[layer]
@@ -467,11 +495,11 @@
         part[layer] = jnp.where(keep, near[layer : layer + 1, :], value)
     part[0] = jnp.where(keep, near[0:1, :], below)
     kept[...] = part[pl.ds(core * 8, 8)]
-    sent[...] = to_planes(part[pl.ds((1 - core) * 8, 8)], table_high, table_low, slab_high, slab_low)
+    planes_into(sent, part[pl.ds((1 - core) * 8, 8)], table_high, table_low, slab_high, slab_low)
 
 
 def backward_kernel(modes, table_high, table_low, slab_high, slab_low, out):
-    out[...] = to_planes(modes[...], table_high, table_low, slab_high, slab_low)
+    planes_into(out, modes[...], table_high, table_low, slab_high, slab_low)
 
 
 def join_kernel(kept, other, out, lines, sems):

time: 65 us -> 65.1 us (level)
  transfers between devices with their start and end apart: 3 -> 3, of which waited for: 2 -> 2; matrix products, arithmetic and copies ran while one was open for 0% -> 0% of each run, Pallas kernels for 9% -> 10%
where the time goes in v8:
time: 65.1 us; the launch traced here: 64.9 us
  starting transfers between devices  20.5 us (31%)
  blocking collectives  18.1 us (28%)
  Pallas kernels  15 us (23%)
  waiting for transfers between devices  10.9 us (17%)
    all_to_all x1, blocking collectives, exchange(): lax.all_to_all(blocks, ('gx', 'gz'), 0, 0, axis_index_groups=groups, tile...  18.1 us
    pallas_call x9, Pallas kernels, call(): pl.pallas_call(kernel, in_specs=in_specs, out_specs=out_specs, out_shape=...  15 us
    all_to_all x1, starting transfers between devices, exchange(): lax.all_to_all(blocks, ('gx', 'gz'), 0, 0, axis_index_groups=groups, tile...  13.8 us
    all_to_all x1, waiting for transfers between devices, exchange(): lax.all_to_all(blocks, ('gx', 'gz'), 0, 0, axis_index_groups=groups, tile...  10.4 us
    ppermute x2, starting transfers between devices, body(): other = lax.ppermute(sent, 'gz', pair)  6.77 us
  transfers between devices with their start and end apart: 3, of which 2 were waited for; matrix products, arithmetic and copies ran while one was open for 0% of the time, Pallas kernels for 10%

profile of v8, /device:TPU:1, one launch (start us, length us, event | category | flops | bytes accessed | tf_op | source)
XLA Modules:
  0.0 64.9 jit_solution(13746826424699625905)
XLA Ops:
  0.0 0.0 copy-start.1
  0.0 0.0 copy-start.2
  0.0 0.0 copy-start.5
  0.0 1.6 %shard_map.181 = (f32[8,32,512]{2,1,0:T(8,128)S(1)}, f32[8,32,512]{2,1,0:T(8,128)S(1)}, bf16[512,512]{1,0:T(8,128)(2,1)S(1)}, f32[192,128]{1,0:T(8,128)S(1)}) custom-call(f32[8,32,1024]{2,1,0:T(8,128)} %charge.1, bf16[2,512,512]{2,1,0:T(8,128)(2,1)} %constant.30.clone.tables_high, f32[1,64]{1,0:T(1,128)} %bitcast.11, f32[1,64]{1,0:T(1,128)} %bitcast.12, ...), custom_call_target="tpu_custom_call" | custom-call | flops 10000000 | bytes 4000000 | tf_op jit(solution)/shard_map/pallas_call | solution.py:526
  1.7 3.3 %collective-permute-start = (f32[8,32,512]{2,1,0:T(8,128)S(1)}, f32[8,32,512]{2,1,0:T(8,128)S(1)}, u32[]{:S(2)}, u32[]{:S(2)}) collective-permute-start(f32[8,32,512]{2,1,0:T(8,128)S(1)} %get-tuple-element.26), channel_id=1, source_target_pairs={{0,1},{1,0},{2,3},{3,2},{4,5},{5,4},{6,7},{7,6},{8,9},{9,8},{10,11... | collective-permute-start | bytes 1572872 | tf_op jit(solution)/shard_map/ppermute | solution.py:575
  5.0 0.0 copy-done.1
  5.0 0.0 copy-done.2
  5.0 0.0 copy-done.5
  5.0 0.0 copy-start.6
  5.0 0.0 copy-start.12
  5.0 2.0 %shard_map.182 = (f32[16,32,512]{2,1,0:T(8,128)S(1)}, f32[8,32,512]{2,1,0:T(8,128)S(1)}, bf16[512,512]{1,0:T(8,128)(2,1)S(1)}) custom-call(f32[8,32,512]{2,1,0:T(8,128)S(1)} %get-tuple-element.22.own, bf16[512,512]{1,0:T(8,128)(2,1)S(1)} %get-tuple-element.23.table_high, bf16[2,512,512]{2,1,0:T(8,128)(2,1)} %constant.31.clone.tables_low, ...), custom_call_target="tpu_custom_call" | custom-call | flops 10000000 | bytes 4000000 | tf_op jit(solution)/shard_map/pallas_call | solution.py:526
  7.0 0.0 collective-permute-done.other
  7.0 0.0 copy-done.6
  7.0 0.0 copy-done.12
  7.0 2.5 %shard_map.183 = (f32[16,32,512]{2,1,0:T(8,128)S(1)}, f32[512,128]{1,0:T(8,128)}) custom-call(f32[8,32,512]{2,1,0:T(8,128)S(1)} %get-tuple-element.25.own_modes, f32[8,32,512]{2,1,0:T(8,128)S(1)} %collective-permute-done.other, bf16[512,512]{1,0:T(8,128)(2,1)S(1)} %get-tuple-element.23.table_high, bf16[512,512]{1,0:T(8,128)(2,1)S(1)} %get-tuple-element.27.table_low, ...), custom_call_target="tpu_custom_call" | custom-call | flops 10000000 | bytes 4000000 | tf_op jit(solution)/shard_map/pallas_call | solution.py:526
  9.5 13.8 %all-to-all-start = ((f32[128,4,128]{2,1,0:T(4,128)}), f32[128,4,128]{2,1,0:T(4,128)S(1)}, u32[]{:S(2)}, u32[]{:S(2)}) async-start(f32[128,4,128]{2,1,0:T(4,128)} %bitcast.10), calls=%async_computation | async-start | bytes 524288 | tf_op jit(solution)/shard_map/all_to_all | solution.py:562
  23.3 0.0 copy-start.7
  23.3 0.0 copy-start.8
  23.3 0.0 copy-start.11
  23.4 0.0 copy-start.13
  23.4 1.0 %shard_map.184.modes = f32[16,32,512]{2,1,0:T(8,128)} custom-call(f32[16,32,512]{2,1,0:T(8,128)S(1)} %get-tuple-element.29.modes), custom_call_target="tpu_custom_call" | custom-call | flops 10000000 | bytes 4000000 | tf_op jit(solution)/shard_map/pallas_call | solution.py:526
  24.4 0.0 copy-done.7
  24.4 0.0 copy-done.8
  24.4 0.0 copy-done.11
  24.4 0.0 copy-done.13
  24.4 0.0 copy-start.9
  24.4 0.0 copy-start.10
  24.4 2.3 %shard_map.185 = (f32[64,32,128]{2,1,0:T(8,128)S(1)}, bf16[512,512]{1,0:T(8,128)(2,1)S(1)}, bf16[512,512]{1,0:T(8,128)(2,1)S(1)}, f32[4,8,128]{2,1,0:T(8,128)S(1...) custom-call(f32[16,32,512]{2,1,0:T(8,128)} %shard_map.184.modes, f32[40,128]{1,0:T(8,128)S(1)} %copy-done.5, ...), custom_call_target="tpu_custom_call" | custom-call | flops 10000000 | bytes 4000000 | tf_op jit(solution)/shard_map/pallas_call | solution.py:526
  26.7 10.4 %all-to-all-done = f32[128,4,128]{2,1,0:T(4,128)S(1)} async-done(((f32[128,4,128]{2,1,0:T(4,128)}), f32[128,4,128]{2,1,0:T(4,128)S(1)}, u32[]{:S(2)}, u32[]{:S(2)}) %all-to-all-start) | async-done | bytes 262176 | tf_op jit(solution)/shard_map/all_to_all | solution.py:562
  37.1 0.0 copy-done.9
  37.1 0.0 copy-done.10
  37.1 0.0 copy-start
  37.1 0.0 copy-start.4
  37.1 1.8 %shard_map.186 = f32[512,128]{1,0:T(8,128)S(1)} custom-call(f32[512,128]{1,0:T(8,128)S(1)} %bitcast.7, bf16[512,512]{1,0:T(8,128)(2,1)S(1)} %get-tuple-element.31.response_high, bf16[512,512]{1,0:T(8,128)(2,1)S(1)} %get-tuple-element.32.response_low, f32[4,8,128]{2,1,0:T(8,128)S(1)} %get-tuple-element.33.corners, ...), custom_call_target="tpu_custom_call" | custom-call | flops 10000000 | bytes 4000000 | tf_op jit(solution)/shard_map/pallas_call | solution.py:526
  38.9 0.0 copy-start.3
  38.9 18.1 %all_to_all.10 = f32[128,4,128]{2,1,0:T(4,128)S(1)} all-to-all(f32[128,4,128]{2,1,0:T(4,128)S(1)} %bitcast.9), channel_id=1, replica_groups={{0,2,4,6,8,10,12,14,16,18,20,22,24,26,28,30,32,34,36,38,40,42,44,46,48,..., dimensions={0} | all-to-all | bytes 524288 | tf_op jit(solution)/shard_map/all_to_all | solution.py:562
  57.0 0.0 copy-done
  57.0 0.0 copy-done.4
  57.0 0.0 copy-done.3
  57.0 1.8 %shard_map.187 = (f32[8,32,512]{2,1,0:T(8,128)S(1)}, f32[8,32,512]{2,1,0:T(8,128)S(1)}) custom-call(f32[16,32,512]{2,1,0:T(8,128)S(1)} %copy-done, f32[512,128]{1,0:T(8,128)S(1)} %bitcast.8, f32[40,128]{1,0:T(8,128)S(1)} %copy-done.5, f32[64,128]{1,0:T(8,128)S(1)} %copy-done.6, bf16[512,512]{1,0:T(8,128)(2,1)S(1)} %copy-done.3, ...), custom_call_target="tpu_custom_call" | custom-call | flops 10000000 | bytes 4000000 | tf_op jit(solution)/shard_map/pallas_call | solution.py:526
  58.9 3.5 %collective-permute-start.1 = (f32[8,32,512]{2,1,0:T(8,128)S(1)}, f32[8,32,512]{2,1,0:T(8,128)S(1)}, u32[]{:S(2)}, u32[]{:S(2)}) collective-permute-start(f32[8,32,512]{2,1,0:T(8,128)S(1)} %get-tuple-element.38), channel_id=1, source_target_pairs={{0,1},{1,0},{2,3},{3,2},{4,5},{5,4},{6,7},{7,6},{8,9},{9,8},{10,11... | collective-permute-start | bytes 1572872 | tf_op jit(solution)/shard_map/ppermute | solution.py:621
  62.3 1.0 %shard_map.188.kept = f32[8,32,512]{2,1,0:T(8,128)S(1)} custom-call(f32[8,32,512]{2,1,0:T(8,128)S(1)} %get-tuple-element.37.modes, bf16[512,512]{1,0:T(8,128)(2,1)S(1)} %copy-done.3, bf16[512,512]{1,0:T(8,128)(2,1)S(1)} %copy-done.4, bf16[256,256]{1,0:T(8,128)(2,1)S(1)} %copy-done.2, bf16[256,256]{1,0:T(8,128)(2,1)S(1)} %copy-done.1), custom_call_target="tpu_custom_call" | custom-call | flops 10000000 | bytes 4000000 | tf_op jit(solution)/shard_map/pallas_call | solution.py:526
  63.3 0.6 collective-permute-done.1.other
  63.9 1.0 %shard_map.189 = f32[8,32,1024]{2,1,0:T(8,128)} custom-call(f32[8,32,512]{2,1,0:T(8,128)S(1)} %shard_map.188.kept, f32[8,32,512]{2,1,0:T(8,128)S(1)} %collective-permute-done.1.other), custom_call_target="tpu_custom_call" | custom-call | flops 10000000 | bytes 4000000 | tf_op jit(solution)/shard_map/pallas_call | solution.py:526
Async XLA Ops:
  0.0 5.0 %copy-start.1 = (bf16[256,256]{1,0:T(8,128)(2,1)S(1)}, bf16[256,256]{1,0:T(8,128)(2,1)}, u32[]{:S(2)}) copy-start(bf16[256,256]{1,0:T(8,128)(2,1)} %constant.33.clone.slab_low) | copy-start | bytes 393220
  0.0 5.0 %copy-start.2 = (bf16[256,256]{1,0:T(8,128)(2,1)S(1)}, bf16[256,256]{1,0:T(8,128)(2,1)}, u32[]{:S(2)}) copy-start(bf16[256,256]{1,0:T(8,128)(2,1)} %constant.32.clone.slab_high) | copy-start | bytes 393220
  0.0 5.0 %copy-start.5 = (f32[40,128]{1,0:T(8,128)S(1)}, f32[40,128]{1,0:T(8,128)}, u32[]{:S(2)}) copy-start(f32[40,128]{1,0:T(8,128)} %constant.34.clone.shifts) | copy-start | bytes 61444
  1.7 5.3 %collective-permute-start = (f32[8,32,512]{2,1,0:T(8,128)S(1)}, f32[8,32,512]{2,1,0:T(8,128)S(1)}, u32[]{:S(2)}, u32[]{:S(2)}) collective-permute-start(f32[8,32,512]{2,1,0:T(8,128)S(1)} %get-tuple-element.26), channel_id=1, source_target_pairs={{0,1},{1,0},{2,3},{3,2},{4,5},{5,4},{6,7},{7,6},{8,9},{9,8},{10,11... | collective-permute-start | bytes 1572872 | tf_op jit(solution)/shard_map/ppermute | solution.py:575
  5.0 2.0 %copy-start.6 = (f32[64,128]{1,0:T(8,128)S(1)}, f32[64,128]{1,0:T(8,128)}, u32[]{:S(2)}) copy-start(f32[64,128]{1,0:T(8,128)} %constant.35.clone.weights) | copy-start | bytes 98308
  5.0 2.0 %copy-start.12 = (bf16[32,128]{1,0:T(8,128)(2,1)S(1)}, bf16[32,128]{1,0:T(8,128)(2,1)}, u32[]{:S(2)}) copy-start(bf16[32,128]{1,0:T(8,128)(2,1)} %constant.36.clone.fold) | copy-start | bytes 24580
  9.5 27.6 %all-to-all-start = ((f32[128,4,128]{2,1,0:T(4,128)}), f32[128,4,128]{2,1,0:T(4,128)S(1)}, u32[]{:S(2)}, u32[]{:S(2)}) async-start(f32[128,4,128]{2,1,0:T(4,128)} %bitcast.10), calls=%async_computation | async-start | bytes 524288 | tf_op jit(solution)/shard_map/all_to_all | solution.py:562
  23.3 1.0 %copy-start.7 = (f32[64,512]{1,0:T(8,128)S(1)}, f32[64,512]{1,0:T(8,128)}, u32[]{:S(2)}) copy-start(f32[64,512]{1,0:T(8,128)} %constant.41.clone.spread) | copy-start | bytes 393220
  23.3 1.0 %copy-start.8 = (f32[128,128]{1,0:T(8,128)S(1)}, f32[128,128]{1,0:T(8,128)}, u32[]{:S(2)}) copy-start(f32[128,128]{1,0:T(8,128)} %constant.42.clone.mask) | copy-start | bytes 196612
  23.3 1.0 %copy-start.11 = (f32[32,128]{1,0:T(8,128)S(1)}, f32[32,128]{1,0:T(8,128)}, u32[]{:S(2)}) copy-start(f32[32,128]{1,0:T(8,128)} %constant.39.clone.alias_shift) | copy-start | bytes 49156
  23.4 1.0 %copy-start.13 = (f32[1,128]{1,0:T(1,128)S(1)}, f32[1,128]{1,0:T(1,128)}, u32[]{:S(2)}) copy-start(f32[1,128]{1,0:T(1,128)} %constant.40.clone.mode_shift) | copy-start | bytes 1540
  24.4 12.7 %copy-start.9 = (bf16[96,256]{1,0:T(8,128)(2,1)S(1)}, bf16[96,256]{1,0:T(8,128)(2,1)}, u32[]{:S(2)}) copy-start(bf16[96,256]{1,0:T(8,128)(2,1)} %constant.43.clone.forward) | copy-start | bytes 147460
  24.4 12.7 %copy-start.10 = (f32[64,128]{1,0:T(8,128)S(1)}, f32[64,128]{1,0:T(8,128)}, u32[]{:S(2)}) copy-start(f32[64,128]{1,0:T(8,128)} %constant.44.clone.backward) | copy-start | bytes 98308
  37.1 19.9 %copy-start = (f32[16,32,512]{2,1,0:T(8,128)S(1)}, f32[16,32,512]{2,1,0:T(8,128)}, u32[]{:S(2)}) copy-start(f32[16,32,512]{2,1,0:T(8,128)} %shard_map.184.modes) | copy-start | bytes 3145732
  37.1 19.9 %copy-start.4 = (bf16[512,512]{1,0:T(8,128)(2,1)S(1)}, bf16[512,512]{1,0:T(8,128)(2,1)}, u32[]{:S(2)}) copy-start(bf16[512,512]{1,0:T(8,128)(2,1)} %get-tuple-element.36.table_low) | copy-start | bytes 1572868
  38.9 18.1 %copy-start.3 = (bf16[512,512]{1,0:T(8,128)(2,1)S(1)}, bf16[512,512]{1,0:T(8,128)(2,1)}, u32[]{:S(2)}) copy-start(bf16[512,512]{1,0:T(8,128)(2,1)} %get-tuple-element.35.table_high) | copy-start | bytes 1572868
  58.9 5.0 %collective-permute-start.1 = (f32[8,32,512]{2,1,0:T(8,128)S(1)}, f32[8,32,512]{2,1,0:T(8,128)S(1)}, u32[]{:S(2)}, u32[]{:S(2)}) collective-permute-start(f32[8,32,512]{2,1,0:T(8,128)S(1)} %get-tuple-element.38), channel_id=1, source_target_pairs={{0,1},{1,0},{2,3},{3,2},{4,5},{5,4},{6,7},{7,6},{8,9},{9,8},{10,11... | collective-permute-start | bytes 1572872 | tf_op jit(solution)/shard_map/ppermute | solution.py:621

commit v9 on v8

--- a/solution.py
+++ b/solution.py
@@ -173,11 +173,12 @@
     )
 
 
-def split_kernel(charge, tables_high, cell, face, screening, own, sent, table_high, coefficients, lines, rows, sems):
+def split_kernel(charge, tables_high, tables_low, cell, face, screening, own, sent, table_high, table_low, coefficients, lines, rows, sems):
     core, _, _ = position()
-    copies = [pltpu.make_async_copy(source, rows.at[step], sems.at[9 + step]) for step, source in enumerate((cell, face, screening))]
+    copies = [pltpu.make_async_copy(source, rows.at[step], sems.at[10 + step]) for step, source in enumerate((cell, face, screening))]
     copies += [pltpu.make_async_copy(charge.at[step], lines.at[step], sems.at[step]) for step in range(8)]
     copies.append(pltpu.make_async_copy(tables_high.at[core], table_high, sems.at[8]))
+    copies.append(pltpu.make_async_copy(tables_low.at[core], table_low, sems.at[9]))
     for copy in copies:
         copy.start()
     for step, copy in enumerate(copies[:3]):
@@ -213,17 +214,15 @@
         inverse[layer] = previous
 
 
-def early_kernel(own, table_high, tables_low, slab_high, slab_low, shifts, coefficients, inverse, modes, table_low, sem):
-    core, _, _ = position()
-    copy = pltpu.make_async_copy(tables_low.at[core], table_low, sem)
-    copy.start()
+def early_kernel(own, table_high, table_low, slab_high, slab_low, shifts, coefficients, inverse, modes):
     chip_pivots(shifts, coefficients, inverse)
-    high, low = split_values(own[...].reshape(8 * PLANES, HALF))
-    dot = functools.partial(jnp.dot, preferred_element_type=jnp.float32)
-    spectrum = dot(high, table_high[...]) + dot(low, table_high[...])
-    copy.wait()
-    spectrum = spectrum + dot(high, table_low[...])
-    modes[...] = dot_split((slab_high[...], slab_low[...]), split_values(spectrum)).reshape(8, PLANES, HALF)
+    modes[...] = to_modes(own, table_high, table_low, slab_high, slab_low)
+
+
+def to_modes(planes, table_high, table_low, slab_high, slab_low):
+    values = planes[...].reshape(8 * PLANES, HALF)
+    spectrum = dot_split(split_values(values), (table_high[...], table_low[...]))
+    return dot_split((slab_high[...], slab_low[...]), split_values(spectrum)).reshape(8, PLANES, HALF)
 
 
 def spectrum_into(out, planes, table_high, table_low):
@@ -564,23 +563,22 @@
     pair = [(s, s ^ 1) for s in range(2 * CHIPS)]
     lines = vmem(8, PLANES, NY)
     coefficient_rows = [in_hbm(array.reshape(1, NZ)) for array in (cell, face, screening)]
-    own, sent, table_high, coefficients = call(
+    own, sent, table_high, table_low, coefficients = call(
         split_kernel,
-        (in_hbm(charge), in_hbm(fy_high), *coefficient_rows),
-        [far] * 5,
-        [vmem(*cube), vmem(*cube), table, vmem(3 * NZ, LANES)],
-        [held] * 4,
-        [lines, vmem(3, 1, NZ), pltpu.SemaphoreType.DMA((12,))],
+        (in_hbm(charge), in_hbm(fy_high), in_hbm(fy_low), *coefficient_rows),
+        [far] * 6,
+        [vmem(*cube), vmem(*cube), table, table, vmem(3 * NZ, LANES)],
+        [held] * 5,
+        [lines, vmem(3, 1, NZ), pltpu.SemaphoreType.DMA((13,))],
     )
     other = lax.ppermute(sent, "gz", pair)
     shifts = np.concatenate([shift_y.reshape(2 * PARTS, LANES), np.broadcast_to(slab_shifts()[:, None], (PLANES, LANES))])
-    inverse, own_modes, table_low = call(
+    inverse, own_modes = call(
         early_kernel,
-        (own, table_high, in_hbm(fy_low), slab_high, slab_low, shifts, coefficients),
-        [held] * 2 + [far] + [held] * 4,
-        [vmem(*field), vmem(*cube), table],
-        [held] * 3,
-        [pltpu.SemaphoreType.DMA],
+        (own, table_high, table_low, slab_high, slab_low, shifts, coefficients),
+        [held] * 7,
+        [vmem(*field), vmem(*cube)],
+        [held] * 2,
     )
     modes, ends = call(
         forward_kernel,

time: 65.1 us -> 64.8 us (level)
  Pallas kernels: 15 us -> 14.3 us
    pallas_call x9, Pallas kernels: 15 us -> 14.3 us  [call(): pl.pallas_call(kernel, in_specs=in_specs, out_specs=out_specs, out_shape=...]
  transfers between devices with their start and end apart: 3 -> 3, of which waited for: 2 -> 3; matrix products, arithmetic and copies ran while one was open for 0% -> 0% of each run, Pallas kernels for 10% -> 8%
where the time goes in v9:
time: 64.8 us; the launch traced here: 64.6 us
  starting transfers between devices  20.6 us (32%)
  blocking collectives  18.7 us (29%)
  Pallas kernels  14.3 us (22%)
  waiting for transfers between devices  10.8 us (17%)
    all_to_all x1, blocking collectives, exchange(): lax.all_to_all(blocks, ('gx', 'gz'), 0, 0, axis_index_groups=groups, tile...  18.7 us
    pallas_call x9, Pallas kernels, call(): pl.pallas_call(kernel, in_specs=in_specs, out_specs=out_specs, out_shape=...  14.3 us
    all_to_all x1, starting transfers between devices, exchange(): lax.all_to_all(blocks, ('gx', 'gz'), 0, 0, axis_index_groups=groups, tile...  13.8 us
    all_to_all x1, waiting for transfers between devices, exchange(): lax.all_to_all(blocks, ('gx', 'gz'), 0, 0, axis_index_groups=groups, tile...  9.77 us
    ppermute x2, starting transfers between devices, body(): other = lax.ppermute(sent, 'gz', pair)  6.79 us
  transfers between devices with their start and end apart: 3, of which 3 were waited for; matrix products, arithmetic and copies ran while one was open for 0% of the time, Pallas kernels for 8%

profile of v9, /device:TPU:1, one launch (start us, length us, event | category | flops | bytes accessed | tf_op | source)
XLA Modules:
  0.0 64.6 jit_solution(939634691351892987)
XLA Ops:
  0.0 0.0 copy-start.3
  0.0 0.0 copy-start.4
  0.0 0.0 copy-start.5
  0.0 1.8 %shard_map.181 = (f32[8,32,512]{2,1,0:T(8,128)S(1)}, f32[8,32,512]{2,1,0:T(8,128)S(1)}, bf16[512,512]{1,0:T(8,128)(2,1)S(1)}, bf16[512,512]{1,0:T(8,128)(2,1)S(1)}, f32[192,128]{1,0:T(8,128)S(1)}) custom-call(f32[8,32,1024]{2,1,0:T(8,128)} %charge.1, bf16[2,512,512]{2,1,0:T(8,128)(2,1)} %constant.30.clone.tables_high, ...), custom_call_target="tpu_custom_call" | custom-call | flops 10000000 | bytes 4000000 | tf_op jit(solution)/shard_map/pallas_call | solution.py:525
  1.8 3.3 %collective-permute-start = (f32[8,32,512]{2,1,0:T(8,128)S(1)}, f32[8,32,512]{2,1,0:T(8,128)S(1)}, u32[]{:S(2)}, u32[]{:S(2)}) collective-permute-start(f32[8,32,512]{2,1,0:T(8,128)S(1)} %get-tuple-element.27), channel_id=1, source_target_pairs={{0,1},{1,0},{2,3},{3,2},{4,5},{5,4},{6,7},{7,6},{8,9},{9,8},{10,11... | collective-permute-start | bytes 1572872 | tf_op jit(solution)/shard_map/ppermute | solution.py:574
  5.2 0.0 copy-done.3
  5.2 0.0 copy-done.4
  5.2 0.0 copy-done.5
  5.2 0.0 copy-start.6
  5.2 0.0 copy-start.12
  5.2 1.1 %shard_map.182 = (f32[16,32,512]{2,1,0:T(8,128)S(1)}, f32[8,32,512]{2,1,0:T(8,128)S(1)}) custom-call(f32[8,32,512]{2,1,0:T(8,128)S(1)} %get-tuple-element.22.own, bf16[512,512]{1,0:T(8,128)(2,1)S(1)} %get-tuple-element.23.table_high, bf16[512,512]{1,0:T(8,128)(2,1)S(1)} %get-tuple-element.24.table_low, bf16[256,256]{1,0:T(8,128)(2,1)S(1)} %copy-done.4, ...), custom_call_target="tpu_custom_call" | custom-call | flops 10000000 | bytes 4000000 | tf_op jit(solution)/shard_map/pallas_call | solution.py:525
  6.3 0.4 collective-permute-done.other
  6.7 0.0 copy-done.6
  6.7 0.0 copy-done.12
  6.7 2.5 %shard_map.183 = (f32[16,32,512]{2,1,0:T(8,128)S(1)}, f32[512,128]{1,0:T(8,128)}) custom-call(f32[8,32,512]{2,1,0:T(8,128)S(1)} %get-tuple-element.26.own_modes, f32[8,32,512]{2,1,0:T(8,128)S(1)} %collective-permute-done.other, bf16[512,512]{1,0:T(8,128)(2,1)S(1)} %get-tuple-element.23.table_high, bf16[512,512]{1,0:T(8,128)(2,1)S(1)} %get-tuple-element.24.table_low, ...), custom_call_target="tpu_custom_call" | custom-call | flops 10000000 | bytes 4000000 | tf_op jit(solution)/shard_map/pallas_call | solution.py:525
  9.2 13.8 %all-to-all-start = ((f32[128,4,128]{2,1,0:T(4,128)}), f32[128,4,128]{2,1,0:T(4,128)S(1)}, u32[]{:S(2)}, u32[]{:S(2)}) async-start(f32[128,4,128]{2,1,0:T(4,128)} %bitcast.10), calls=%async_computation | async-start | bytes 524288 | tf_op jit(solution)/shard_map/all_to_all | solution.py:561
  23.0 0.0 copy-start.7
  23.0 0.0 copy-start.8
  23.0 0.0 copy-start.11
  23.0 0.0 copy-start.13
  23.1 1.0 %shard_map.184.modes = f32[16,32,512]{2,1,0:T(8,128)} custom-call(f32[16,32,512]{2,1,0:T(8,128)S(1)} %get-tuple-element.29.modes), custom_call_target="tpu_custom_call" | custom-call | flops 10000000 | bytes 4000000 | tf_op jit(solution)/shard_map/pallas_call | solution.py:525
  24.0 0.0 copy-done.7
  24.1 0.0 copy-done.8
  24.1 0.0 copy-done.11
  24.1 0.0 copy-done.13
  24.1 0.0 copy-start.9
  24.1 0.0 copy-start.10
  24.1 2.3 %shard_map.185 = (f32[64,32,128]{2,1,0:T(8,128)S(1)}, bf16[512,512]{1,0:T(8,128)(2,1)S(1)}, bf16[512,512]{1,0:T(8,128)(2,1)S(1)}, f32[4,8,128]{2,1,0:T(8,128)S(1...) custom-call(f32[16,32,512]{2,1,0:T(8,128)} %shard_map.184.modes, f32[40,128]{1,0:T(8,128)S(1)} %copy-done.5, ...), custom_call_target="tpu_custom_call" | custom-call | flops 10000000 | bytes 4000000 | tf_op jit(solution)/shard_map/pallas_call | solution.py:525
  26.4 9.8 %all-to-all-done = f32[128,4,128]{2,1,0:T(4,128)S(1)} async-done(((f32[128,4,128]{2,1,0:T(4,128)}), f32[128,4,128]{2,1,0:T(4,128)S(1)}, u32[]{:S(2)}, u32[]{:S(2)}) %all-to-all-start) | async-done | bytes 262176 | tf_op jit(solution)/shard_map/all_to_all | solution.py:561
  36.2 0.0 copy-done.9
  36.2 0.0 copy-done.10
  36.2 0.0 copy-start
  36.2 0.0 copy-start.2
  36.2 1.8 %shard_map.186 = f32[512,128]{1,0:T(8,128)S(1)} custom-call(f32[512,128]{1,0:T(8,128)S(1)} %bitcast.7, bf16[512,512]{1,0:T(8,128)(2,1)S(1)} %get-tuple-element.31.response_high, bf16[512,512]{1,0:T(8,128)(2,1)S(1)} %get-tuple-element.32.response_low, f32[4,8,128]{2,1,0:T(8,128)S(1)} %get-tuple-element.33.corners, ...), custom_call_target="tpu_custom_call" | custom-call | flops 10000000 | bytes 4000000 | tf_op jit(solution)/shard_map/pallas_call | solution.py:525
  38.0 0.0 copy-start.1
  38.0 18.7 %all_to_all.10 = f32[128,4,128]{2,1,0:T(4,128)S(1)} all-to-all(f32[128,4,128]{2,1,0:T(4,128)S(1)} %bitcast.9), channel_id=1, replica_groups={{0,2,4,6,8,10,12,14,16,18,20,22,24,26,28,30,32,34,36,38,40,42,44,46,48,..., dimensions={0} | all-to-all | bytes 524288 | tf_op jit(solution)/shard_map/all_to_all | solution.py:561
  56.7 0.0 copy-done
  56.7 0.0 copy-done.2
  56.7 0.0 copy-done.1
  56.7 1.8 %shard_map.187 = (f32[8,32,512]{2,1,0:T(8,128)S(1)}, f32[8,32,512]{2,1,0:T(8,128)S(1)}) custom-call(f32[16,32,512]{2,1,0:T(8,128)S(1)} %copy-done, f32[512,128]{1,0:T(8,128)S(1)} %bitcast.8, f32[40,128]{1,0:T(8,128)S(1)} %copy-done.5, f32[64,128]{1,0:T(8,128)S(1)} %copy-done.6, bf16[512,512]{1,0:T(8,128)(2,1)S(1)} %copy-done.1, ...), custom_call_target="tpu_custom_call" | custom-call | flops 10000000 | bytes 4000000 | tf_op jit(solution)/shard_map/pallas_call | solution.py:525
  58.5 3.5 %collective-permute-start.1 = (f32[8,32,512]{2,1,0:T(8,128)S(1)}, f32[8,32,512]{2,1,0:T(8,128)S(1)}, u32[]{:S(2)}, u32[]{:S(2)}) collective-permute-start(f32[8,32,512]{2,1,0:T(8,128)S(1)} %get-tuple-element.38), channel_id=1, source_target_pairs={{0,1},{1,0},{2,3},{3,2},{4,5},{5,4},{6,7},{7,6},{8,9},{9,8},{10,11... | collective-permute-start | bytes 1572872 | tf_op jit(solution)/shard_map/ppermute | solution.py:619
  62.0 1.0 %shard_map.188.kept = f32[8,32,512]{2,1,0:T(8,128)S(1)} custom-call(f32[8,32,512]{2,1,0:T(8,128)S(1)} %get-tuple-element.37.modes, bf16[512,512]{1,0:T(8,128)(2,1)S(1)} %copy-done.1, bf16[512,512]{1,0:T(8,128)(2,1)S(1)} %copy-done.2, bf16[256,256]{1,0:T(8,128)(2,1)S(1)} %copy-done.4, bf16[256,256]{1,0:T(8,128)(2,1)S(1)} %copy-done.3), custom_call_target="tpu_custom_call" | custom-call | flops 10000000 | bytes 4000000 | tf_op jit(solution)/shard_map/pallas_call | solution.py:525
  63.0 0.6 collective-permute-done.1.other
  63.5 1.0 %shard_map.189 = f32[8,32,1024]{2,1,0:T(8,128)} custom-call(f32[8,32,512]{2,1,0:T(8,128)S(1)} %shard_map.188.kept, f32[8,32,512]{2,1,0:T(8,128)S(1)} %collective-permute-done.1.other), custom_call_target="tpu_custom_call" | custom-call | flops 10000000 | bytes 4000000 | tf_op jit(solution)/shard_map/pallas_call | solution.py:525
Async XLA Ops:
  0.0 5.2 %copy-start.3 = (bf16[256,256]{1,0:T(8,128)(2,1)S(1)}, bf16[256,256]{1,0:T(8,128)(2,1)}, u32[]{:S(2)}) copy-start(bf16[256,256]{1,0:T(8,128)(2,1)} %constant.33.clone.slab_low) | copy-start | bytes 393220
  0.0 5.2 %copy-start.4 = (bf16[256,256]{1,0:T(8,128)(2,1)S(1)}, bf16[256,256]{1,0:T(8,128)(2,1)}, u32[]{:S(2)}) copy-start(bf16[256,256]{1,0:T(8,128)(2,1)} %constant.32.clone.slab_high) | copy-start | bytes 393220
  0.0 5.2 %copy-start.5 = (f32[40,128]{1,0:T(8,128)S(1)}, f32[40,128]{1,0:T(8,128)}, u32[]{:S(2)}) copy-start(f32[40,128]{1,0:T(8,128)} %constant.34.clone.shifts) | copy-start | bytes 61444
  1.8 4.9 %collective-permute-start = (f32[8,32,512]{2,1,0:T(8,128)S(1)}, f32[8,32,512]{2,1,0:T(8,128)S(1)}, u32[]{:S(2)}, u32[]{:S(2)}) collective-permute-start(f32[8,32,512]{2,1,0:T(8,128)S(1)} %get-tuple-element.27), channel_id=1, source_target_pairs={{0,1},{1,0},{2,3},{3,2},{4,5},{5,4},{6,7},{7,6},{8,9},{9,8},{10,11... | collective-permute-start | bytes 1572872 | tf_op jit(solution)/shard_map/ppermute | solution.py:574
  5.2 1.5 %copy-start.6 = (f32[64,128]{1,0:T(8,128)S(1)}, f32[64,128]{1,0:T(8,128)}, u32[]{:S(2)}) copy-start(f32[64,128]{1,0:T(8,128)} %constant.35.clone.weights) | copy-start | bytes 98308
  5.2 1.5 %copy-start.12 = (bf16[32,128]{1,0:T(8,128)(2,1)S(1)}, bf16[32,128]{1,0:T(8,128)(2,1)}, u32[]{:S(2)}) copy-start(bf16[32,128]{1,0:T(8,128)(2,1)} %constant.36.clone.fold) | copy-start | bytes 24580
  9.2 27.0 %all-to-all-start = ((f32[128,4,128]{2,1,0:T(4,128)}), f32[128,4,128]{2,1,0:T(4,128)S(1)}, u32[]{:S(2)}, u32[]{:S(2)}) async-start(f32[128,4,128]{2,1,0:T(4,128)} %bitcast.10), calls=%async_computation | async-start | bytes 524288 | tf_op jit(solution)/shard_map/all_to_all | solution.py:561
  23.0 1.0 %copy-start.7 = (f32[64,512]{1,0:T(8,128)S(1)}, f32[64,512]{1,0:T(8,128)}, u32[]{:S(2)}) copy-start(f32[64,512]{1,0:T(8,128)} %constant.41.clone.spread) | copy-start | bytes 393220
  23.0 1.0 %copy-start.8 = (f32[128,128]{1,0:T(8,128)S(1)}, f32[128,128]{1,0:T(8,128)}, u32[]{:S(2)}) copy-start(f32[128,128]{1,0:T(8,128)} %constant.42.clone.mask) | copy-start | bytes 196612
  23.0 1.0 %copy-start.11 = (f32[32,128]{1,0:T(8,128)S(1)}, f32[32,128]{1,0:T(8,128)}, u32[]{:S(2)}) copy-start(f32[32,128]{1,0:T(8,128)} %constant.39.clone.alias_shift) | copy-start | bytes 49156
  23.0 1.0 %copy-start.13 = (f32[1,128]{1,0:T(1,128)S(1)}, f32[1,128]{1,0:T(1,128)}, u32[]{:S(2)}) copy-start(f32[1,128]{1,0:T(1,128)} %constant.40.clone.mode_shift) | copy-start | bytes 1540
  24.1 12.1 %copy-start.9 = (bf16[96,256]{1,0:T(8,128)(2,1)S(1)}, bf16[96,256]{1,0:T(8,128)(2,1)}, u32[]{:S(2)}) copy-start(bf16[96,256]{1,0:T(8,128)(2,1)} %constant.43.clone.forward) | copy-start | bytes 147460
  24.1 12.1 %copy-start.10 = (f32[64,128]{1,0:T(8,128)S(1)}, f32[64,128]{1,0:T(8,128)}, u32[]{:S(2)}) copy-start(f32[64,128]{1,0:T(8,128)} %constant.44.clone.backward) | copy-start | bytes 98308
  36.2 20.5 %copy-start = (f32[16,32,512]{2,1,0:T(8,128)S(1)}, f32[16,32,512]{2,1,0:T(8,128)}, u32[]{:S(2)}) copy-start(f32[16,32,512]{2,1,0:T(8,128)} %shard_map.184.modes) | copy-start | bytes 3145732
  36.2 20.5 %copy-start.2 = (bf16[512,512]{1,0:T(8,128)(2,1)S(1)}, bf16[512,512]{1,0:T(8,128)(2,1)}, u32[]{:S(2)}) copy-start(bf16[512,512]{1,0:T(8,128)(2,1)} %get-tuple-element.36.table_low) | copy-start | bytes 1572868
  38.0 18.7 %copy-start.1 = (bf16[512,512]{1,0:T(8,128)(2,1)S(1)}, bf16[512,512]{1,0:T(8,128)(2,1)}, u32[]{:S(2)}) copy-start(bf16[512,512]{1,0:T(8,128)(2,1)} %get-tuple-element.35.table_high) | copy-start | bytes 1572868
  58.5 5.0 %collective-permute-start.1 = (f32[8,32,512]{2,1,0:T(8,128)S(1)}, f32[8,32,512]{2,1,0:T(8,128)S(1)}, u32[]{:S(2)}, u32[]{:S(2)}) collective-permute-start(f32[8,32,512]{2,1,0:T(8,128)S(1)} %get-tuple-element.38), channel_id=1, source_target_pairs={{0,1},{1,0},{2,3},{3,2},{4,5},{5,4},{6,7},{7,6},{8,9},{9,8},{10,11... | collective-permute-start | bytes 1572872 | tf_op jit(solution)/shard_map/ppermute | solution.py:619
